TPU v7x, 32 devices: a whole 2x2x4 slice. The times are simulated.
32 devices in a mesh: blk: 8 (over z, y), tp: 4 (over x, core).
Axes of the slice: x: 2, y: 2, z: 4, core: 2. Of those that a mesh axis runs over, the one named last changes fastest.
Arguments:
- layer_input: bfloat16 [4096, 2048], P('blk'), may hold values from -6 to 6
- ln1_gain: float32 [2048], replicated, may hold values from 0.5 to 1.5
- ln1_bias: float32 [2048], replicated, may hold values from -1.75 to 1.75
- w_qkv: bfloat16 [3, 2048, 2048], P(None, None, 'tp'), may hold values from -0.1875 to 0.1875
- w_out: bfloat16 [2048, 2048], P('tp'), may hold values from -0.5 to 0.5
- ln2_gain: float32 [2048], replicated, may hold values from 0.5 to 1.5
- ln2_bias: float32 [2048], replicated, may hold values from -1.75 to 1.75
- w_up: bfloat16 [2048, 8192], P(None, 'tp'), may hold values from -0.125 to 0.125
- w_down: bfloat16 [8192, 2048], P('tp'), may hold values from -0.0625 to 0.0625
- buckets: int32 [4096], P('blk'), may hold values from 0 to 3
- lengths: int32 [3], replicated, may hold values from 256 to 2048, as said below
- block_order: int32 [16], replicated, may hold values from 0 to 15, as said below
- grad_out: bfloat16 [4096, 2048], P('blk'), may hold values from -6 to 6
Outputs:
- layer_output: bfloat16 [4096, 2048], P('blk')
- grad_input: float32 [4096, 2048], P('blk')
- grad_ln1_gain: float32 [2048], replicated
- grad_ln1_bias: float32 [2048], replicated
- grad_qkv: float32 [3, 2048, 2048], P(None, 'blk', 'tp')
- grad_w_out: float32 [2048, 2048], P('tp', 'blk')
- grad_ln2_gain: float32 [2048], replicated
- grad_ln2_bias: float32 [2048], replicated
- grad_up: float32 [2048, 8192], P('blk', 'tp')
- grad_down: float32 [8192, 2048], P('tp', 'blk')
- bucket_counts: int32 [4], replicated
Inputs may be any that keep to these rules, and one draw needn't show every extreme that they name: 3 lengths in packed order summing to 4096; exactly one is 2048, and its document holds tokens of the first, the middle and the last device of blk. a permutation of the 2 * 8 blocks of 256 packed positions; device d of blk holds block_order[2 d] and then block_order[2 d + 1].
All inputs are finite; a program needn't handle non-finite values.
Results may differ from a plain program's by a relative error of at most 0.028.
Values may be sent and summed in bfloat16 or wider, within the bound.
No kernel may reach another device: no remote copies, remote signals or barrier semaphores. Data moves between devices by JAX's collectives and lax.ppermute only.
A program may use at most 256 MiB of HBM per device.

v0:
```python
import math

import jax
import jax.numpy as jnp
from jax import lax
from jax.sharding import PartitionSpec as P

HD = 128
FF = 8192
NB = 4


EPSILON = 1e-05
ROPE_BASE = 10000.0


def packed_place(row_ids, block_order, lengths, block_len):
    slot_ids = row_ids // block_len
    table = jnp.arange(block_order.shape[0], dtype=jnp.int32)
    offsets = jnp.sum(
        jnp.where(slot_ids[:, None] == table[None, :], block_order[None, :], 0), axis=1
    )
    places = offsets * block_len + row_ids % block_len
    starts = jnp.cumsum(lengths) - lengths
    firsts = jnp.max(jnp.where(starts[None, :] <= places[:, None], starts[None, :], 0), axis=1)
    return (places, firsts)


def rotary_tables(positions):
    freqs = ROPE_BASE ** (-(jnp.arange(HD // 2, dtype=jnp.float32) * 2.0 / HD))
    angles = positions.astype(jnp.float32)[:, None] * freqs[None, :]
    return (jnp.cos(angles)[:, None, :], jnp.sin(angles)[:, None, :])


def rotate(values, cosine, sine):
    half_dim = HD // 2
    first_half = values[..., :half_dim]
    second_half = values[..., half_dim:]
    return jnp.concatenate(
        [first_half * cosine - second_half * sine, second_half * cosine + first_half * sine],
        axis=-1,
    )


def rotate_back(grads, cosine, sine):
    half_dim = HD // 2
    first_half = grads[..., :half_dim]
    second_half = grads[..., half_dim:]
    return jnp.concatenate(
        [first_half * cosine + second_half * sine, second_half * cosine - first_half * sine],
        axis=-1,
    )


def layer_norm(values, gain, bias):
    centre = values - jnp.mean(values, axis=-1, keepdims=True)
    inverse = lax.rsqrt(jnp.mean(centre * centre, axis=-1, keepdims=True) + EPSILON)
    normed = centre * inverse
    return (normed * gain + bias, normed, inverse)


def layer_norm_back(grad, normed, inverse, gain):
    grad_normed = grad * gain
    grad_in = inverse * (
        grad_normed
        - jnp.mean(grad_normed, axis=-1, keepdims=True)
        - normed * jnp.mean(grad_normed * normed, axis=-1, keepdims=True)
    )
    return (grad_in, jnp.sum(grad * normed, axis=0), jnp.sum(grad, axis=0))


def visible_pairs(q_place, q_first, k_place, k_first):
    return (k_first[None, :] == q_first[:, None]) & (k_place[None, :] <= q_place[:, None])


def block_grads(
    queries, out_grads, log_sums, row_dots, q_place, q_first, keys, values, k_place, k_first, scale
):
    scores = jnp.einsum("qhd,khd->hqk", queries, keys, preferred_element_type=jnp.float32) * scale
    visible = visible_pairs(q_place, q_first, k_place, k_first)
    probs = jnp.where(visible[None], jnp.exp(scores - log_sums.T[:, :, None]), 0.0)
    grad_probs = jnp.einsum("qhd,khd->hqk", out_grads, values, preferred_element_type=jnp.float32)
    grad_scores = (probs * (grad_probs - row_dots.T[:, :, None])).astype(jnp.bfloat16)
    grad_q = (
        jnp.einsum("hqk,khd->qhd", grad_scores, keys, preferred_element_type=jnp.float32) * scale
    )
    grad_k = (
        jnp.einsum("hqk,qhd->khd", grad_scores, queries, preferred_element_type=jnp.float32) * scale
    )
    grad_v = jnp.einsum(
        "hqk,qhd->khd", probs.astype(jnp.bfloat16), out_grads, preferred_element_type=jnp.float32
    )
    return (grad_q, grad_k, grad_v)


def body(
    layer_input,
    ln1_gain,
    ln1_bias,
    w_qkv,
    w_out,
    ln2_gain,
    ln2_bias,
    w_up,
    w_down,
    buckets,
    lengths,
    block_order,
    grad_out,
):
    tok_rows = layer_input.shape[0]
    model_dim = layer_input.shape[1]
    head_cols = w_qkv.shape[2]
    heads_here = head_cols // HD
    ffn_here = w_up.shape[1]
    block_len = tok_rows // 2
    scale = 1.0 / math.sqrt(HD)
    own_rows = lax.axis_index("blk") * tok_rows + jnp.arange(tok_rows, dtype=jnp.int32)
    own_place, own_first = packed_place(own_rows, block_order, lengths, block_len)
    cosine, sine = rotary_tables(own_place - own_first)
    input_float = layer_input.astype(jnp.float32)
    normed_one, centred_one, inverse_one = layer_norm(input_float, ln1_gain, ln1_bias)
    h_one = normed_one.astype(jnp.bfloat16)
    projected = jnp.einsum("td,sde->ste", h_one, w_qkv, preferred_element_type=jnp.float32)
    queries = rotate(projected[0].reshape(tok_rows, heads_here, HD), cosine, sine).astype(
        jnp.bfloat16
    )
    keys = rotate(projected[1].reshape(tok_rows, heads_here, HD), cosine, sine).astype(jnp.bfloat16)
    values = projected[2].astype(jnp.bfloat16)
    keys_flat = keys.reshape(tok_rows, head_cols)
    start_state = (
        jnp.full((heads_here, tok_rows), -1e30, jnp.float32),
        jnp.zeros((heads_here, tok_rows), jnp.float32),
        jnp.zeros((tok_rows, heads_here, HD), jnp.float32),
    )
    key_piece = lax.all_gather(keys_flat, "blk", axis=0, tiled=True)
    value_piece = lax.all_gather(values, "blk", axis=0, tiled=True)
    count = key_piece.shape[0]
    absorb_step_rows = math.gcd(count, 1024)

    def one_step(step_id, state):
        run_max, run_sum, run_acc = state
        key_part = lax.dynamic_slice_in_dim(
            key_piece, step_id * absorb_step_rows, absorb_step_rows, 0
        ).reshape(absorb_step_rows, heads_here, HD)
        value_part = lax.dynamic_slice_in_dim(
            value_piece, step_id * absorb_step_rows, absorb_step_rows, 0
        ).reshape(absorb_step_rows, heads_here, HD)
        key_ids = step_id * absorb_step_rows + jnp.arange(absorb_step_rows, dtype=jnp.int32)
        key_place, key_first = packed_place(key_ids, block_order, lengths, block_len)
        visible = visible_pairs(own_place, own_first, key_place, key_first)
        scores = (
            jnp.einsum("qhd,khd->hqk", queries, key_part, preferred_element_type=jnp.float32)
            * scale
        )
        scores = jnp.where(visible[None], scores, -1e30)
        new_max = jnp.maximum(run_max, jnp.max(scores, axis=-1))
        factor = jnp.exp(run_max - new_max)
        probs = jnp.where(visible[None], jnp.exp(scores - new_max[:, :, None]), 0.0)
        new_sum = run_sum * factor + jnp.sum(probs, axis=-1)
        new_acc = run_acc * factor.T[:, :, None] + jnp.einsum(
            "hqk,khd->qhd",
            probs.astype(jnp.bfloat16),
            value_part,
            preferred_element_type=jnp.float32,
        )
        return (new_max, new_sum, new_acc)

    run_max, run_sum, run_acc = lax.fori_loop(0, count // absorb_step_rows, one_step, start_state)
    attended = (run_acc / run_sum.T[:, :, None]).astype(jnp.bfloat16)
    attended_flat = attended.reshape(tok_rows, head_cols)
    log_sums = (run_max + jnp.log(run_sum)).T
    branch = lax.psum(
        jnp.dot(attended_flat, w_out, preferred_element_type=jnp.float32).astype(jnp.bfloat16), "tp"
    ).astype(jnp.float32)
    x_mid = input_float + branch
    normed_two, centred_two, inverse_two = layer_norm(x_mid, ln2_gain, ln2_bias)
    h_two = normed_two.astype(jnp.bfloat16)
    up_val = jnp.dot(h_two, w_up, preferred_element_type=jnp.float32)
    units = lax.axis_index("tp") * ffn_here + jnp.arange(ffn_here, dtype=jnp.int32)
    unit_mask = (units[None, :] < (buckets[:, None] + 1) * (FF // NB)).astype(jnp.float32)
    relu_up = jnp.maximum(up_val, 0.0)
    act = (relu_up * relu_up * unit_mask).astype(jnp.bfloat16)
    feed = lax.psum(
        jnp.dot(act, w_down, preferred_element_type=jnp.float32).astype(jnp.bfloat16), "tp"
    ).astype(jnp.float32)
    layer_output = (x_mid + feed).astype(jnp.bfloat16)
    grad_down = jnp.einsum("tf,td->fd", act, grad_out, preferred_element_type=jnp.float32)
    grad_act = jnp.einsum("td,fd->tf", grad_out, w_down, preferred_element_type=jnp.float32)
    grad_upval = (grad_act * 2.0 * relu_up * unit_mask).astype(jnp.bfloat16)
    grad_up = jnp.einsum("td,tf->df", h_two, grad_upval, preferred_element_type=jnp.float32)
    grad_h_two = lax.psum(
        jnp.einsum("tf,df->td", grad_upval, w_up, preferred_element_type=jnp.float32).astype(
            jnp.bfloat16
        ),
        "tp",
    ).astype(jnp.float32)
    grad_mid_ln, gain_two_grad, bias_two_grad = layer_norm_back(
        grad_h_two, centred_two, inverse_two, ln2_gain
    )
    grad_mid = grad_out.astype(jnp.float32) + grad_mid_ln
    grad_branch = grad_mid.astype(jnp.bfloat16)
    grad_wout = jnp.einsum(
        "tc,td->cd", attended_flat, grad_branch, preferred_element_type=jnp.float32
    )
    grad_att = jnp.einsum(
        "td,cd->tc", grad_branch, w_out, preferred_element_type=jnp.float32
    ).astype(jnp.bfloat16)
    grad_att3 = grad_att.reshape(tok_rows, heads_here, HD)
    row_dots = jnp.sum(grad_att3.astype(jnp.float32) * attended.astype(jnp.float32), axis=-1)
    all_keys, all_values = (
        lax.all_gather(keys_flat, "blk", axis=0, tiled=True),
        lax.all_gather(values, "blk", axis=0, tiled=True),
    )
    total_rows = all_keys.shape[0]
    step_rows = math.gcd(total_rows, 1024)
    step_count = total_rows // step_rows

    def key_step(grad_q_sum, item):
        key_part, value_part, step_id = item
        key_ids = step_id * step_rows + jnp.arange(step_rows, dtype=jnp.int32)
        key_place, key_first = packed_place(key_ids, block_order, lengths, block_len)
        grad_q, grad_k, grad_v = block_grads(
            queries,
            grad_att3,
            log_sums,
            row_dots,
            own_place,
            own_first,
            key_part,
            value_part,
            key_place,
            key_first,
            scale,
        )
        return (
            grad_q_sum + grad_q,
            (grad_k.reshape(step_rows, head_cols), grad_v.reshape(step_rows, head_cols)),
        )

    grad_queries, key_terms = lax.scan(
        key_step,
        jnp.zeros((tok_rows, heads_here, HD), jnp.float32),
        (
            all_keys.reshape(step_count, step_rows, heads_here, HD),
            all_values.reshape(step_count, step_rows, heads_here, HD),
            jnp.arange(step_count, dtype=jnp.int32),
        ),
    )
    grad_keys, grad_values = (
        lax.psum_scatter(
            key_terms[0].reshape(total_rows, head_cols).astype(jnp.bfloat16),
            "blk",
            scatter_dimension=0,
            tiled=True,
        ).astype(jnp.float32),
        lax.psum_scatter(
            key_terms[1].reshape(total_rows, head_cols).astype(jnp.bfloat16),
            "blk",
            scatter_dimension=0,
            tiled=True,
        ).astype(jnp.float32),
    )
    grad_keys = grad_keys.reshape(tok_rows, heads_here, HD)
    grad_qpre = (
        rotate_back(grad_queries, cosine, sine).astype(jnp.bfloat16).reshape(tok_rows, head_cols)
    )
    grad_kpre = (
        rotate_back(grad_keys, cosine, sine).astype(jnp.bfloat16).reshape(tok_rows, head_cols)
    )
    grad_proj = jnp.stack([grad_qpre, grad_kpre, grad_values.astype(jnp.bfloat16)], axis=0)
    grad_qkv = jnp.einsum("td,ste->sde", h_one, grad_proj, preferred_element_type=jnp.float32)
    grad_h_one = lax.psum(
        jnp.einsum("ste,sde->td", grad_proj, w_qkv, preferred_element_type=jnp.float32).astype(
            jnp.bfloat16
        ),
        "tp",
    ).astype(jnp.float32)
    grad_in_ln, gain_one_grad, bias_one_grad = layer_norm_back(
        grad_h_one, centred_one, inverse_one, ln1_gain
    )
    grad_input = grad_mid + grad_in_ln
    local_counts = jnp.sum(
        (buckets[:, None] == jnp.arange(NB, dtype=jnp.int32)[None, :]).astype(jnp.float32), axis=0
    )
    gain_one_sum, bias_one_sum, gain_two_sum, bias_two_sum, count_sum = (
        lax.psum(gain_one_grad.astype(jnp.bfloat16), "blk").astype(jnp.float32),
        lax.psum(bias_one_grad.astype(jnp.bfloat16), "blk").astype(jnp.float32),
        lax.psum(gain_two_grad.astype(jnp.bfloat16), "blk").astype(jnp.float32),
        lax.psum(bias_two_grad.astype(jnp.bfloat16), "blk").astype(jnp.float32),
        lax.psum(local_counts.astype(jnp.bfloat16), "blk").astype(jnp.float32),
    )
    qkv_part, wout_part, up_part, down_part = (
        lax.psum_scatter(
            grad_qkv.astype(jnp.bfloat16), "blk", scatter_dimension=1, tiled=True
        ).astype(jnp.float32),
        lax.psum_scatter(
            grad_wout.astype(jnp.bfloat16), "blk", scatter_dimension=1, tiled=True
        ).astype(jnp.float32),
        lax.psum_scatter(
            grad_up.reshape(1, model_dim, ffn_here).astype(jnp.bfloat16),
            "blk",
            scatter_dimension=1,
            tiled=True,
        ).astype(jnp.float32),
        lax.psum_scatter(
            grad_down.astype(jnp.bfloat16), "blk", scatter_dimension=1, tiled=True
        ).astype(jnp.float32),
    )
    up_part = up_part.reshape(up_part.shape[1], ffn_here)
    return (
        layer_output,
        grad_input,
        gain_one_sum,
        bias_one_sum,
        qkv_part,
        wout_part,
        gain_two_sum,
        bias_two_sum,
        up_part,
        down_part,
        count_sum.astype(jnp.int32),
    )


def solution(mesh):
    placed = (
        P("blk", None),
        P(),
        P(),
        P(None, None, "tp"),
        P("tp", None),
        P(),
        P(),
        P(None, "tp"),
        P("tp", None),
        P("blk"),
        P(),
        P(),
        P("blk", None),
    )
    return jax.shard_map(
        body,
        mesh=mesh,
        in_specs=placed,
        out_specs=(
            P("blk", None),
            P("blk", None),
            P(),
            P(),
            P(None, "blk", "tp"),
            P("tp", "blk"),
            P(),
            P(),
            P("blk", "tp"),
            P("tp", "blk"),
            P(),
        ),
        check_vma=False,
    )
```

profile of v0, /device:TPU:0, one launch (start us, length us, event | category | flops | bytes accessed | tf_op | source)
XLA Modules:
  0.0 1220.2 jit_solution(3820240425445492068)
XLA Ops:
  11.7 6.0 convolution_bitcast_fusion
  26.4 71.7 %all-gather.6.cloned.1.call-done = bf16[1,4096,512]{1,2,0:T(8,128)(2,1)} async-done(((bf16[1,512,512]{1,2,0:T(8,128)(2,1)}), bf16[1,4096,512]{1,2,0:T(8,128)(2,1)}) %all-gather.6.cloned.1.call-update) | async-done | bytes 4194320 | tf_op jit(solution)/shard_map/all_gather | solution.py:137
  98.1 75.8 %all-gather.4.cloned.1.call-done = bf16[4096,512]{0,1:T(8,128)(2,1)} async-done(((bf16[512,512]{0,1:T(8,128)(2,1)}), bf16[4096,512]{0,1:T(8,128)(2,1)}) %all-gather.4.cloned.1.call-update) | async-done | bytes 4194320 | tf_op jit(solution)/shard_map/all_gather | solution.py:136
  174.0 37.8 %while.37 = (s32[]{:T(128)}, f32[4,512]{1,0:T(4,128)S(1)}, f32[4,512]{1,0:T(4,128)S(1)}, f32[512,4,128]{0,2,1:T(8,128)}, s32[1,3]{1,0:T(1,128)S(1)}, /*index=5*/...) while((s32[]{:T(128)}, f32[4,512]{1,0:T(4,128)S(1)}, ...), condition=%wide.region_10.11_spmd.clone, body=%wide.region_5.10_spmd.clone.sunk | while | flops 1103463424 | bytes 44736860 | solution.py:169
  216.4 49.1 %all-reduce.6.cloned.1.call-done = bf16[512,2048]{1,0:T(8,128)(2,1)} async-done(((bf16[512,2048]{1,0:T(8,128)(2,1)}), bf16[512,2048]{1,0:T(8,128)(2,1)}) %all-reduce.6.cloned.1.call-update) | async-done | bytes 2097168 | tf_op jit(solution)/shard_map/psum | solution.py:173
  265.6 3.0 fusion.76
  270.0 10.3 fusion.82
  280.3 9.4 fusion.75
  291.0 5.7 convolution_convert_fusion.2
  296.9 8.0 reshape.549
  304.9 7.9 copy.72
  312.8 7.9 reshape.533
  320.6 7.9 copy.73
  328.5 19.9 %all-reduce.8.cloned.1.call-done = bf16[512,2048]{1,0:T(8,128)(2,1)} async-done(((bf16[512,2048]{1,0:T(8,128)(2,1)}), bf16[512,2048]{1,0:T(8,128)(2,1)}) %all-reduce.8.cloned.1.call-update) | async-done | bytes 2097168 | tf_op jit(solution)/shard_map/psum | solution.py:192
  348.4 5.4 fusion.71
  353.8 3.6 fusion.69
  359.6 83.9 %while.38 = (s32[]{:T(128)}, f32[512,4,128]{0,2,1:T(8,128)S(1)}, bf16[4,1024,512]{2,1,0:T(8,128)(2,1)}, bf16[4,1024,512]{1,2,0:T(8,128)(2,1)}, bf16[4,1024,4,128...) while((s32[]{:T(128)}, f32[512,4,128]{0,2,1:T(8,128)S(1)}, ...), condition=%wide.region_22.23_spmd.clone, body=%wide.region_19.22_spmd.clone.sunk | while | flops 2708820992 | bytes 63504776 | solution.py:241
  362.0 2.7 fusion.160
  364.6 3.1 fusion.164
  367.7 4.2 fusion.162
  383.0 2.7 fusion.160
  385.7 3.1 fusion.164
  388.8 4.2 fusion.162
  403.9 2.7 fusion.160
  406.6 3.1 fusion.164
  409.6 4.2 fusion.162
  424.8 2.7 fusion.160
  427.5 3.1 fusion.164
  430.5 4.2 fusion.162
  443.7 6.2 copy.79
  450.9 4.8 convolution_convert_fusion.1
  455.8 10.6 convolution_convert_fusion.3
  466.5 65.3 %reduce-scatter.7.cloned.1.call-done = bf16[512,512]{1,0:T(8,128)(2,1)} async-done(((bf16[4096,512]{1,0:T(8,128)(2,1)}), bf16[512,512]{1,0:T(8,128)(2,1)}) %reduce-scatter.7.cloned.1.call-update) | async-done | bytes 524304 | tf_op jit(solution)/shard_map/reduce_scatter | solution.py:251
  533.9 89.5 %reduce-scatter.9.cloned.1.call-done = bf16[512,512]{1,0:T(8,128)(2,1)} async-done(((bf16[4096,512]{1,0:T(8,128)(2,1)}), bf16[512,512]{1,0:T(8,128)(2,1)}) %reduce-scatter.9.cloned.1.call-update) | async-done | bytes 524304 | tf_op jit(solution)/shard_map/reduce_scatter | solution.py:257
  623.4 7.7 bitcast_convert_fusion
  632.7 9.4 convolution_convert_fusion
  643.7 10.5 convert_bitcast_fusion
  654.9 6.9 convert_bitcast_fusion.1
  664.6 31.1 %reduce-scatter.13.cloned.1.call-done = bf16[512,256]{1,0:T(8,128)(2,1)} async-done(((bf16[512,2048]{1,0:T(8,128)(2,1)}), bf16[512,256]{1,0:T(8,128)(2,1)}) %reduce-scatter.13.cloned.1.call-update) | async-done | bytes 262160 | tf_op jit(solution)/shard_map/reduce_scatter | solution.py:297
  697.5 85.9 %all-reduce.10.cloned.1.call-done = (bf16[512,2048]{1,0:T(8,128)(2,1)}, bf16[512,2048]{1,0:T(8,128)(2,1)}) async-done(((bf16[512,2048]{1,0:T(8,128)(2,1)}, bf16[512,2048]{1,0:T(8,128)(2,1)}), (bf16[512,2048]{1,0:T(8,128)(2,1)}, bf16[512,2048]{1,0:T(8,128)(2,1)})) %all-reduce.10.cloned.1.call-update) | async-done | bytes 4194320 | tf_op jit(solution)/shard_map/psum | solution.py:184
  785.4 3.5 fusion.73
  788.9 39.6 %all-reduce = (bf16[2048]{0:T(1024)(128)(2,1)S(1)}, bf16[2048]{0:T(1024)(128)(2,1)S(1)}, bf16[2048]{0:T(1024)(128)(2,1)S(1)}, bf16[2048]{0:T(1024)(128)(2,1)S(1)}, bf16[4]{0:T(256)(128)(2,1)S(1)}) all-reduce(bf16[2048]{0:T(1024)(128)(2,1)S(1)} %get-tuple-element.679, ...), channel_id=1, replica_groups=mesh['blk'=8,'tp'=4] {'blk'}, use_global_device_ids=true, to_apply=%region_29.30 | all-reduce | flops 8196 | bytes 32784 | tf_op jit(solution)/shard_map/psum | solution.py:287
  831.4 7.8 fusion.65
  839.2 98.4 %reduce-scatter.17.cloned.1.call-done = bf16[2048,256]{1,0:T(8,128)(2,1)} async-done(((bf16[2048,2048]{1,0:T(8,128)(2,1)}), bf16[2048,256]{1,0:T(8,128)(2,1)}) %reduce-scatter.17.cloned.1.call-update) | async-done | bytes 1048592 | tf_op jit(solution)/shard_map/reduce_scatter | solution.py:306
  937.6 2.7 convert_element_type.240
  940.3 148.9 %reduce-scatter.15.cloned.1.call-done = bf16[1,256,2048]{2,1,0:T(8,128)(2,1)} async-done(((bf16[1,2048,2048]{2,1,0:T(8,128)(2,1)}), bf16[1,256,2048]{2,1,0:T(8,128)(2,1)}) %reduce-scatter.15.cloned.1.call-update) | async-done | bytes 1048592 | tf_op jit(solution)/shard_map/reduce_scatter | solution.py:300
  1089.1 2.8 bitcast_convert_fusion.1
  1091.9 118.7 %reduce-scatter.11.cloned.1.call-done = bf16[3,256,512]{1,2,0:T(8,128)(2,1)} async-done(((bf16[3,2048,512]{1,2,0:T(8,128)(2,1)}), bf16[3,256,512]{1,2,0:T(8,128)(2,1)}) %reduce-scatter.11.cloned.1.call-update) | async-done | bytes 786448 | tf_op jit(solution)/shard_map/reduce_scatter | solution.py:294
  (289 shorter events, 120.0 us)
Async XLA Ops:
  7.2 206.0 %copy-start = (bf16[512,2048]{1,0:T(8,128)(2,1)S(1)}, bf16[512,2048]{1,0:T(8,128)(2,1)}, u32[]{:S(2)}) copy-start(bf16[512,2048]{1,0:T(8,128)(2,1)} %param.21) | copy-start | bytes 6291460
  7.2 4.5 copy-start.27
  7.2 4.5 copy-start.38
  7.2 90.9 %all-gather.6.cloned.1.call-start = ((), (), s32[]{:S(2)}) async-start(), calls=%async_computation.15 | async-start | bytes 4718592 | tf_op jit(solution)/shard_map/all_gather | solution.py:137
  7.3 4.4 copy-start.2
  9.4 8.3 copy-start.29
  11.7 6.0 copy-start.31
  11.7 8.6 copy-start.40
  11.7 8.8 copy-start.25
  20.3 153.7 %all-gather.4.cloned.1.call-start = ((), (), s32[]{:S(2)}) async-start(), calls=%async_computation.6 | async-start | bytes 4718592 | tf_op jit(solution)/shard_map/all_gather | solution.py:136
  21.3 3.7 copy-start.16
  21.3 3.7 copy-start.18
  25.1 240.5 %all-reduce.6.cloned.1.call-start = ((), (), s32[]{:S(2)}) async-start(), calls=%async_computation.7 | async-start | bytes 4194304 | tf_op jit(solution)/shard_map/psum | solution.py:173
  26.1 147.9 %copy-start.8 = (bf16[512,4,128]{0,2,1:T(8,128)(2,1)}, bf16[512,4,128]{0,2,1:T(8,128)(2,1)S(1)}, u32[]{:S(2)}) copy-start(bf16[512,4,128]{0,2,1:T(8,128)(2,1)S(1)} %pad_maximum_fusion.4) | copy-start | bytes 1572868
  213.2 55.4 %copy-start.22 = (bf16[512,4,128]{0,2,1:T(8,128)(2,1)}, bf16[512,4,128]{0,2,1:T(8,128)(2,1)S(1)}, u32[]{:S(2)}) copy-start(bf16[512,4,128]{0,2,1:T(8,128)(2,1)S(1)} %divide_convert_fusion) | copy-start | bytes 1572868
  213.2 3.2 copy-start.34
  215.8 132.6 %all-reduce.8.cloned.1.call-start = ((), (), s32[]{:S(2)}) async-start(), calls=%async_computation.8 | async-start | bytes 4194304 | tf_op jit(solution)/shard_map/psum | solution.py:192
  265.5 3.0 copy-start.3
  265.5 3.5 copy-start.6
  265.5 4.4 copy-start.26
  265.5 4.4 copy-start.36
  269.0 22.0 %slice-start = ((s8[8388608]{0:T(1024)(128)(4,1)}), s8[4194304]{0:T(1024)(128)(4,1)S(1)}, s32[]{:S(2)}) async-start(s8[8388608]{0:T(1024)(128)(4,1)} %bitcast.196), calls=%async_computation.17 | async-start | bytes 8388608
  270.0 10.3 copy-start.14
  270.0 21.0 %slice-start.1 = ((s8[8388608]{0:T(1024)(128)(4,1)}), s8[4194304]{0:T(1024)(128)(4,1)S(1)}, s32[]{:S(2)}) async-start(s8[8388608]{0:T(1024)(128)(4,1)} %bitcast.196), calls=%async_computation.18 | async-start | bytes 8388608
  296.8 235.0 %reduce-scatter.7.cloned.1.call-start = ((), (), s32[]{:S(2)}) async-start(), calls=%async_computation.9 | async-start | bytes 4718592 | tf_op jit(solution)/shard_map/reduce_scatter | solution.py:251
  348.4 5.4 copy-start.4
  348.4 5.4 copy-start.7
  348.4 5.4 copy-start.11
  353.8 3.7 copy-start.23
  362.0 2.7 copy-start.41
  372.0 2.4 copy-start.9
  376.9 2.7 copy-start.10
  383.0 2.7 copy-start.41
  397.9 2.6 copy-start.10
  403.9 2.7 copy-start.41
  418.8 2.6 copy-start.10
  424.8 2.7 copy-start.41
  439.7 2.6 copy-start.10
  443.6 179.8 %reduce-scatter.9.cloned.1.call-start = ((), (), s32[]{:S(2)}) async-start(), calls=%async_computation.10 | async-start | bytes 4718592 | tf_op jit(solution)/shard_map/reduce_scatter | solution.py:257
  449.9 245.8 %reduce-scatter.13.cloned.1.call-start = ((), (), s32[]{:S(2)}) async-start(), calls=%async_computation.12 | async-start | bytes 2359296 | tf_op jit(solution)/shard_map/reduce_scatter | solution.py:297
  455.8 77.2 %copy-start.17 = (f32[512,64]{0,1:T(8,128)S(1)}, f32[512,64]{0,1:T(8,128)}, u32[]{:S(2)}) copy-start(f32[512,64]{0,1:T(8,128)} %copy-done.16) | copy-start | bytes 393220
  455.8 77.2 %copy-start.19 = (f32[512,64]{0,1:T(8,128)S(1)}, f32[512,64]{0,1:T(8,128)}, u32[]{:S(2)}) copy-start(f32[512,64]{0,1:T(8,128)} %copy-done.18) | copy-start | bytes 393220
  455.8 327.6 %all-reduce.10.cloned.1.call-start = ((), (), s32[]{:S(2)}) async-start(), calls=%async_computation.16 | async-start | bytes 8388608 | tf_op jit(solution)/shard_map/psum | solution.py:184
  631.1 306.4 %reduce-scatter.17.cloned.1.call-start = ((), (), s32[]{:S(2)}) async-start(), calls=%async_computation.14 | async-start | bytes 9437184 | tf_op jit(solution)/shard_map/reduce_scatter | solution.py:306
  642.1 447.0 %reduce-scatter.15.cloned.1.call-start = ((), (), s32[]{:S(2)}) async-start(), calls=%async_computation.13 | async-start | bytes 9437184 | tf_op jit(solution)/shard_map/reduce_scatter | solution.py:300
  654.2 556.4 %reduce-scatter.11.cloned.1.call-start = ((), (), s32[]{:S(2)}) async-start(), calls=%async_computation.11 | async-start | bytes 7077888 | tf_op jit(solution)/shard_map/reduce_scatter | solution.py:294
  662.7 126.2 %copy-start.33 = (bf16[2048]{0:T(1024)(128)(2,1)S(1)}, bf16[2048]{0:T(1024)(128)(2,1)}, u32[]{:S(2)}) copy-start(bf16[2048]{0:T(1024)(128)(2,1)} %get-tuple-element.677) | copy-start | bytes 12292
  831.4 381.8 %copy-start.1 = (bf16[512,2048]{1,0:T(8,128)(2,1)S(1)}, bf16[512,2048]{1,0:T(8,128)(2,1)}, u32[]{:S(2)}) copy-start(bf16[512,2048]{1,0:T(8,128)(2,1)} %param.21) | copy-start | bytes 6291460
  (23 other events, 37.6 us)
Sparse Core Ops, SparseCore 0:
  20.4 77.6 all-gather.5
  100.8 73.1 all-gather.3
  215.9 49.5 all-reduce.5
  296.9 51.4 all-reduce.7
  443.7 87.9 reduce-scatter.6
  535.7 87.6 reduce-scatter.8
  627.5 68.2 reduce-scatter.12
  698.7 84.6 all-reduce.9
  787.5 150.0 reduce-scatter.16
  941.0 148.0 reduce-scatter.14
  1093.2 117.3 reduce-scatter.10
where the time goes:
time: 1230 us; the launch traced here: 1220 us
  waiting for transfers between devices  854 us (69%)
  matrix products  163 us (13%)
  local copies, waits for them, and re-layouts  77.9 us (6%)
  other arithmetic  65.3 us (5%)
  blocking collectives  39.6 us (3%)
  between operations  14.9 us (1%)
    reduce_scatter x1, waiting for transfers between devices, body(): lax.psum_scatter(grad_up.reshape(1, model_dim, ffn_here).astype(jnp.bfloa...  149 us
    reduce_scatter x1, waiting for transfers between devices, body(): lax.psum_scatter(grad_qkv.astype(jnp.bfloat16), 'blk', scatter_dimension=...  119 us
    reduce_scatter x1, waiting for transfers between devices, body(): lax.psum_scatter(grad_down.astype(jnp.bfloat16), 'blk', scatter_dimension...  98.4 us
    reduce_scatter x1, waiting for transfers between devices, body(): lax.psum_scatter(key_terms[1].reshape(total_rows, head_cols).astype(jnp.b...  89.5 us
    psum x1, waiting for transfers between devices, body(): lax.psum(jnp.dot(act, w_down, preferred_element_type=jnp.float32).astype(...  85.9 us
    all_gather x1, waiting for transfers between devices, body(): key_piece = lax.all_gather(keys_flat, 'blk', axis=0, tiled=True)  75.8 us
    all_gather x1, waiting for transfers between devices, body(): value_piece = lax.all_gather(values, 'blk', axis=0, tiled=True)  71.7 us
    reduce_scatter x1, waiting for transfers between devices, body(): lax.psum_scatter(key_terms[0].reshape(total_rows, head_cols).astype(jnp.b...  65.3 us
  transfers between devices with their start and end apart: 11, of which 11 were waited for; matrix products, arithmetic and copies ran while one was open for 10% of the time, Pallas kernels for 0%

commit v1 on v0

v1 whole, which is shorter than its diff:
```python
import functools
import math

import jax
import jax.numpy as jnp
from jax import lax
from jax.experimental import pallas as pl
from jax.experimental.pallas import tpu as pltpu
from jax.sharding import Mesh
from jax.sharding import PartitionSpec as P

HD = 128
FF = 8192
NB = 4
HEADS = 4
EPSILON = 1e-05
ROPE_BASE = 10000.0
SWAP = [(0, 1), (1, 0)]
BLK = ("r", "h", "y")
TP = ("x", "c")
F32 = jnp.float32
BF16 = jnp.bfloat16


def swap(value, axis):
    return lax.ppermute(value, axis, SWAP)


def ordered(first, second):
    return lax.optimization_barrier((first, second))


def rotary_tables(positions):
    freqs = ROPE_BASE ** (-(jnp.arange(HD // 2, dtype=F32) * 2.0 / HD))
    angles = positions.astype(F32)[:, None] * freqs[None, :]
    return (jnp.cos(angles), jnp.sin(angles))


def rotate(values, cosine, sine):
    first_half, second_half = values[..., : HD // 2], values[..., HD // 2 :]
    return jnp.concatenate(
        [first_half * cosine - second_half * sine, second_half * cosine + first_half * sine],
        axis=-1,
    )


def norm_parts(values):
    centre = values - jnp.mean(values, axis=-1, keepdims=True)
    inverse = lax.rsqrt(jnp.mean(centre * centre, axis=-1, keepdims=True) + EPSILON)
    return (centre * inverse, inverse)


def layer_norm_back(grad, normed, inverse, gain):
    grad_normed = grad * gain
    grad_in = inverse * (
        grad_normed
        - jnp.mean(grad_normed, axis=-1, keepdims=True)
        - normed * jnp.mean(grad_normed * normed, axis=-1, keepdims=True)
    )
    return (grad_in, jnp.sum(grad * normed, axis=0), jnp.sum(grad, axis=0))


def nt(lhs, rhs):
    return lax.dot_general(lhs, rhs, (((1,), (1,)), ((), ())), preferred_element_type=F32)


def tn(lhs, rhs):
    return lax.dot_general(lhs, rhs, (((0,), (0,)), ((), ())), preferred_element_type=F32)


def nn(lhs, rhs):
    return lax.dot_general(lhs, rhs, (((1,), (0,)), ((), ())), preferred_element_type=F32)


def visible_of(tile, key_block, query_places, query_firsts):
    key_places = key_block * tile + lax.broadcasted_iota(jnp.int32, (tile, 1), 0)
    return (key_places <= query_places) & (key_places >= query_firsts)


def attend_kernel(tile, scale, at_ref, low_ref, row_ref, q_ref, first_ref, kv_ref, o_ref, lse_ref):
    lanes = lax.broadcasted_iota(jnp.int32, (1, tile), 1)

    def one_block(i, carry):
        rows = pl.ds(pl.multiple_of(i * tile, tile), tile)
        queries = q_ref[rows, :HD]
        firsts = first_ref[i]
        places = at_ref[i] * tile + lanes

        def one_step(b, state):
            run_max, run_sum, run_acc = state
            krows = pl.ds(pl.multiple_of(row_ref[b] * tile, tile), tile)
            scores = nt(kv_ref[krows, :HD], queries) * scale
            visible = visible_of(tile, b, places, firsts)
            scores = jnp.where(visible, scores, -1e30)
            new_max = jnp.maximum(run_max, jnp.max(scores, axis=0, keepdims=True))
            factor = jnp.exp(run_max - new_max)
            probs = jnp.where(visible, jnp.exp(scores - new_max), 0.0)
            new_sum = run_sum * factor + jnp.sum(probs, axis=0, keepdims=True)
            new_acc = run_acc * factor + tn(kv_ref[krows, HD:], probs.astype(BF16))
            return (new_max, new_sum, new_acc)

        run_max, run_sum, run_acc = lax.fori_loop(
            low_ref[i],
            at_ref[i] + 1,
            one_step,
            (
                jnp.full((1, tile), -1e30, F32),
                jnp.zeros((1, tile), F32),
                jnp.zeros((HD, tile), F32),
            ),
        )
        o_ref[rows, :] = (run_acc / run_sum).T.astype(BF16)
        lse_ref[i] = run_max + jnp.log(run_sum)
        return carry

    lax.fori_loop(0, q_ref.shape[0] // tile, one_block, 0)


def attend_back_kernel(
    tile,
    scale,
    at_ref,
    low_ref,
    row_ref,
    q_ref,
    first_ref,
    kv_ref,
    o_ref,
    lse_ref,
    do_ref,
    dq_ref,
    dkv_ref,
    far_ref,
    acc_ref,
):
    lanes = lax.broadcasted_iota(jnp.int32, (1, tile), 1)
    acc_ref[...] = jnp.zeros_like(acc_ref)

    def one_block(i, carry):
        rows = pl.ds(pl.multiple_of(i * tile, tile), tile)
        queries = q_ref[rows, :HD]
        grads = do_ref[rows, :]
        firsts = first_ref[i]
        places = at_ref[i] * tile + lanes
        log_sums = lse_ref[i]
        products = grads.astype(F32) * o_ref[rows, :].astype(F32)
        deltas = jnp.sum(products.T, axis=0, keepdims=True)

        def one_step(b, grad_q):
            krows = pl.ds(pl.multiple_of(row_ref[b] * tile, tile), tile)
            keys = kv_ref[krows, :HD]
            scores = nt(keys, queries) * scale
            visible = visible_of(tile, b, places, firsts)
            probs = jnp.where(visible, jnp.exp(scores - log_sums), 0.0)
            grad_probs = nt(kv_ref[krows, HD:], grads)
            grad_scores = (probs * (grad_probs - deltas)).astype(BF16)
            acc_ref[krows, HD:] += nn(probs.astype(BF16), grads)
            acc_ref[krows, :HD] += nn(grad_scores, queries)
            return grad_q + tn(keys, grad_scores)

        grad_q = lax.fori_loop(low_ref[i], at_ref[i] + 1, one_step, jnp.zeros((HD, tile), F32))
        dq_ref[rows, :] = (grad_q * scale).T
        return carry

    lax.fori_loop(0, q_ref.shape[0] // tile, one_block, 0)
    near = dkv_ref.shape[0]
    dkv_ref[:, :HD] = acc_ref[:near, :HD] * scale
    dkv_ref[:, HD:] = acc_ref[:near, HD:]
    far_ref[:, :HD] = (acc_ref[near:, :HD] * scale).astype(BF16)
    far_ref[:, HD:] = acc_ref[near:, HD:].astype(BF16)


SMEM = pl.BlockSpec(memory_space=pltpu.SMEM)
VMEM = pl.BlockSpec(memory_space=pltpu.VMEM)


def attend(tile, scale, at, low, row, queries, firsts, keys_values):
    rows = queries.shape[0]
    return pl.pallas_call(
        functools.partial(attend_kernel, tile, scale),
        out_shape=(
            jax.ShapeDtypeStruct((rows, HD), BF16),
            jax.ShapeDtypeStruct((rows // tile, 1, tile), F32),
        ),
        in_specs=[SMEM] * 3 + [VMEM] * 3,
        out_specs=(VMEM, VMEM),
        compiler_params=pltpu.CompilerParams(vmem_limit_bytes=40 * 2**20),
        cost_estimate=pl.CostEstimate(
            flops=4 * rows * 1280 * HD, bytes_accessed=4 * 2**20, transcendentals=rows * 1280
        ),
        name="attend",
    )(at, low, row, queries, firsts, keys_values)


def attend_back(tile, scale, at, low, row, queries, firsts, keys_values, outs, lse, grads):
    rows = queries.shape[0]
    near = keys_values.shape[0] // 2
    return pl.pallas_call(
        functools.partial(attend_back_kernel, tile, scale),
        out_shape=(
            jax.ShapeDtypeStruct((rows, HD), F32),
            jax.ShapeDtypeStruct((near, 2 * HD), F32),
            jax.ShapeDtypeStruct((near, 2 * HD), BF16),
        ),
        in_specs=[SMEM] * 3 + [VMEM] * 6,
        out_specs=(VMEM, VMEM, VMEM),
        scratch_shapes=[pltpu.VMEM(keys_values.shape, F32)],
        compiler_params=pltpu.CompilerParams(vmem_limit_bytes=50 * 2**20),
        cost_estimate=pl.CostEstimate(
            flops=10 * rows * 1280 * HD, bytes_accessed=8 * 2**20, transcendentals=rows * 1280
        ),
        name="attend_back",
    )(at, low, row, queries, firsts, keys_values, outs, lse, grads)


def body(
    depth,
    layer_input,
    ln1_gain,
    ln1_bias,
    w_qkv,
    w_out,
    ln2_gain,
    ln2_bias,
    w_up,
    w_down,
    buckets,
    lengths,
    block_order,
    grad_out,
):
    tok, dim = layer_input.shape
    head_cols = w_qkv.shape[2]
    ffn_here = w_up.shape[1]
    half = tok // 2
    outer = HEADS * depth
    scale = 1.0 / math.sqrt(HD)
    r, h, y, c = (lax.axis_index(a) for a in ("r", "h", "y", "c"))
    blk = lax.axis_index(BLK)

    def parity(values, which):
        split = values.reshape(tok, outer, 2, dim // (2 * outer))
        return lax.dynamic_index_in_dim(split, which, 2, keepdims=False).reshape(tok, dim // 2)

    def my_half(values):
        return lax.dynamic_slice_in_dim(values, c * half, half, 0)

    def other_half(values):
        return lax.dynamic_slice_in_dim(values, (1 - c) * half, half, 0)

    def join_halves(mine):
        other = swap(mine, "c")
        return jnp.where(
            c == 0, jnp.concatenate([mine, other]), jnp.concatenate([other, mine])
        )

    def reduce_tp(part):
        got = swap(other_half(part), "c")
        chip = (my_half(part).astype(F32) + got.astype(F32)).astype(BF16)
        return chip.astype(F32) + swap(chip, "x").astype(F32)

    starts = jnp.cumsum(lengths) - lengths

    def firsts_of(places):
        return jnp.max(jnp.where(starts <= places[..., None], starts, 0), axis=-1)

    inside = jnp.arange(half, dtype=jnp.int32)
    own_places = (
        lax.dynamic_slice_in_dim(block_order, 2 * blk, 2, 0)[:, None] * half + inside
    ).reshape(tok)
    cosine, sine = rotary_tables(own_places - firsts_of(own_places))
    group_order = lax.dynamic_slice_in_dim(
        block_order.reshape(depth, HEADS, 2, 2), r, 1, 0
    )
    query_at = lax.dynamic_slice_in_dim(group_order, y, 1, 2).reshape(2 * HEADS)
    query_places = query_at[:, None] * half + inside
    query_firsts = firsts_of(query_places)
    query_low = query_firsts[:, 0] // half
    block_count = block_order.shape[0]
    slots = jnp.argmax(
        block_order[None, :] == jnp.arange(block_count, dtype=jnp.int32)[:, None], axis=1
    ).astype(jnp.int32)
    slot_dev = slots // 2
    key_row = jnp.where(slot_dev % 2 == y, 0, block_count // 2) + slot_dev // 2 * 2 + slots % 2
    group_cos, group_sin = rotary_tables((query_places - query_firsts).reshape(2 * HEADS * half))

    grad_near = parity(grad_out, y)
    grad_far = swap(parity(grad_out, 1 - y), "y")

    input_float = layer_input.astype(F32)
    normed_one, _ = norm_parts(input_float)
    h_one = (normed_one * ln1_gain + ln1_bias).astype(BF16)
    projected = jnp.einsum(
        "td,sdhe->shte", h_one, w_qkv.reshape(3, dim, HEADS, HD), preferred_element_type=F32
    )
    packed = jnp.concatenate(
        [
            rotate(projected[0], cosine, sine).astype(BF16),
            rotate(projected[1], cosine, sine).astype(BF16),
            projected[2].astype(BF16),
        ],
        axis=-1,
    )
    packed = lax.all_to_all(packed, "h", 0, 0, tiled=True)
    packed = packed.reshape(HEADS * tok, 3 * HD)
    near_kv = packed[:, HD:]
    if depth > 1:
        near_kv = lax.all_gather(near_kv, "r", axis=0, tiled=True)
    far_kv = swap(near_kv, "y")
    all_kv = jnp.concatenate([near_kv, far_kv], axis=0)
    first_rows = query_firsts.reshape(2 * HEADS, 1, half)
    attended, lse = attend(
        half, scale, query_at, query_low, key_row, packed, first_rows, all_kv
    )
    heads_out = lax.all_to_all(attended.reshape(HEADS, tok, HD), "h", 0, 0, tiled=True)
    attended_flat = heads_out.transpose(1, 0, 2).reshape(tok, head_cols)
    part = jnp.dot(attended_flat, w_out, preferred_element_type=F32).astype(BF16)
    branch = reduce_tp(part)
    x_mid = my_half(input_float) + branch
    normed_two, inverse_two = norm_parts(x_mid)
    h_two = join_halves((normed_two * ln2_gain + ln2_bias).astype(BF16))

    up_val = jnp.dot(h_two, w_up, preferred_element_type=F32)
    units = lax.axis_index(TP) * ffn_here + jnp.arange(ffn_here, dtype=jnp.int32)
    unit_mask = (units[None, :] < (buckets[:, None] + 1) * (FF // NB)).astype(F32)
    relu_up = jnp.maximum(up_val, 0.0) * unit_mask
    act = (relu_up * relu_up).astype(BF16)
    grad_act = nt(grad_out, w_down)
    grad_upval = (grad_act * 2.0 * relu_up).astype(BF16)
    act_far = swap(act, "y")
    h_one_far = swap(parity(h_one, 1 - y), "y")
    h_two_far = swap(parity(h_two, 1 - y), "y")
    att_far = swap(attended_flat, "y")

    def pair_product(near, far, cols_near, cols_far):
        return tn(jnp.concatenate([near, far]), jnp.concatenate([cols_near, cols_far]))

    def scatter(values, dimension):
        return lax.psum_scatter(
            values.astype(BF16), ("r", "h"), scatter_dimension=dimension, tiled=True
        ).astype(F32)

    grad_h_two = reduce_tp(nt(grad_upval, w_up).astype(BF16))
    down_part = scatter(pair_product(act, act_far, grad_near, grad_far), 1)
    grad_mid_ln, gain_two_grad, bias_two_grad = layer_norm_back(
        grad_h_two, normed_two, inverse_two, ln2_gain
    )
    grad_mid = my_half(grad_out).astype(F32) + grad_mid_ln
    grad_branch = join_halves(grad_mid.astype(BF16))
    grad_att = jnp.einsum(
        "td,hcd->htc", grad_branch, w_out.reshape(HEADS, HD, dim), preferred_element_type=F32
    ).astype(BF16)
    grad_att = lax.all_to_all(grad_att, "h", 0, 0, tiled=True).reshape(HEADS * tok, HD)
    grad_up_far = swap(grad_upval, "y")
    up_part = scatter(
        pair_product(parity(h_two, y), h_two_far, grad_upval, grad_up_far), 0
    )
    feed = reduce_tp(jnp.dot(act, w_down, preferred_element_type=F32).astype(BF16))
    layer_output = join_halves((x_mid + feed).astype(BF16))
    branch_far = swap(parity(grad_branch, 1 - y), "y")
    wout_part = scatter(
        pair_product(attended_flat, att_far, parity(grad_branch, y), branch_far), 1
    )

    grad_q, grad_kv, grad_kv_far = attend_back(
        half, scale, query_at, query_low, key_row, packed, first_rows, all_kv, attended, lse, grad_att
    )
    grad_kv = grad_kv + swap(grad_kv_far, "y").astype(F32)
    if depth > 1:
        grad_kv = lax.psum_scatter(grad_kv, "r", scatter_dimension=0, tiled=True)
    grad_packed = jnp.concatenate(
        [
            rotate(grad_q, group_cos, -group_sin).astype(BF16),
            rotate(grad_kv[:, :HD], group_cos, -group_sin).astype(BF16),
            grad_kv[:, HD:].astype(BF16),
        ],
        axis=-1,
    )
    grad_packed = lax.all_to_all(
        grad_packed.reshape(HEADS, tok, 3 * HD), "h", 0, 0, tiled=True
    )
    grad_proj = (
        grad_packed.reshape(HEADS, tok, 3, HD).transpose(1, 2, 0, 3).reshape(tok, 3, head_cols)
    )
    grad_h_one = reduce_tp(
        jnp.einsum("tse,sde->td", grad_proj, w_qkv, preferred_element_type=F32).astype(BF16)
    )
    proj_far = swap(grad_proj, "y")
    qkv_part = scatter(
        jnp.einsum(
            "td,tse->sde",
            jnp.concatenate([parity(h_one, y), h_one_far]),
            jnp.concatenate([grad_proj, proj_far]),
            preferred_element_type=F32,
        ),
        1,
    )
    normed_own, inverse_own = norm_parts(my_half(input_float))
    grad_in_ln, gain_one_grad, bias_one_grad = layer_norm_back(
        grad_h_one, normed_own, inverse_own, ln1_gain
    )
    grad_input = join_halves((grad_mid + grad_in_ln).astype(BF16)).astype(F32)
    local_counts = jnp.sum(
        (my_half(buckets)[:, None] == jnp.arange(NB, dtype=jnp.int32)[None, :]).astype(F32), axis=0
    )
    sums = lax.psum(
        jnp.concatenate(
            [gain_one_grad, bias_one_grad, gain_two_grad, bias_two_grad, local_counts]
        ),
        BLK + ("c",),
    )
    return (
        layer_output,
        grad_input,
        sums[:dim],
        sums[dim : 2 * dim],
        qkv_part,
        wout_part,
        sums[2 * dim : 3 * dim],
        sums[3 * dim : 4 * dim],
        up_part,
        down_part,
        sums[4 * dim :].astype(jnp.int32),
    )


def solution(mesh):
    depth = mesh.shape["blk"] // (2 * HEADS)
    fine = Mesh(mesh.devices.reshape(depth, HEADS, 2, 2, 2), BLK + TP)
    return jax.shard_map(
        functools.partial(body, depth),
        mesh=fine,
        in_specs=(
            P(BLK, None),
            P(),
            P(),
            P(None, None, TP),
            P(TP, None),
            P(),
            P(),
            P(None, TP),
            P(TP, None),
            P(BLK),
            P(),
            P(),
            P(BLK, None),
        ),
        out_specs=(
            P(BLK, None),
            P(BLK, None),
            P(),
            P(),
            P(None, BLK, TP),
            P(TP, BLK),
            P(),
            P(),
            P(BLK, TP),
            P(TP, BLK),
            P(),
        ),
        check_vma=False,
    )
```

time: 1230 us -> 837 us (0.68)
  waiting for transfers between devices: 854 us -> 386 us
  blocking collectives: 39.6 us -> 132 us
  matrix products: 163 us -> 78.8 us
  Pallas kernels: 0 us -> 39.6 us
  starting transfers between devices: 1.23 us -> 25.1 us
  local copies, waits for them, and re-layouts: 77.9 us -> 97.9 us
    reduce_scatter x6 -> x4, waiting for transfers between devices: 552 us -> 0.01 us  [scatter(): lax.psum_scatter(values.astype(BF16), ('r', 'h'), scatter_dimension=dimen...]
    ppermute x0 -> x22, waiting for transfers between devices: none -> 337 us  [swap(): return lax.ppermute(value, axis, SWAP)]
    psum x3 -> x0, waiting for transfers between devices: 155 us -> none  [the longest x1 85.9 us: body(): lax.psum(jnp.dot(act, w_down, preferred_element_type=jnp.float32).astype(...]
    all_gather x2 -> x0, waiting for transfers between devices: 148 us -> none  [the longest x1 75.8 us: body(): key_piece = lax.all_gather(keys_flat, 'blk', axis=0, tiled=True)]
    dot_general x40 -> x11, matrix products: 163 us -> 72.4 us  [the longest x3 19.1 us: tn(): lax.dot_general(lhs, rhs, (((0,), (0,)), ((), ())), preferred_element_typ...]
    all_to_all x0 -> x2, blocking collectives: none -> 71 us  [the longest x1 40.2 us: body(): lax.all_to_all(grad_packed.reshape(HEADS, tok, 3 * HD), 'h', 0, 0, tiled=...]
    all_to_all x0 -> x2, waiting for transfers between devices: none -> 49.6 us  [the longest x1 36.9 us: body(): packed = lax.all_to_all(packed, 'h', 0, 0, tiled=True)]
    pallas_call x0 -> x2, Pallas kernels: none -> 39.6 us  [the longest x1 22 us: attend_back(): pl.pallas_call(functools.partial(attend_back_kernel, tile, scale), out_sh...]
  transfers between devices with their start and end apart: 11 -> 28, of which waited for: 11 -> 17; matrix products, arithmetic and copies ran while one was open for 10% -> 17% of each run, Pallas kernels for 0% -> 3%
where the time goes in v1:
time: 837 us; the launch traced here: 830 us
  waiting for transfers between devices  386 us (46%)
  blocking collectives  132 us (16%)
  local copies, waits for them, and re-layouts  97.9 us (12%)
  matrix products  78.8 us (9%)
  other arithmetic  55.5 us (7%)
  Pallas kernels  39.6 us (5%)
  starting transfers between devices  25.1 us (3%)
  between operations  14.8 us (2%)
    ppermute x22, waiting for transfers between devices, swap(): return lax.ppermute(value, axis, SWAP)  337 us
    psum x1, blocking collectives, body(): lax.psum(jnp.concatenate([gain_one_grad, bias_one_grad, gain_two_grad, bi...  61.1 us
    all_to_all x1, blocking collectives, body(): lax.all_to_all(grad_packed.reshape(HEADS, tok, 3 * HD), 'h', 0, 0, tiled=...  40.2 us
    all_to_all x1, waiting for transfers between devices, body(): packed = lax.all_to_all(packed, 'h', 0, 0, tiled=True)  36.9 us
    all_to_all x1, blocking collectives, body(): lax.all_to_all(grad_att, 'h', 0, 0, tiled=True).reshape(HEADS * tok, HD)  30.8 us
    concatenate x8, local copies, waits for them, and re-layouts, join_halves(): jnp.concatenate([mine, other])  25.2 us
    pallas_call x1, Pallas kernels, attend_back(): pl.pallas_call(functools.partial(attend_back_kernel, tile, scale), out_sh...  22 us
    unnamed x62, local copies, waits for them, and re-layouts  19.1 us
  transfers between devices with their start and end apart: 28, of which 17 were waited for; matrix products, arithmetic and copies ran while one was open for 17% of the time, Pallas kernels for 3%

profile of v1, /device:TPU:0, one launch (start us, length us, event | category | flops | bytes accessed | tf_op | source)
XLA Modules:
  0.0 830.2 jit_solution(15501917275741230121)
XLA Ops:
  11.7 8.8 %copy.110 = bf16[3,2048,512]{1,2,0:T(8,128)(2,1)} copy(bf16[3,2048,512]{2,1,0:T(8,128)(2,1)} %param.16) | data formatting | bytes 12582912 | tf_op jit(solution)/shard_map/reshape | solution.py:294
  23.0 6.3 fusion.102
  39.7 6.3 all-to-all-start
  46.2 36.9 %all-to-all-done = bf16[4,512,384]{1,2,0:T(8,128)(2,1)} async-done(((bf16[4,512,384]{1,2,0:T(8,128)(2,1)}), bf16[4,512,384]{1,2,0:T(8,128)(2,1)}, u32[]{:S(2)}, u32[]{:S(2)}) %all-to-all-start) | async-done | bytes 1572896 | tf_op jit(solution)/shard_map/all_to_all | solution.py:304
  89.5 21.6 %collective-permute-done = bf16[2048,256]{1,0:T(8,128)(2,1)S(1)} collective-permute-done((bf16[2048,256]{1,0:T(8,128)(2,1)S(1)}, bf16[2048,256]{1,0:T(8,128)(2,1)S(1)}, u32[]{:S(2)}, u32[]{:S(2)}) %collective-permute-start) | collective-permute-done | bytes 1048608 | tf_op jit(solution)/shard_map/ppermute | solution.py:26
  111.3 17.7 %attend.1 = (bf16[2048,128]{1,0:T(8,128)(2,1)S(1)}, f32[8,1,256]{2,1,0:T(1,128)S(1)}) custom-call(s32[8]{0:T(128)S(1)} %reshape.344.at_ref, s32[8]{0:T(128)S(1)} %and_select_fusion.4.low_ref, s32[16]{0:T(128)S(1)} %fusion.91.row_ref, bf16[2048,384]{1,0:T(8,128)(2,1)S(1)} %bitcast.80, s32[8,1,256]{2,1,0:T(1,128)S(1)} %reshape.349.first_ref, ...), custom_call_target="tpu_custom_call" | custom-call | flops 1342177280 | bytes 4194304 | tf_op jit(solution)/shard_map/attend/pallas_call | solution.py:179
  130.0 3.5 all-to-all-start.1
  133.7 12.8 %all-to-all-done.1 = bf16[4,512,128]{1,2,0:T(8,128)(2,1)S(1)} async-done(((bf16[4,512,128]{1,2,0:T(8,128)(2,1)}), bf16[4,512,128]{1,2,0:T(8,128)(2,1)S(1)}, u32[]{:S(2)}, u32[]{:S(2)}) %all-to-all-start.1) | async-done | bytes 524320 | tf_op jit(solution)/shard_map/all_to_all | solution.py:315
  150.2 3.0 collective-permute-done.1
  157.4 23.0 %collective-permute-done.2 = bf16[256,2048]{1,0:T(8,128)(2,1)S(1)} collective-permute-done((bf16[256,2048]{1,0:T(8,128)(2,1)S(1)}, bf16[256,2048]{1,0:T(8,128)(2,1)S(1)}, u32[]{:S(2)}, u32[]{:S(2)}) %collective-permute-start.2) | collective-permute-done | bytes 1048608 | tf_op jit(solution)/shard_map/ppermute | solution.py:26
  186.3 12.0 %multiply_convert_fusion.1 = (bf16[512,2048]{1,0:T(8,128)(2,1)}, f32[512,2048]{1,0:T(8,128)}) fusion(s32[2048]{0:T(1024)S(1)} %iota_add_fusion, s32[512]{0:T(512)S(1)} %add_multiply_fusion, bf16[2048,2048]{1,0:T(8,128)(2,1)} %param.20, bf16[256,2048]{1,0:T(8,128)(2,1)} %collective-permute-done.3, bf16[256,2048]{1,0:T(8,128)(2,1)} %add_convert_fusion.6, ...), kind=kOutput, calls=%fused_computation.10 | convolution fusion | flops 4309647360 | bytes 16787456 | tf_op jit(solution)/shard_map/dot_general | solution.py:323
  198.3 6.8 multiply_convert_fusion
  205.1 8.9 %convolution_convert_fusion = bf16[512,2048]{1,0:T(8,128)(2,1)S(1)} fusion(bf16[512,2048]{1,0:T(8,128)(2,1)S(1)} %multiply_convert_fusion, bf16[2048,2048]{1,0:T(8,128)(2,1)} %param.20), kind=kOutput, calls=%fused_computation.22 | convolution fusion | flops 4296015872 | bytes 12582912 | tf_op jit(solution)/shard_map/dot_general | solution.py:64
  214.7 6.3 convolution_convert_fusion.1
  225.8 21.8 %collective-permute-done.8 = bf16[256,2048]{1,0:T(8,128)(2,1)S(1)} collective-permute-done((bf16[256,2048]{1,0:T(8,128)(2,1)S(1)}, bf16[256,2048]{1,0:T(8,128)(2,1)S(1)}, u32[]{:S(2)}, u32[]{:S(2)}) %collective-permute-start.8) | collective-permute-done | bytes 1048608 | tf_op jit(solution)/shard_map/ppermute | solution.py:26
  248.8 20.9 %collective-permute-done.5 = bf16[256,2048]{1,0:T(8,128)(2,1)S(1)} collective-permute-done((bf16[256,2048]{1,0:T(8,128)(2,1)S(1)}, bf16[256,2048]{1,0:T(8,128)(2,1)S(1)}, u32[]{:S(2)}, u32[]{:S(2)}) %collective-permute-start.5) | collective-permute-done | bytes 1048608 | tf_op jit(solution)/shard_map/ppermute | solution.py:26
  269.7 3.5 fusion.99
  275.8 3.6 copy.103
  282.0 3.7 copy.104
  285.7 4.2 maximum_select_fusion.7
  292.5 3.7 copy.99
  298.9 3.6 copy.100
  309.2 35.1 %collective-permute-done.16 = bf16[512,512]{0,1:T(8,128)(2,1)S(1)} collective-permute-done((bf16[512,512]{0,1:T(8,128)(2,1)S(1)}, bf16[512,512]{0,1:T(8,128)(2,1)S(1)}, u32[]{:S(2)}, u32[]{:S(2)}) %collective-permute-start.16) | collective-permute-done | bytes 524320 | tf_op jit(solution)/shard_map/ppermute | solution.py:26
  346.6 3.9 copy.107
  352.5 58.8 %collective-permute-done.21 = bf16[512,1024]{0,1:T(8,128)(2,1)S(1)} collective-permute-done((bf16[512,1024]{0,1:T(8,128)(2,1)S(1)}, bf16[512,1024]{0,1:T(8,128)(2,1)S(1)}, u32[]{:S(2)}, u32[]{:S(2)}) %collective-permute-start.21) | collective-permute-done | bytes 1048608 | tf_op jit(solution)/shard_map/ppermute | solution.py:26
  411.3 8.4 %fusion.8 = bf16[2048,1024]{1,0:T(8,128)(2,1)} fusion(bf16[512,2048]{1,0:T(8,128)(2,1)} %collective-permute-done.20, bf16[512,2048]{1,0:T(8,128)(2,1)} %get-tuple-element.114, bf16[512,1024]{0,1:T(8,128)(2,1)S(1)} %collective-permute-done.21, bf16[512,1024]{0,1:T(8,128)(2,1)S(1)} %bitcast.95), kind=kOutput, calls=%fused_computation.14 | convolution fusion | flops 4309647360 | bytes 10485760 | tf_op jit(solution)/shard_map/dot_general | solution.py:68
  421.9 46.7 %collective-permute-done.19 = bf16[512,2048]{1,0:T(8,128)(2,1)S(1)} collective-permute-done((bf16[512,2048]{1,0:T(8,128)(2,1)}, bf16[512,2048]{1,0:T(8,128)(2,1)S(1)}, u32[]{:S(2)}, u32[]{:S(2)}) %collective-permute-start.19) | collective-permute-done | bytes 2097184 | tf_op jit(solution)/shard_map/ppermute | solution.py:26
  468.6 21.2 %collective-permute-done.18 = bf16[512,1024]{0,1:T(8,128)(2,1)S(1)} collective-permute-done((bf16[512,1024]{0,1:T(8,128)(2,1)}, bf16[512,1024]{0,1:T(8,128)(2,1)S(1)}, u32[]{:S(2)}, u32[]{:S(2)}) %collective-permute-start.18) | collective-permute-done | bytes 1048608 | tf_op jit(solution)/shard_map/ppermute | solution.py:26
  489.8 8.4 %fusion.11 = bf16[1024,2048]{1,0:T(8,128)(2,1)} fusion(bf16[512,2048]{1,0:T(8,128)(2,1)S(1)} %collective-permute-done.19, bf16[512,2048]{1,0:T(8,128)(2,1)} %copy-done.23, bf16[512,1024]{0,1:T(8,128)(2,1)S(1)} %collective-permute-done.18, bf16[512,1024]{0,1:T(8,128)(2,1)} %bitcast.91), kind=kOutput, calls=%fused_computation.15 | convolution fusion | flops 4309647360 | bytes 10485760 | tf_op jit(solution)/shard_map/dot_general | solution.py:68
  498.3 3.6 fusion.65
  501.9 30.8 %all_to_all.20 = bf16[4,512,128]{2,1,0:T(8,128)(2,1)S(1)} all-to-all(bf16[4,512,128]{2,1,0:T(8,128)(2,1)S(1)} %fusion.65), channel_id=1, replica_groups=mesh['r'=1,'h'=4,'y'=2,'x'=2,'c'=2] {'h'}, dimensions={0} | all-to-all | bytes 1048576 | tf_op jit(solution)/shard_map/all_to_all | solution.py:353
  532.7 22.0 %attend_back.1 = (f32[2048,128]{1,0:T(8,128)S(1)}, f32[2048,256]{1,0:T(8,128)}, bf16[2048,256]{1,0:T(8,128)(2,1)S(1)}) custom-call(s32[8]{0:T(128)S(1)} %reshape.344.at_ref, s32[8]{0:T(128)S(1)} %and_select_fusion.4.low_ref, s32[16]{0:T(128)S(1)} %fusion.91.row_ref, bf16[2048,384]{1,0:T(8,128)(2,1)} %bitcast.79, s32[8,1,256]{2,1,0:T(1,128)S(1)} %reshape.349.first_ref, ...), custom_call_target="tpu_custom_call" | custom-call | flops 3355443200 | bytes 8388608 | tf_op jit(solution)/shard_map/attend_back/pallas_call | solution.py:198
  554.8 24.2 %collective-permute-done.10 = bf16[2048,256]{1,0:T(8,128)(2,1)S(1)} collective-permute-done((bf16[2048,256]{1,0:T(8,128)(2,1)S(1)}, bf16[2048,256]{1,0:T(8,128)(2,1)S(1)}, u32[]{:S(2)}, u32[]{:S(2)}) %collective-permute-start.10) | collective-permute-done | bytes 1048608 | tf_op jit(solution)/shard_map/ppermute | solution.py:26
  581.7 5.8 fusion.75
  587.4 4.0 concatenate.98
  594.0 40.2 %all_to_all.21 = bf16[4,512,384]{1,2,0:T(8,128)(2,1)} all-to-all(bf16[4,512,384]{1,2,0:T(8,128)(2,1)} %copy.92), channel_id=1, replica_groups=mesh['r'=1,'h'=4,'y'=2,'x'=2,'c'=2] {'h'}, dimensions={0} | all-to-all | bytes 3145728 | tf_op jit(solution)/shard_map/all_to_all | solution.py:379
  634.2 3.8 copy.93
  638.0 3.7 reshape.356
  642.3 4.5 reshape.357
  646.7 8.6 %constant_dynamic-slice_fusion.7 = (bf16[512,4,1,256]{3,2,1,0:T(2,128)(2,1)}, bf16[512,4,1,256]{3,2,1,0:T(2,128)(2,1)}) fusion(bf16[512,4,2,256]{3,2,1,0:T(2,128)(2,1)} %reshape.357, s32[]{:T(128)S(6)} %select_n.104, s32[]{:T(128)S(6)} %select_n.119), kind=kLoop, calls=%fused_computation.144 | loop fusion | bytes 4194312 | tf_op jit(solution)/shard_map/jit(dynamic_index_in_dim)/dynamic_slice | solution.py:243
  655.4 4.6 copy.112
  662.6 4.6 copy.111
  668.7 30.5 %collective-permute-done.15 = bf16[512,1024]{1,0:T(8,128)(2,1)} collective-permute-done((bf16[512,1024]{1,0:T(8,128)(2,1)}, bf16[512,1024]{1,0:T(8,128)(2,1)}, u32[]{:S(2)}, u32[]{:S(2)}) %collective-permute-start.15) | collective-permute-done | bytes 1048608 | tf_op jit(solution)/shard_map/ppermute | solution.py:26
  699.2 7.7 convert_bitcast_fusion
  707.0 6.7 bitcast_convert_fusion
  718.7 23.5 %collective-permute-done.12 = bf16[256,2048]{1,0:T(8,128)(2,1)S(1)} collective-permute-done((bf16[256,2048]{1,0:T(8,128)(2,1)S(1)}, bf16[256,2048]{1,0:T(8,128)(2,1)S(1)}, u32[]{:S(2)}, u32[]{:S(2)}) %collective-permute-start.12) | collective-permute-done | bytes 1048608 | tf_op jit(solution)/shard_map/ppermute | solution.py:26
  748.6 61.1 %psum.7 = f32[8196]{0:T(1024)S(1)} all-reduce(f32[8196]{0:T(1024)S(1)} %constant_dynamic-update-slice_fusion.1), channel_id=1, replica_groups=mesh['r'=1,'h'=4,'y'=2,'x'=2,'c'=2] {'r','h','y','c'}, use_global_device_ids=true, to_apply=%region_19.20 | all-reduce | flops 8196 | bytes 65568 | tf_op jit(solution)/shard_map/psum | solution.py:406
  813.6 4.3 fusion.34
  (187 shorter events, 99.9 us)
Async XLA Ops:
  7.2 139.3 %copy-start = (bf16[512,2048]{1,0:T(8,128)(2,1)S(1)}, bf16[512,2048]{1,0:T(8,128)(2,1)}, u32[]{:S(2)}) copy-start(bf16[512,2048]{1,0:T(8,128)(2,1)} %param.17) | copy-start | bytes 6291460
  8.2 2.8 copy-start.7
  11.6 8.9 %copy-start.18 = (f32[2048]{0:T(1024)S(1)}, f32[2048]{0:T(1024)}, u32[]{:S(2)}) copy-start(f32[2048]{0:T(1024)} %param.14) | copy-start | bytes 24580
  11.7 8.9 %copy-start.19 = (f32[2048]{0:T(1024)S(1)}, f32[2048]{0:T(1024)}, u32[]{:S(2)}) copy-start(f32[2048]{0:T(1024)} %param.15) | copy-start | bytes 24580
  23.0 6.4 copy-start.11
  32.2 2.9 copy-start.9
  39.7 43.4 %all-to-all-start = ((bf16[4,512,384]{1,2,0:T(8,128)(2,1)}), bf16[4,512,384]{1,2,0:T(8,128)(2,1)}, u32[]{:S(2)}, u32[]{:S(2)}) async-start(bf16[4,512,384]{1,2,0:T(8,128)(2,1)} %fusion.85), calls=%async_computation | async-start | bytes 3145728 | tf_op jit(solution)/shard_map/all_to_all | solution.py:304
  86.9 24.2 %collective-permute-start = (bf16[2048,256]{1,0:T(8,128)(2,1)S(1)}, bf16[2048,256]{1,0:T(8,128)(2,1)S(1)}, u32[]{:S(2)}, u32[]{:S(2)}) collective-permute-start(bf16[2048,256]{1,0:T(8,128)(2,1)S(1)} %slice.89), channel_id=1, source_target_pairs={{0,4},{4,0},{1,5},{5,1},{2,6},{6,2},{3,7},{7,3},{8,12},{12,8},{9,1... | collective-permute-start | bytes 3145736 | tf_op jit(solution)/shard_map/ppermute | solution.py:26
  89.4 21.8 %copy-start.1 = (bf16[4,512,384]{2,1,0:T(8,128)(2,1)S(1)}, bf16[4,512,384]{2,1,0:T(8,128)(2,1)}, u32[]{:S(2)}) copy-start(bf16[4,512,384]{2,1,0:T(8,128)(2,1)} %copy.89) | copy-start | bytes 4718596
  111.3 17.7 %copy-start.2 = (bf16[4096,256]{1,0:T(8,128)(2,1)}, bf16[4096,256]{1,0:T(8,128)(2,1)S(1)}, u32[]{:S(2)}) copy-start(bf16[4096,256]{1,0:T(8,128)(2,1)S(1)} %pad_maximum_fusion.kv_ref) | copy-start | bytes 6291460
  130.0 16.5 %all-to-all-start.1 = ((bf16[4,512,128]{1,2,0:T(8,128)(2,1)}), bf16[4,512,128]{1,2,0:T(8,128)(2,1)S(1)}, u32[]{:S(2)}, u32[]{:S(2)}) async-start(bf16[4,512,128]{1,2,0:T(8,128)(2,1)} %copy.90), calls=%async_computation.1 | async-start | bytes 1048576 | tf_op jit(solution)/shard_map/all_to_all | solution.py:315
  133.4 613.4 %reduce-scatter.7.cloned.1.call-start = ((), (), s32[]{:S(2)}) async-start(), calls=%async_computation.9 | async-start | bytes 1310720 | tf_op jit(solution)/shard_map/reduce_scatter | solution.py:339
  150.1 3.0 collective-permute-start.1
  150.1 6.5 copy-start.8
  155.1 25.3 %collective-permute-start.2 = (bf16[256,2048]{1,0:T(8,128)(2,1)S(1)}, bf16[256,2048]{1,0:T(8,128)(2,1)S(1)}, u32[]{:S(2)}, u32[]{:S(2)}) collective-permute-start(bf16[256,2048]{1,0:T(8,128)(2,1)S(1)} %add_convert_fusion.7), channel_id=1, source_target_pairs={{0,2},{2,0},{1,3},{3,1},{4,6},{6,4},{5,7},{7,5},{8,10},{10,8},{9,1... | collective-permute-start | bytes 3145736 | tf_op jit(solution)/shard_map/ppermute | solution.py:26
  157.2 23.8 %copy-start.5 = (f32[512,2048]{1,0:T(8,128)}, f32[512,2048]{1,0:T(8,128)S(1)}, u32[]{:S(2)}) copy-start(f32[512,2048]{1,0:T(8,128)S(1)} %convert_element_type.171) | copy-start | bytes 12582916
  181.0 2.3 copy-start.3
  183.2 3.0 collective-permute-start.3
  183.3 15.0 %slice-start = ((s8[8388608]{0:T(1024)(128)(4,1)}), s8[4194304]{0:T(1024)(128)(4,1)S(1)}, s32[]{:S(2)}) async-start(s8[8388608]{0:T(1024)(128)(4,1)} %bitcast.103), calls=%async_computation.12 | async-start | bytes 8388608
  183.3 14.9 %copy-start.13 = (bf16[512,2048]{1,0:T(8,128)(2,1)S(1)}, bf16[512,2048]{1,0:T(8,128)(2,1)}, u32[]{:S(2)}) copy-start(bf16[512,2048]{1,0:T(8,128)(2,1)} %param.25) | copy-start | bytes 6291460
  183.3 14.9 %slice-start.1 = ((s8[8388608]{0:T(1024)(128)(4,1)}), s8[4194304]{0:T(1024)(128)(4,1)S(1)}, s32[]{:S(2)}) async-start(s8[8388608]{0:T(1024)(128)(4,1)} %bitcast.103), calls=%async_computation.13 | async-start | bytes 8388608
  205.1 8.9 %copy-start.23 = (bf16[512,2048]{1,0:T(8,128)(2,1)}, bf16[512,2048]{1,0:T(8,128)(2,1)S(1)}, u32[]{:S(2)}) copy-start(bf16[512,2048]{1,0:T(8,128)(2,1)S(1)} %multiply_convert_fusion) | copy-start | bytes 6291460
  214.2 7.1 collective-permute-start.7
  221.1 2.7 collective-permute-start.4
  221.6 26.0 %copy-start.4 = (f32[256,2048]{1,0:T(8,128)S(1)}, f32[256,2048]{1,0:T(8,128)}, u32[]{:S(2)}) copy-start(f32[256,2048]{1,0:T(8,128)} %copy-done.3) | copy-start | bytes 6291460
  221.6 26.0 %collective-permute-start.8 = (bf16[256,2048]{1,0:T(8,128)(2,1)S(1)}, bf16[256,2048]{1,0:T(8,128)(2,1)S(1)}, u32[]{:S(2)}, u32[]{:S(2)}) collective-permute-start(bf16[256,2048]{1,0:T(8,128)(2,1)S(1)} %add_convert_fusion.3), channel_id=1, source_target_pairs={{0,2},{2,0},{1,3},{3,1},{4,6},{6,4},{5,7},{7,5},{8,10},{10,8},{9,1... | collective-permute-start | bytes 3145736 | tf_op jit(solution)/shard_map/ppermute | solution.py:26
  224.2 45.5 %collective-permute-start.5 = (bf16[256,2048]{1,0:T(8,128)(2,1)S(1)}, bf16[256,2048]{1,0:T(8,128)(2,1)S(1)}, u32[]{:S(2)}, u32[]{:S(2)}) collective-permute-start(bf16[256,2048]{1,0:T(8,128)(2,1)S(1)} %add_convert_fusion.5), channel_id=1, source_target_pairs={{0,2},{2,0},{1,3},{3,1},{4,6},{6,4},{5,7},{7,5},{8,10},{10,8},{9,1... | collective-permute-start | bytes 3145736 | tf_op jit(solution)/shard_map/ppermute | solution.py:26
  273.1 23.0 %collective-permute-start.9 = (bf16[256,2048]{1,0:T(8,128)(2,1)}, bf16[256,2048]{1,0:T(8,128)(2,1)}, u32[]{:S(2)}, u32[]{:S(2)}) collective-permute-start(bf16[256,2048]{1,0:T(8,128)(2,1)} %get-tuple-element.86), channel_id=1, source_target_pairs={{0,1},{1,0},{2,3},{3,2},{4,5},{5,4},{6,7},{7,6},{8,9},{9,8},{10,11... | collective-permute-start | bytes 3145736 | tf_op jit(solution)/shard_map/ppermute | solution.py:26
  302.5 2.9 copy-start.10
  307.1 37.2 %collective-permute-start.17 = (bf16[512,1024]{0,1:T(8,128)(2,1)S(1)}, bf16[512,1024]{0,1:T(8,128)(2,1)S(1)}, u32[]{:S(2)}, u32[]{:S(2)}) collective-permute-start(bf16[512,1024]{0,1:T(8,128)(2,1)S(1)} %bitcast.94), channel_id=1, source_target_pairs={{0,4},{4,0},{1,5},{5,1},{2,6},{6,2},{3,7},{7,3},{8,12},{12,8},{9,1... | collective-permute-start | bytes 3145736 | tf_op jit(solution)/shard_map/ppermute | solution.py:26
  307.1 37.2 %collective-permute-start.16 = (bf16[512,512]{0,1:T(8,128)(2,1)S(1)}, bf16[512,512]{0,1:T(8,128)(2,1)S(1)}, u32[]{:S(2)}, u32[]{:S(2)}) collective-permute-start(bf16[512,512]{0,1:T(8,128)(2,1)S(1)} %bitcast.98), channel_id=1, source_target_pairs={{0,4},{4,0},{1,5},{5,1},{2,6},{6,2},{3,7},{7,3},{8,12},{12,8},{9,1... | collective-permute-start | bytes 1572872 | tf_op jit(solution)/shard_map/ppermute | solution.py:26
  309.1 102.2 %collective-permute-start.20 = (bf16[512,2048]{1,0:T(8,128)(2,1)}, bf16[512,2048]{1,0:T(8,128)(2,1)}, u32[]{:S(2)}, u32[]{:S(2)}) collective-permute-start(bf16[512,2048]{1,0:T(8,128)(2,1)} %get-tuple-element.114), channel_id=1, source_target_pairs={{0,4},{4,0},{1,5},{5,1},{2,6},{6,2},{3,7},{7,3},{8,12},{12,8},{9,1... | collective-permute-start | bytes 6291464 | tf_op jit(solution)/shard_map/ppermute | solution.py:26
  346.6 464.3 %reduce-scatter.11.cloned.1.call-start = ((), (), s32[]{:S(2)}) async-start(), calls=%async_computation.11 | async-start | bytes 5242880 | tf_op jit(solution)/shard_map/reduce_scatter | solution.py:339
  352.4 59.0 %collective-permute-start.21 = (bf16[512,1024]{0,1:T(8,128)(2,1)S(1)}, bf16[512,1024]{0,1:T(8,128)(2,1)S(1)}, u32[]{:S(2)}, u32[]{:S(2)}) collective-permute-start(bf16[512,1024]{0,1:T(8,128)(2,1)S(1)} %bitcast.96), channel_id=1, source_target_pairs={{0,4},{4,0},{1,5},{5,1},{2,6},{6,2},{3,7},{7,3},{8,12},{12,8},{9,1... | collective-permute-start | bytes 3145736 | tf_op jit(solution)/shard_map/ppermute | solution.py:26
  419.8 398.1 %reduce-scatter.9.cloned.1.call-start = ((), (), s32[]{:S(2)}) async-start(), calls=%async_computation.10 | async-start | bytes 5242880 | tf_op jit(solution)/shard_map/reduce_scatter | solution.py:339
  419.8 48.8 %collective-permute-start.19 = (bf16[512,2048]{1,0:T(8,128)(2,1)}, bf16[512,2048]{1,0:T(8,128)(2,1)S(1)}, u32[]{:S(2)}, u32[]{:S(2)}) collective-permute-start(bf16[512,2048]{1,0:T(8,128)(2,1)} %copy-done.23), channel_id=1, source_target_pairs={{0,4},{4,0},{1,5},{5,1},{2,6},{6,2},{3,7},{7,3},{8,12},{12,8},{9,1... | collective-permute-start | bytes 6291464 | tf_op jit(solution)/shard_map/ppermute | solution.py:26
  420.2 69.7 %collective-permute-start.18 = (bf16[512,1024]{0,1:T(8,128)(2,1)}, bf16[512,1024]{0,1:T(8,128)(2,1)S(1)}, u32[]{:S(2)}, u32[]{:S(2)}) collective-permute-start(bf16[512,1024]{0,1:T(8,128)(2,1)} %bitcast.92), channel_id=1, source_target_pairs={{0,4},{4,0},{1,5},{5,1},{2,6},{6,2},{3,7},{7,3},{8,12},{12,8},{9,1... | collective-permute-start | bytes 3145736 | tf_op jit(solution)/shard_map/ppermute | solution.py:26
  498.2 322.4 %reduce-scatter.5.cloned.1.call-start = ((), (), s32[]{:S(2)}) async-start(), calls=%async_computation.8 | async-start | bytes 3932160 | tf_op jit(solution)/shard_map/reduce_scatter | solution.py:339
  554.7 24.3 %collective-permute-start.10 = (bf16[2048,256]{1,0:T(8,128)(2,1)S(1)}, bf16[2048,256]{1,0:T(8,128)(2,1)S(1)}, u32[]{:S(2)}, u32[]{:S(2)}) collective-permute-start(bf16[2048,256]{1,0:T(8,128)(2,1)S(1)} %get-tuple-element.22), channel_id=1, source_target_pairs={{0,4},{4,0},{1,5},{5,1},{2,6},{6,2},{3,7},{7,3},{8,12},{12,8},{9,1... | collective-permute-start | bytes 3145736 | tf_op jit(solution)/shard_map/ppermute | solution.py:26
  641.6 57.6 %collective-permute-start.14 = (bf16[512,3,512]{2,0,1:T(8,128)(2,1)}, bf16[512,3,512]{2,0,1:T(8,128)(2,1)}, u32[]{:S(2)}, u32[]{:S(2)}) collective-permute-start(bf16[512,3,512]{2,0,1:T(8,128)(2,1)} %reshape.356), channel_id=1, source_target_pairs={{0,4},{4,0},{1,5},{5,1},{2,6},{6,2},{3,7},{7,3},{8,12},{12,8},{9,1... | collective-permute-start | bytes 4718600 | tf_op jit(solution)/shard_map/ppermute | solution.py:26
  661.2 38.0 %collective-permute-start.15 = (bf16[512,1024]{1,0:T(8,128)(2,1)}, bf16[512,1024]{1,0:T(8,128)(2,1)}, u32[]{:S(2)}, u32[]{:S(2)}) collective-permute-start(bf16[512,1024]{1,0:T(8,128)(2,1)} %copy.96), channel_id=1, source_target_pairs={{0,4},{4,0},{1,5},{5,1},{2,6},{6,2},{3,7},{7,3},{8,12},{12,8},{9,1... | collective-permute-start | bytes 3145736 | tf_op jit(solution)/shard_map/ppermute | solution.py:26
  713.7 28.5 %copy-start.6 = (f32[512,2048]{1,0:T(8,128)S(1)}, f32[512,2048]{1,0:T(8,128)}, u32[]{:S(2)}) copy-start(f32[512,2048]{1,0:T(8,128)} %copy-done.5) | copy-start | bytes 12582916
  713.8 4.8 copy-start.14
  713.8 2.7 collective-permute-start.11
  717.0 25.3 %collective-permute-start.12 = (bf16[256,2048]{1,0:T(8,128)(2,1)S(1)}, bf16[256,2048]{1,0:T(8,128)(2,1)S(1)}, u32[]{:S(2)}, u32[]{:S(2)}) collective-permute-start(bf16[256,2048]{1,0:T(8,128)(2,1)S(1)} %add_convert_fusion.2), channel_id=1, source_target_pairs={{0,2},{2,0},{1,3},{3,1},{4,6},{6,4},{5,7},{7,5},{8,10},{10,8},{9,1... | collective-permute-start | bytes 3145736 | tf_op jit(solution)/shard_map/ppermute | solution.py:26
  718.6 24.8 %copy-start.12 = (f32[256,2048]{1,0:T(8,128)S(1)}, f32[256,2048]{1,0:T(8,128)}, u32[]{:S(2)}) copy-start(f32[256,2048]{1,0:T(8,128)} %get-tuple-element.87) | copy-start | bytes 6291460
  718.6 25.9 %collective-permute-start.6 = (bf16[256,2048]{1,0:T(8,128)(2,1)S(1)}, bf16[256,2048]{1,0:T(8,128)(2,1)S(1)}, u32[]{:S(2)}, u32[]{:S(2)}) collective-permute-start(bf16[256,2048]{1,0:T(8,128)(2,1)S(1)} %copy-done.14), channel_id=1, source_target_pairs={{0,1},{1,0},{2,3},{3,2},{4,5},{5,4},{6,7},{7,6},{8,9},{9,8},{10,11... | collective-permute-start | bytes 3145736 | tf_op jit(solution)/shard_map/ppermute | solution.py:26
  744.4 69.2 %collective-permute-start.13 = (bf16[256,2048]{1,0:T(8,128)(2,1)S(1)}, bf16[256,2048]{1,0:T(8,128)(2,1)}, u32[]{:S(2)}, u32[]{:S(2)}) collective-permute-start(bf16[256,2048]{1,0:T(8,128)(2,1)S(1)} %add_convert_fusion.1), channel_id=1, source_target_pairs={{0,1},{1,0},{2,3},{3,2},{4,5},{5,4},{6,7},{7,6},{8,9},{9,8},{10,11... | collective-permute-start | bytes 3145736 | tf_op jit(solution)/shard_map/ppermute | solution.py:26
  (6 other events, 7.6 us)
Sparse Core Ops, SparseCore 0:
  346.7 25.2 reduce-scatter.6
  419.9 74.8 reduce-scatter.10
  498.3 84.4 reduce-scatter.8
  707.1 59.1 reduce-scatter.4

commit v2 on v1

v2 whole, which is shorter than its diff:
```python
import functools
import math

import jax
import jax.numpy as jnp
from jax import lax
from jax.experimental import pallas as pl
from jax.experimental.pallas import tpu as pltpu
from jax.sharding import Mesh
from jax.sharding import PartitionSpec as P

HD = 128
FF = 8192
NB = 4
HEADS = 4
EPSILON = 1e-05
ROPE_BASE = 10000.0
BLK = ("r", "h", "y")
TP = ("x", "c")
F32 = jnp.float32
BF16 = jnp.bfloat16
SMEM = pl.BlockSpec(memory_space=pltpu.SMEM)
VMEM = pl.BlockSpec(memory_space=pltpu.VMEM)


def swap(value, axis):
    return lax.ppermute(value, axis, [(0, 1), (1, 0)])


def plane_swap(value, k):
    return lax.ppermute(value, "h", [(i, i ^ k) for i in range(HEADS)])


def ordered(*values):
    return lax.optimization_barrier(values)


def nt(lhs, rhs):
    return lax.dot_general(lhs, rhs, (((1,), (1,)), ((), ())), preferred_element_type=F32)


def tn(lhs, rhs):
    return lax.dot_general(lhs, rhs, (((0,), (0,)), ((), ())), preferred_element_type=F32)


def nn(lhs, rhs):
    return lax.dot_general(lhs, rhs, (((1,), (0,)), ((), ())), preferred_element_type=F32)


def params(mib, **more):
    return pltpu.CompilerParams(vmem_limit_bytes=mib * 2**20, **more)


def cost(flops, moved):
    return pl.CostEstimate(flops=int(flops), bytes_accessed=int(moved), transcendentals=0)


def whole(shape):
    return pl.BlockSpec(shape, lambda *_: (0,) * len(shape))


def normalise(values):
    centre = values - jnp.mean(values, axis=-1, keepdims=True)
    inverse = lax.rsqrt(jnp.mean(centre * centre, axis=-1, keepdims=True) + EPSILON)
    return (centre * inverse, inverse)


def rotary_tables(positions):
    freqs = ROPE_BASE ** (-(jnp.arange(HD // 2, dtype=F32) * 2.0 / HD))
    angles = positions.astype(F32)[:, None] * freqs[None, :]
    cosine, sine = jnp.cos(angles), jnp.sin(angles)
    return (
        jnp.concatenate([cosine, cosine], axis=-1),
        jnp.concatenate([-sine, sine], axis=-1),
    )


def rotate(values, cosine, sine):
    return values * cosine + pltpu.roll(values, HD // 2, 1) * sine


def project_kernel(idx, x_ref, gain_ref, bias_ref, cos_ref, sin_ref, w_ref, *refs):
    outs, h_ref = refs[:HEADS], refs[HEADS]
    step = pl.program_id(0)

    @pl.when(step == 0)
    def _():
        normed, _ = normalise(x_ref[...].astype(F32))
        h_ref[...] = (normed * gain_ref[...] + bias_ref[...]).astype(BF16)

    both = nn(h_ref[...], jnp.concatenate([w_ref[0], w_ref[1]], axis=1))
    cosine, sine = cos_ref[...], sin_ref[...]
    queries = rotate(both[:, :HD], cosine, sine).astype(BF16)
    keys = rotate(both[:, HD:], cosine, sine).astype(BF16)
    values = nn(h_ref[...], w_ref[2]).astype(BF16)
    for k, out in enumerate(outs):

        @pl.when(step == k)
        def _(out=out):
            out[:, :HD] = queries
            out[:, HD : 2 * HD] = keys
            out[:, 2 * HD :] = values


def project(idx, x, gain, bias, cosine, sine, w_qkv):
    tok, dim = x.shape
    return pl.pallas_call(
        project_kernel,
        grid_spec=pltpu.PrefetchScalarGridSpec(
            num_scalar_prefetch=1,
            grid=(HEADS,),
            in_specs=[
                whole((tok, dim)),
                whole((1, dim)),
                whole((1, dim)),
                whole((tok, HD)),
                whole((tok, HD)),
                pl.BlockSpec((3, dim, HD), lambda k, idx: (0, 0, idx[0] ^ k)),
            ],
            out_specs=[whole((tok, 3 * HD))] * HEADS,
            scratch_shapes=[pltpu.VMEM((tok, dim), BF16)],
        ),
        out_shape=[jax.ShapeDtypeStruct((tok, 3 * HD), BF16)] * HEADS,
        compiler_params=params(40),
        cost_estimate=cost(2 * tok * dim * 12 * HD, 10 * 2**20),
        name="project",
    )(idx, x, gain, bias, cosine, sine, w_qkv)


def visible_of(tile, key_block, query_places, query_firsts):
    key_places = key_block * tile + lax.broadcasted_iota(jnp.int32, (tile, 1), 0)
    return (key_places <= query_places) & (key_places >= query_firsts)


def gather_refs(q_refs, kv_refs, lane0s, q_all, kv_all):
    at = 0
    for ref in q_refs:
        q_all[at : at + ref.shape[0], :] = ref[:, :HD]
        at += ref.shape[0]
    at = 0
    for ref, lane0 in zip(kv_refs, lane0s, strict=True):
        kv_all[at : at + ref.shape[0], :] = ref[:, lane0 : lane0 + 2 * HD]
        at += ref.shape[0]


def attend_kernel(tile, scale, lane0s, near_is_q, at_ref, low_ref, row_ref, first_ref, *refs):
    n_kv = len(lane0s)
    q_refs = refs[:HEADS]
    kv_refs = refs[:n_kv] if near_is_q else refs[HEADS : HEADS + n_kv]
    n_in = n_kv if near_is_q else HEADS + n_kv
    outs = refs[n_in : n_in + HEADS]
    lse_ref, q_all, kv_all = refs[n_in + HEADS :]
    gather_refs(q_refs, kv_refs, lane0s, q_all, kv_all)
    lanes = lax.broadcasted_iota(jnp.int32, (1, tile), 1)
    per_out = outs[0].shape[0] // tile

    for k, out in enumerate(outs):

        def one_block(j, carry, k=k, out=out):
            i = k * per_out + j
            queries = q_all[pl.ds(pl.multiple_of(i * tile, tile), tile), :]
            firsts = first_ref[i]
            places = at_ref[i] * tile + lanes

            def one_step(b, state):
                run_max, run_sum, run_acc = state
                krows = pl.ds(pl.multiple_of(row_ref[b] * tile, tile), tile)
                scores = nt(kv_all[krows, :HD], queries) * scale
                visible = visible_of(tile, b, places, firsts)
                scores = jnp.where(visible, scores, -1e30)
                new_max = jnp.maximum(run_max, jnp.max(scores, axis=0, keepdims=True))
                factor = jnp.exp(run_max - new_max)
                probs = jnp.where(visible, jnp.exp(scores - new_max), 0.0)
                new_sum = run_sum * factor + jnp.sum(probs, axis=0, keepdims=True)
                new_acc = run_acc * factor + tn(kv_all[krows, HD:], probs.astype(BF16))
                return (new_max, new_sum, new_acc)

            run_max, run_sum, run_acc = lax.fori_loop(
                low_ref[i],
                at_ref[i] + 1,
                one_step,
                (
                    jnp.full((1, tile), -1e30, F32),
                    jnp.zeros((1, tile), F32),
                    jnp.zeros((HD, tile), F32),
                ),
            )
            out[pl.ds(pl.multiple_of(j * tile, tile), tile), :] = (run_acc / run_sum).T.astype(BF16)
            lse_ref[i] = run_max + jnp.log(run_sum)
            return carry

        lax.fori_loop(0, per_out, one_block, 0)


def attend_back_kernel(
    tile, scale, lane0s, near_is_q, at_ref, low_ref, row_ref, first_ref, lse_ref, cos_ref, sin_ref, *refs
):
    n_kv = len(lane0s)
    q_refs = refs[:HEADS]
    kv_refs = refs[:n_kv] if near_is_q else refs[HEADS : HEADS + n_kv]
    refs = refs[n_kv if near_is_q else HEADS + n_kv :]
    o_refs, do_refs, dq_refs = refs[:HEADS], refs[HEADS : 2 * HEADS], refs[2 * HEADS : 3 * HEADS]
    near_ref, far_ref, q_all, kv_all, acc_ref = refs[3 * HEADS :]
    gather_refs(q_refs, kv_refs, lane0s, q_all, kv_all)
    acc_ref[...] = jnp.zeros_like(acc_ref)
    lanes = lax.broadcasted_iota(jnp.int32, (1, tile), 1)
    per_out = dq_refs[0].shape[0] // tile

    for k in range(HEADS):

        def one_block(j, carry, k=k):
            i = k * per_out + j
            rows = pl.ds(pl.multiple_of(i * tile, tile), tile)
            piece = pl.ds(pl.multiple_of(j * tile, tile), tile)
            queries = q_all[rows, :]
            grads = do_refs[k][piece, :]
            firsts = first_ref[i]
            places = at_ref[i] * tile + lanes
            log_sums = lse_ref[i]
            products = grads.astype(F32) * o_refs[k][piece, :].astype(F32)
            deltas = jnp.sum(products.T, axis=0, keepdims=True)

            def one_step(b, grad_q):
                krows = pl.ds(pl.multiple_of(row_ref[b] * tile, tile), tile)
                keys = kv_all[krows, :HD]
                scores = nt(keys, queries) * scale
                visible = visible_of(tile, b, places, firsts)
                probs = jnp.where(visible, jnp.exp(scores - log_sums), 0.0)
                grad_probs = nt(kv_all[krows, HD:], grads)
                grad_scores = (probs * (grad_probs - deltas)).astype(BF16)
                acc_ref[krows, HD:] += nn(probs.astype(BF16), grads)
                acc_ref[krows, :HD] += nn(grad_scores, queries)
                return grad_q + tn(keys, grad_scores)

            grad_q = lax.fori_loop(low_ref[i], at_ref[i] + 1, one_step, jnp.zeros((HD, tile), F32))
            dq_refs[k][piece, :] = rotate(
                (grad_q * scale).T, cos_ref[rows, :], -sin_ref[rows, :]
            ).astype(BF16)
            return carry

        lax.fori_loop(0, per_out, one_block, 0)
    near = near_ref.shape[0]
    near_ref[:, :HD] = (acc_ref[:near, :HD] * scale).astype(BF16)
    near_ref[:, HD:] = acc_ref[:near, HD:].astype(BF16)
    far_ref[:, :HD] = (acc_ref[near:, :HD] * scale).astype(BF16)
    far_ref[:, HD:] = acc_ref[near:, HD:].astype(BF16)


def attend(tile, scale, tables, pieces, keys_values, lane0s, near_is_q):
    rows = HEADS * pieces[0].shape[0]
    kv_rows = sum(a.shape[0] for a in keys_values)
    operands = keys_values if near_is_q else pieces + keys_values
    return pl.pallas_call(
        functools.partial(attend_kernel, tile, scale, lane0s, near_is_q),
        out_shape=[jax.ShapeDtypeStruct((rows // HEADS, HD), BF16)] * HEADS
        + [jax.ShapeDtypeStruct((rows // tile, 1, tile), F32)],
        in_specs=[SMEM] * 3 + [VMEM] * (1 + len(operands)),
        out_specs=[VMEM] * (HEADS + 1),
        scratch_shapes=[pltpu.VMEM((rows, HD), BF16), pltpu.VMEM((kv_rows, 2 * HD), BF16)],
        compiler_params=params(50),
        cost_estimate=cost(4 * rows * 1280 * HD, 4 * 2**20),
        name="attend",
    )(*tables, *operands)


def attend_back(
    tile, scale, tables, lse, cosine, sine, pieces, keys_values, lane0s, near_is_q, outs, grads
):
    rows = HEADS * pieces[0].shape[0]
    kv_rows = sum(a.shape[0] for a in keys_values)
    operands = (keys_values if near_is_q else pieces + keys_values) + outs + grads
    return pl.pallas_call(
        functools.partial(attend_back_kernel, tile, scale, lane0s, near_is_q),
        out_shape=[jax.ShapeDtypeStruct((rows // HEADS, HD), BF16)] * HEADS
        + [jax.ShapeDtypeStruct((kv_rows // 2, 2 * HD), BF16)] * 2,
        in_specs=[SMEM] * 3 + [VMEM] * (4 + len(operands)),
        out_specs=[VMEM] * (HEADS + 2),
        scratch_shapes=[
            pltpu.VMEM((rows, HD), BF16),
            pltpu.VMEM((kv_rows, 2 * HD), BF16),
            pltpu.VMEM((kv_rows, 2 * HD), F32),
        ],
        compiler_params=params(56),
        cost_estimate=cost(10 * rows * 1280 * HD, 8 * 2**20),
        name="attend_back",
    )(*tables, lse, cosine, sine, *operands)


def settle_kernel(near_ref, got_ref, cos_ref, sin_ref, out_ref):
    total = near_ref[...].astype(F32) + got_ref[...].astype(F32)
    out_ref[:, :HD] = rotate(total[:, :HD], cos_ref[...], -sin_ref[...]).astype(BF16)
    out_ref[:, HD:] = total[:, HD:].astype(BF16)


def settle(near, got, cosine, sine):
    rows = near.shape[0]
    tile = rows // HEADS
    spec = pl.BlockSpec((tile, 2 * HD), lambda k: (k, 0))
    table = pl.BlockSpec((tile, HD), lambda k: (k, 0))
    return pl.pallas_call(
        settle_kernel,
        grid=(HEADS,),
        out_shape=jax.ShapeDtypeStruct(near.shape, BF16),
        in_specs=[spec, spec, table, table],
        out_specs=spec,
        compiler_params=params(24),
        cost_estimate=cost(rows * 1024, 5 * 2**20),
        name="settle",
    )(near, got, cosine, sine)


def out_project_kernel(idx, w_ref, *refs):
    pieces, (flat_ref, keep_ref, give_ref) = refs[:HEADS], refs[HEADS:]
    for k, piece in enumerate(pieces):
        flat_ref[:, pl.ds(pl.multiple_of((idx[0] ^ k) * HD, HD), HD)] = piece[...]
    half = keep_ref.shape[0]
    core = idx[2]
    mine = flat_ref[pl.ds(pl.multiple_of(core * half, half), half), :]
    other = flat_ref[pl.ds(pl.multiple_of((1 - core) * half, half), half), :]
    give_ref[...] = nn(other, w_ref[...]).astype(BF16)
    keep_ref[...] = nn(mine, w_ref[...]).astype(BF16)


def out_project(idx, w_out, pieces):
    cols, dim = w_out.shape
    tok = pieces[0].shape[0]
    half = jax.ShapeDtypeStruct((tok // 2, dim), BF16)
    return pl.pallas_call(
        out_project_kernel,
        out_shape=[jax.ShapeDtypeStruct((tok, cols), BF16), half, half],
        in_specs=[SMEM] + [VMEM] * (1 + HEADS),
        out_specs=[VMEM] * 3,
        compiler_params=params(40),
        cost_estimate=cost(2 * tok * dim * cols, 6 * 2**20),
        name="out_project",
    )(idx, w_out, *pieces)


def out_back_kernel(idx, w_ref, mine_ref, other_ref, *outs):
    half = mine_ref.shape[0]
    core = idx[2]
    for k, out in enumerate(outs):
        weights = w_ref[pl.ds(pl.multiple_of((idx[0] ^ k) * HD, HD), HD), :]
        out[pl.ds(pl.multiple_of(core * half, half), half), :] = nt(mine_ref[...], weights).astype(BF16)
        out[pl.ds(pl.multiple_of((1 - core) * half, half), half), :] = nt(
            other_ref[...], weights
        ).astype(BF16)


def out_back(idx, w_out, mine, other):
    half, dim = mine.shape
    return pl.pallas_call(
        out_back_kernel,
        out_shape=[jax.ShapeDtypeStruct((2 * half, HD), BF16)] * HEADS,
        in_specs=[SMEM] + [VMEM] * 3,
        out_specs=[VMEM] * HEADS,
        compiler_params=params(40),
        cost_estimate=cost(4 * half * dim * HEADS * HD, 5 * 2**20),
        name="out_back",
    )(idx, w_out, mine, other)


def norm_kernel(x_ref, chip_ref, far_ref, gain_ref, bias_ref, sum_ref, out_ref):
    total = x_ref[...].astype(F32) + (chip_ref[...].astype(F32) + far_ref[...].astype(F32))
    sum_ref[...] = total
    normed, _ = normalise(total)
    out_ref[...] = (normed * gain_ref[...] + bias_ref[...]).astype(BF16)


def norm(x, chip, far, gain, bias):
    rows, dim = x.shape
    tile = rows // 4
    spec = pl.BlockSpec((tile, dim), lambda i: (i, 0))
    return pl.pallas_call(
        norm_kernel,
        grid=(4,),
        out_shape=[jax.ShapeDtypeStruct((rows, dim), F32), jax.ShapeDtypeStruct((rows, dim), BF16)],
        in_specs=[spec, spec, spec, whole((1, dim)), whole((1, dim))],
        out_specs=[spec, spec],
        compiler_params=params(24),
        cost_estimate=cost(16 * rows * dim, 12 * rows * dim),
        name="norm",
    )(x, chip, far, gain, bias)


def norm_all_kernel(x_ref, gain_ref, bias_ref, out_ref):
    normed, _ = normalise(x_ref[...].astype(F32))
    out_ref[...] = (normed * gain_ref[...] + bias_ref[...]).astype(BF16)


def norm_all(x, gain, bias):
    rows, dim = x.shape
    tile = 128
    spec = pl.BlockSpec((tile, dim), lambda i: (i, 0))
    return pl.pallas_call(
        norm_all_kernel,
        grid=(rows // tile,),
        out_shape=jax.ShapeDtypeStruct((rows, dim), BF16),
        in_specs=[spec, whole((1, dim)), whole((1, dim))],
        out_specs=spec,
        compiler_params=params(24),
        cost_estimate=cost(16 * rows * dim, 4 * rows * dim),
        name="norm_all",
    )(x, gain, bias)


def norm_back_kernel(chip_ref, far_ref, x_ref, base_ref, gain_ref, wide_ref, low_ref, dg_ref, db_ref):
    grad = chip_ref[...].astype(F32) + far_ref[...].astype(F32)
    normed, inverse = normalise(x_ref[...].astype(F32))
    scaled = grad * gain_ref[...]
    back = inverse * (
        scaled
        - jnp.mean(scaled, axis=-1, keepdims=True)
        - normed * jnp.mean(scaled * normed, axis=-1, keepdims=True)
    )
    total = base_ref[...].astype(F32) + back
    wide_ref[...] = total
    low_ref[...] = total.astype(BF16)

    @pl.when(pl.program_id(0) == 0)
    def _():
        dg_ref[...] = jnp.zeros_like(dg_ref)
        db_ref[...] = jnp.zeros_like(db_ref)

    dg_ref[...] += jnp.sum(grad * normed, axis=0, keepdims=True)
    db_ref[...] += jnp.sum(grad, axis=0, keepdims=True)


def norm_back(chip, far, x, base, gain):
    rows, dim = chip.shape
    tile = rows // 4
    spec = pl.BlockSpec((tile, dim), lambda i: (i, 0))
    row = whole((1, dim))
    return pl.pallas_call(
        norm_back_kernel,
        grid=(4,),
        out_shape=[
            jax.ShapeDtypeStruct((rows, dim), F32),
            jax.ShapeDtypeStruct((rows, dim), BF16),
            jax.ShapeDtypeStruct((1, dim), F32),
            jax.ShapeDtypeStruct((1, dim), F32),
        ],
        in_specs=[spec] * 4 + [row],
        out_specs=[spec, spec, row, row],
        compiler_params=params(24),
        cost_estimate=cost(30 * rows * dim, 18 * rows * dim),
        name="norm_back",
    )(chip, far, x, base, gain)


def feed_kernel(mine_ref, other_ref, w_ref, gact_ref, keep_ref, act_ref, du_ref, *refs):
    half = mine_ref.shape[0]
    weights = w_ref[...]
    for at, ref in ((0, mine_ref), (half, other_ref)):
        rows = slice(at, at + half)
        relu = jnp.maximum(nn(ref[...], weights), 0.0) * keep_ref[rows, :]
        act_ref[rows, :] = (relu * relu).astype(BF16)
        du_ref[rows, :] = (gact_ref[rows, :].astype(F32) * 2.0 * relu).astype(BF16)
    if refs:
        keep_out, give_out, acc_ref = refs
        step = pl.program_id(0)

        @pl.when(step == 0)
        def _():
            acc_ref[...] = nt(du_ref[...], weights)

        @pl.when(step > 0)
        def _():
            acc_ref[...] += nt(du_ref[...], weights)

        @pl.when(step == pl.num_programs(0) - 1)
        def _():
            keep_out[...] = acc_ref[:half, :].astype(BF16)
            give_out[...] = acc_ref[half:, :].astype(BF16)


def feed_forward(mine, other, w_up, gact, keep, with_back):
    half, dim = mine.shape
    hidden = w_up.shape[1]
    tile = min(hidden, 512)
    tall = jax.ShapeDtypeStruct((2 * half, hidden), BF16)
    part = jax.ShapeDtypeStruct((half, dim), BF16)
    spec = pl.BlockSpec((2 * half, tile), lambda i: (0, i))
    return pl.pallas_call(
        feed_kernel,
        grid=(hidden // tile,),
        out_shape=[tall, tall] + ([part, part] if with_back else []),
        in_specs=[
            whole((half, dim)),
            whole((half, dim)),
            pl.BlockSpec((dim, tile), lambda i: (0, i)),
            spec,
            whole((2 * half, 1)),
        ],
        out_specs=[spec, spec] + ([whole((half, dim))] * 2 if with_back else []),
        scratch_shapes=[pltpu.VMEM((2 * half, dim), F32)] if with_back else [],
        compiler_params=params(48),
        cost_estimate=cost((8 if with_back else 4) * half * dim * hidden, 16 * 2**20),
        name="feed_own" if with_back else "feed_far",
    )(mine, other, w_up, gact, keep)


def product_kernel(idx, *refs):
    cols, near_ref, far_ref, out_ref, turn_ref = refs[:4], refs[4], refs[5], refs[6], refs[7]
    half = cols[0].shape[0]
    for k, ref in enumerate(cols):
        turn_ref[:, k * half : (k + 1) * half] = ref[...].astype(F32).T.astype(BF16)
    width = out_ref.shape[1]
    tile = min(width, 512)
    starts = [pl.multiple_of(idx[3 + j] * half, half) for j in range(2)]
    for at in range(0, width, tile):
        lanes = slice(at, at + tile)
        total = None
        for k in range(4):
            rows = (near_ref, far_ref)[k // 2][pl.ds(starts[k % 2], half), lanes]
            term = nn(turn_ref[:, k * half : (k + 1) * half], rows)
            total = term if total is None else total + term
        out_ref[:, lanes] = total.astype(BF16)


def product(idx, cols, near, far):
    half, dim = cols[0].shape
    tok, width = near.shape
    block = dim // (2 * HEADS)
    spec = pl.BlockSpec((half, block), lambda k, idx: (0, 2 * k + idx[1]))
    return pl.pallas_call(
        product_kernel,
        grid_spec=pltpu.PrefetchScalarGridSpec(
            num_scalar_prefetch=1,
            grid=(HEADS,),
            in_specs=[spec] * 4 + [whole((tok, width))] * 2,
            out_specs=pl.BlockSpec((block, width), lambda k, idx: (k, 0)),
            scratch_shapes=[pltpu.VMEM((block, 4 * half), BF16)],
        ),
        out_shape=jax.ShapeDtypeStruct((HEADS * block, width), BF16),
        compiler_params=params(40),
        cost_estimate=cost(2 * tok * width * dim, 12 * 2**20),
        name="product",
    )(idx, *cols, near, far)


def head_product_kernel(idx, h_ref, dkv_ref, *refs):
    dq_refs, (give_ref, keep_ref, turn_ref) = refs[:HEADS], refs[HEADS:]
    tok = dq_refs[0].shape[0]
    first = (pl.program_id(0) == 0) & (pl.program_id(1) == 0)

    @pl.when(first)
    def _():
        for k, ref in enumerate(dq_refs):
            turn_ref[:HD, k * tok : (k + 1) * tok] = ref[...].astype(F32).T.astype(BF16)
            rows = slice(k * tok, (k + 1) * tok)
            turn_ref[HD:, rows] = dkv_ref[rows, :].astype(F32).T.astype(BF16)

    total = None
    for k in range(HEADS):
        rows = h_ref[pl.ds(pl.multiple_of((idx[0] ^ k) * tok, tok), tok), :]
        term = nn(turn_ref[:, k * tok : (k + 1) * tok], rows)
        total = term if total is None else total + term

    @pl.when(pl.program_id(0) == 0)
    def _():
        give_ref[0] = total.astype(BF16)

    @pl.when(pl.program_id(0) == 1)
    def _():
        keep_ref[0] = total.astype(BF16)


def head_product(idx, h_all, dkv, dq_pieces):
    rows, dim = h_all.shape
    block = dim // (2 * HEADS)
    out = jax.ShapeDtypeStruct((HEADS, 3 * HD, block), BF16)

    def columns(turn, k, idx):
        return (0, (idx[0] ^ k) * 2 + jnp.where(turn == 0, 1 - idx[1], idx[1]))

    return pl.pallas_call(
        head_product_kernel,
        grid_spec=pltpu.PrefetchScalarGridSpec(
            num_scalar_prefetch=1,
            grid=(2, HEADS),
            in_specs=[pl.BlockSpec((rows, block), columns), whole((rows, 2 * HD))]
            + [whole((rows // HEADS, HD))] * HEADS,
            out_specs=[
                pl.BlockSpec(
                    (1, 3 * HD, block),
                    lambda turn, k, idx: (jnp.where(turn == 0, k, HEADS - 1), 0, 0),
                ),
                pl.BlockSpec(
                    (1, 3 * HD, block), lambda turn, k, idx: (jnp.where(turn == 0, 0, k), 0, 0)
                ),
            ],
            scratch_shapes=[pltpu.VMEM((3 * HD, rows), BF16)],
        ),
        out_shape=[out, out],
        compiler_params=params(40),
        cost_estimate=cost(2 * rows * dim * 3 * HD, 12 * 2**20),
        name="head_product",
    )(idx, h_all, dkv, *dq_pieces)


def head_place_kernel(idx, *refs):
    pieces, out_ref = refs[:HEADS], refs[HEADS]
    for k, piece in enumerate(pieces):
        for s in range(3):
            out_ref[s, :, pl.ds(pl.multiple_of((idx[0] ^ k) * HD, HD), HD)] = (
                piece[s * HD : (s + 1) * HD, :].astype(F32).T
            )


def head_place(idx, pieces):
    rows, block = pieces[0].shape
    return pl.pallas_call(
        head_place_kernel,
        out_shape=jax.ShapeDtypeStruct((3, block, HEADS * HD), F32),
        in_specs=[SMEM] + [VMEM] * HEADS,
        out_specs=VMEM,
        compiler_params=params(24),
        cost_estimate=cost(rows * block * 8, 4 * 2**20),
        name="head_place",
    )(idx, *pieces)


def project_back_kernel(idx, w_ref, *refs):
    dq_refs, dkv_refs = refs[:HEADS], refs[HEADS : 2 * HEADS]
    keep_ref, give_ref, flat_ref, acc_ref = refs[2 * HEADS :]
    half = keep_ref.shape[0]
    core = idx[2]
    step = pl.program_id(0)

    for s in range(3):

        @pl.when(step == s)
        def _(s=s):
            for k in range(HEADS):
                lanes = pl.ds(pl.multiple_of((idx[0] ^ k) * HD, HD), HD)
                if s == 0:
                    flat_ref[:, lanes] = dq_refs[k][...]
                else:
                    flat_ref[:, lanes] = dkv_refs[k][:, (s - 1) * HD : s * HD]

    @pl.when(step == 0)
    def _():
        acc_ref[...] = nt(flat_ref[...], w_ref[0])

    @pl.when(step > 0)
    def _():
        acc_ref[...] += nt(flat_ref[...], w_ref[0])

    @pl.when(step == 2)
    def _():
        give_ref[...] = acc_ref[pl.ds(pl.multiple_of((1 - core) * half, half), half), :].astype(BF16)
        keep_ref[...] = acc_ref[pl.ds(pl.multiple_of(core * half, half), half), :].astype(BF16)


def project_back(idx, w_qkv, dq_pieces, dkv_pieces):
    tok = dq_pieces[0].shape[0]
    _, dim, cols = w_qkv.shape
    part = jax.ShapeDtypeStruct((tok // 2, dim), BF16)
    return pl.pallas_call(
        project_back_kernel,
        grid_spec=pltpu.PrefetchScalarGridSpec(
            num_scalar_prefetch=1,
            grid=(3,),
            in_specs=[pl.BlockSpec((1, dim, cols), lambda s, idx: (s, 0, 0))]
            + [whole((tok, HD))] * HEADS
            + [whole((tok, 2 * HD))] * HEADS,
            out_specs=[whole((tok // 2, dim))] * 2,
            scratch_shapes=[pltpu.VMEM((tok, cols), BF16), pltpu.VMEM((tok, dim), F32)],
        ),
        out_shape=[part, part],
        compiler_params=params(40),
        cost_estimate=cost(6 * tok * dim * cols, 12 * 2**20),
        name="project_back",
    )(idx, w_qkv, *dq_pieces, *dkv_pieces)


def join_kernel(idx, mine_ref, other_ref, out_ref):
    half = mine_ref.shape[0]
    core = idx[2]
    out_ref[pl.ds(pl.multiple_of(core * half, half), half), :] = mine_ref[...].astype(out_ref.dtype)
    out_ref[pl.ds(pl.multiple_of((1 - core) * half, half), half), :] = other_ref[...].astype(
        out_ref.dtype
    )


def join(idx, mine, other, dtype):
    half, dim = mine.shape
    return pl.pallas_call(
        join_kernel,
        out_shape=jax.ShapeDtypeStruct((2 * half, dim), dtype),
        in_specs=[SMEM, VMEM, VMEM],
        out_specs=VMEM,
        compiler_params=params(24),
        cost_estimate=cost(half * dim, 8 * half * dim),
        name="join",
    )(idx, mine, other)


def body(
    depth,
    layer_input,
    ln1_gain,
    ln1_bias,
    w_qkv,
    w_out,
    ln2_gain,
    ln2_bias,
    w_up,
    w_down,
    buckets,
    lengths,
    block_order,
    grad_out,
):
    tok, dim = layer_input.shape
    half = tok // 2
    scale = 1.0 / math.sqrt(HD)
    r, h, y, x, c = (lax.axis_index(a) for a in BLK + TP)
    blk = lax.axis_index(BLK)
    tp = lax.axis_index(TP)
    idx = jnp.stack([h, y, c, jnp.zeros_like(c), jnp.ones_like(c)]).astype(jnp.int32)
    idx_rows = jnp.stack([h, y, c, c, 1 - c]).astype(jnp.int32)
    gains = [v.reshape(1, dim) for v in (ln1_gain, ln1_bias, ln2_gain, ln2_bias)]

    def half_of(values, which):
        return lax.dynamic_slice_in_dim(values, which * half, half, 0)

    def regroup(values):
        if depth == 1:
            return values
        rows = values.shape[0]
        split = values.reshape(rows, depth, HEADS, 2, dim // (2 * HEADS * depth))
        return split.transpose(0, 2, 3, 1, 4).reshape(rows, dim)

    def scatter(values):
        if depth > 1:
            split = values.reshape(HEADS, depth, -1, values.shape[1])
            values = split.transpose(1, 0, 2, 3).reshape(values.shape)
        return lax.psum_scatter(values, ("r", "h"), scatter_dimension=0, tiled=True)

    starts = jnp.cumsum(lengths) - lengths

    def firsts_of(places):
        return jnp.max(jnp.where(starts <= places[..., None], starts, 0), axis=-1)

    inside = jnp.arange(half, dtype=jnp.int32)
    own_places = (
        lax.dynamic_slice_in_dim(block_order, 2 * blk, 2, 0)[:, None] * half + inside
    ).reshape(tok)
    cosine, sine = rotary_tables(own_places - firsts_of(own_places))

    grad_mine, grad_other = half_of(grad_out, c), half_of(grad_out, 1 - c)
    far_grad_mine = swap(grad_mine, "y")

    packed = list(project(idx, layer_input, gains[0], gains[1], cosine, sine, w_qkv))
    packed = [packed[0]] + [plane_swap(packed[k], k) for k in range(1, HEADS)]

    relative = h ^ jnp.arange(HEADS, dtype=jnp.int32)
    group_order = lax.dynamic_index_in_dim(
        block_order.reshape(depth, HEADS, 2, 2), r, 0, keepdims=False
    )
    group_order = lax.dynamic_index_in_dim(group_order, y, 1, keepdims=False)
    chosen = relative[:, None] == jnp.arange(HEADS, dtype=jnp.int32)[None, :]
    query_at = jnp.sum(jnp.where(chosen[:, :, None], group_order[None], 0), axis=1).reshape(-1)
    query_places = query_at[:, None] * half + inside
    query_firsts = firsts_of(query_places)
    query_low = query_firsts[:, 0] // half
    block_count = block_order.shape[0]
    slots = jnp.argmax(
        block_order[None, :] == jnp.arange(block_count, dtype=jnp.int32)[:, None], axis=1
    ).astype(jnp.int32)
    slot_dev = slots // 2
    slot_plane = slot_dev // 2
    key_row = (
        jnp.where(slot_dev % 2 == y, 0, block_count // 2)
        + slot_plane // HEADS * (2 * HEADS)
        + ((slot_plane % HEADS) ^ h) * 2
        + slots % 2
    )
    group_cos, group_sin = rotary_tables((query_places - query_firsts).reshape(2 * HEADS * half))
    tables = (query_at, query_low, key_row, query_firsts.reshape(2 * HEADS, 1, half))

    if depth == 1:
        far_a = swap(jnp.concatenate([packed[0][:, HD:], packed[1][:, HD:]]), "y")
        far_b = swap(jnp.concatenate([packed[2][:, HD:], packed[3][:, HD:]]), "y")
        keys_values, lane0s, near_is_q = packed + [far_a, far_b], [HD] * HEADS + [0, 0], True
    else:
        near_kv = lax.all_gather(
            jnp.concatenate([p[:, HD:] for p in packed]), "r", axis=0, tiled=True
        )
        keys_values, lane0s, near_is_q = [near_kv, swap(near_kv, "y")], [0, 0], False

    quarter = lax.dynamic_slice_in_dim(layer_input, tp * (tok // 4), tok // 4, 0)
    quarter, packed[3] = ordered(quarter, packed[3])
    if depth == 1:
        keys_values[3] = packed[3]
    x_all = lax.all_gather(quarter, ("h",) + TP, axis=0, tiled=True)

    far_grad_other = swap(far_grad_mine, "c")
    grad_act = nt(jnp.concatenate([grad_mine, grad_other]), w_down).astype(BF16)
    far_grad_act = nt(jnp.concatenate([far_grad_mine, far_grad_other]), w_down).astype(BF16)
    keep_rows = (buckets >= tp).astype(F32)
    far_keep = swap(keep_rows, "y")
    keep_rows = jnp.concatenate([half_of(keep_rows, c), half_of(keep_rows, 1 - c)])[:, None]
    far_keep = jnp.concatenate([half_of(far_keep, c), half_of(far_keep, 1 - c)])[:, None]
    grad_act, far_grad_act, group_cos, group_sin, keys_values[-1] = ordered(
        grad_act, far_grad_act, group_cos, group_sin, keys_values[-1]
    )

    *attended, lse = attend(half, scale, tables, packed, keys_values, lane0s, near_is_q)
    pieces = [attended[0]] + [plane_swap(attended[k], k) for k in range(1, HEADS)]
    flat, keep, give = out_project(idx, w_out, pieces)

    def chip_sum(keep, give):
        return (keep.astype(F32) + swap(give, "c").astype(F32)).astype(BF16)

    chip = chip_sum(keep, give)
    x_mid, h_mine = norm(half_of(layer_input, c), chip, swap(chip, "x"), gains[2], gains[3])
    h_other = swap(h_mine, "c")
    far_h_mine = swap(h_mine, "y")
    far_flat = swap(flat, "y")
    act, du, keep, give = feed_forward(h_mine, h_other, w_up, grad_act, keep_rows, True)
    chip = chip_sum(keep, give)
    chip_far = swap(chip, "x")

    far_h_other = swap(far_h_mine, "c")
    far_act, far_du = feed_forward(far_h_mine, far_h_other, w_up, far_grad_act, far_keep, False)
    down_part = scatter(
        product(
            idx,
            [regroup(v) for v in (grad_mine, grad_other, far_grad_mine, far_grad_other)],
            act,
            far_act,
        )
    )
    up_part = scatter(
        product(idx, [regroup(v) for v in (h_mine, h_other, far_h_mine, far_h_other)], du, far_du)
    )

    grad_mid, dy_mine, gain_two_grad, bias_two_grad = norm_back(
        chip, chip_far, x_mid, grad_mine, gains[2]
    )
    dy_other = swap(dy_mine, "c")
    grads = list(out_back(idx, w_out, dy_mine, dy_other))
    grads = [grads[0]] + [plane_swap(grads[k], k) for k in range(1, HEADS)]

    far_dy_mine = swap(dy_mine, "y")
    far_dy_other = swap(far_dy_mine, "c")
    wout_part = scatter(
        product(
            idx_rows,
            [regroup(v) for v in (dy_mine, dy_other, far_dy_mine, far_dy_other)],
            flat,
            far_flat,
        )
    )
    feed = [jnp.dot(act[s], w_down, preferred_element_type=F32).astype(BF16) for s in (slice(half), slice(half, tok))]
    feed_chip = chip_sum(feed[0], feed[1])
    out_mine = (
        x_mid + (feed_chip.astype(F32) + swap(feed_chip, "x").astype(F32))
    ).astype(BF16)
    layer_output = join(idx, out_mine, swap(out_mine, "c"), BF16)

    *dq, near, far = attend_back(
        half,
        scale,
        tables,
        lse,
        group_cos,
        group_sin,
        packed,
        keys_values,
        lane0s,
        near_is_q,
        attended,
        grads,
    )
    got = swap(far, "y")
    dq_pieces = [dq[0]] + [plane_swap(dq[k], k) for k in range(1, HEADS)]
    if depth > 1:
        near = lax.psum_scatter(near, "r", scatter_dimension=0, tiled=True)
        got = lax.psum_scatter(got, "r", scatter_dimension=0, tiled=True)
    dkv = settle(near, got, group_cos, group_sin)
    dkv_pieces = [dkv[:tok]] + [
        plane_swap(dkv[k * tok : (k + 1) * tok], k) for k in range(1, HEADS)
    ]
    keep, give = project_back(idx, w_qkv, dq_pieces, dkv_pieces)
    chip = chip_sum(keep, give)
    chip_far = swap(chip, "x")

    h_all = regroup(norm_all(x_all, gains[0], gains[1]))
    head_give, head_keep = head_product(idx, h_all, dkv, dq)
    head_sum = (head_keep.astype(F32) + swap(head_give, "y").astype(F32)).astype(BF16)
    if depth > 1:
        head_sum = lax.psum_scatter(head_sum, "r", scatter_dimension=2, tiled=True)
    head_pieces = [head_sum[0]] + [plane_swap(head_sum[k], k) for k in range(1, HEADS)]
    qkv_part = head_place(idx, head_pieces)

    _, grad_low, gain_one_grad, bias_one_grad = norm_back(
        chip, chip_far, half_of(layer_input, c), grad_mid, gains[0]
    )
    grad_input = join(idx, grad_low, swap(grad_low, "c"), F32)

    counts = jnp.sum(
        (half_of(buckets, c)[:, None] == jnp.arange(NB, dtype=jnp.int32)[None, :]).astype(F32),
        axis=0,
    )
    sums = jnp.concatenate(
        [v.reshape(dim) for v in (gain_one_grad, bias_one_grad, gain_two_grad, bias_two_grad)]
        + [counts]
    )
    if depth > 1:
        sums = lax.psum(sums, "r")
    sums = sums + swap(sums, "c")
    sums = sums + swap(sums, "y")
    one, two, three = (plane_swap(sums, k) for k in range(1, HEADS))
    sums = (sums + one) + (two + three)
    return (
        layer_output,
        grad_input,
        sums[:dim],
        sums[dim : 2 * dim],
        qkv_part,
        wout_part.astype(F32).T,
        sums[2 * dim : 3 * dim],
        sums[3 * dim : 4 * dim],
        up_part.astype(F32),
        down_part.astype(F32).T,
        sums[4 * dim :].astype(jnp.int32),
    )


def solution(mesh):
    depth = mesh.shape["blk"] // (2 * HEADS)
    fine = Mesh(mesh.devices.reshape(depth, HEADS, 2, 2, 2), BLK + TP)
    return jax.shard_map(
        functools.partial(body, depth),
        mesh=fine,
        in_specs=(
            P(BLK, None),
            P(),
            P(),
            P(None, None, TP),
            P(TP, None),
            P(),
            P(),
            P(None, TP),
            P(TP, None),
            P(BLK),
            P(),
            P(),
            P(BLK, None),
        ),
        out_specs=(
            P(BLK, None),
            P(BLK, None),
            P(),
            P(),
            P(None, BLK, TP),
            P(TP, BLK),
            P(),
            P(),
            P(BLK, TP),
            P(TP, BLK),
            P(),
        ),
        check_vma=False,
    )
```

time: 837 us -> 594 us (0.71)
  blocking collectives: 132 us -> 0 us
  waiting for transfers between devices: 386 us -> 258 us
  Pallas kernels: 39.6 us -> 127 us
  starting transfers between devices: 25.1 us -> 89.4 us
  local copies, waits for them, and re-layouts: 97.9 us -> 35.9 us
  matrix products: 78.8 us -> 30.8 us
  other arithmetic: 55.5 us -> 26.9 us
    pallas_call x2 -> x20, Pallas kernels: 39.6 us -> 127 us  [the longest x2 23.6 us: feed_forward(): pl.pallas_call(feed_kernel, grid=(hidden // tile,), out_shape=[tall, tall...]
    ppermute x22 -> x47, waiting for transfers between devices: 337 us -> 257 us  [the longest x26 191 us: swap(): return lax.ppermute(value, axis, [(0, 1), (1, 0)])]
    ppermute x22 -> x47, starting transfers between devices: 14.9 us -> 89.2 us  [the longest x21 61.7 us: plane_swap(): return lax.ppermute(value, 'h', [(i, i ^ k) for i in range(HEADS)])]
    all_to_all x2 -> x0, blocking collectives: 71 us -> none  [the longest x1 40.2 us: body(): lax.all_to_all(grad_packed.reshape(HEADS, tok, 3 * HD), 'h', 0, 0, tiled=...]
    psum x1 -> x0, blocking collectives: 61.1 us -> none  [body(): lax.psum(jnp.concatenate([gain_one_grad, bias_one_grad, gain_two_grad, bi...]
    all_to_all x2 -> x0, waiting for transfers between devices: 49.6 us -> none  [the longest x1 36.9 us: body(): packed = lax.all_to_all(packed, 'h', 0, 0, tiled=True)]
    dot_general x9 -> x2, matrix products: 56.7 us -> 11.5 us  [body(): jnp.dot(act[s], w_down, preferred_element_type=F32).astype(BF16)]
    concatenate x11 -> x1, local copies, waits for them, and re-layouts: 31.3 us -> 0.01 us  [body(): jnp.concatenate([v.reshape(dim) for v in (gain_one_grad, bias_one_grad, g...]
  transfers between devices with their start and end apart: 28 -> 51, of which waited for: 17 -> 23; matrix products, arithmetic and copies ran while one was open for 17% -> 12% of each run, Pallas kernels for 3% -> 13%
where the time goes in v2:
time: 594 us; the launch traced here: 584 us
  waiting for transfers between devices  258 us (43%)
  Pallas kernels  127 us (21%)
  starting transfers between devices  89.4 us (15%)
  local copies, waits for them, and re-layouts  35.9 us (6%)
  matrix products  30.8 us (5%)
  other arithmetic  26.9 us (5%)
  between operations  16.6 us (3%)
    ppermute x26, waiting for transfers between devices, swap(): return lax.ppermute(value, axis, [(0, 1), (1, 0)])  191 us
    ppermute x21, waiting for transfers between devices, plane_swap(): return lax.ppermute(value, 'h', [(i, i ^ k) for i in range(HEADS)])  66.3 us
    ppermute x21, starting transfers between devices, plane_swap(): return lax.ppermute(value, 'h', [(i, i ^ k) for i in range(HEADS)])  61.7 us
    ppermute x26, starting transfers between devices, swap(): return lax.ppermute(value, axis, [(0, 1), (1, 0)])  27.5 us
    pallas_call x2, Pallas kernels, feed_forward(): pl.pallas_call(feed_kernel, grid=(hidden // tile,), out_shape=[tall, tall...  23.6 us
    unnamed x126, local copies, waits for them, and re-layouts  22.9 us
    dot_general x2, matrix products, nt(): lax.dot_general(lhs, rhs, (((1,), (1,)), ((), ())), preferred_element_typ...  19.3 us
    pallas_call x1, Pallas kernels, attend_back(): pl.pallas_call(functools.partial(attend_back_kernel, tile, scale, lane0s,...  19 us
  transfers between devices with their start and end apart: 51, of which 23 were waited for; matrix products, arithmetic and copies ran while one was open for 12% of the time, Pallas kernels for 13%

profile of v2, /device:TPU:0, one launch (start us, length us, event | category | flops | bytes accessed | tf_op | source)
XLA Modules:
  0.0 584.1 jit_solution(15908294956377421239)
XLA Ops:
  12.0 2.8 copy-done.28
  14.8 9.8 %project.1 = (bf16[512,384]{1,0:T(8,128)(2,1)S(1)}, bf16[512,384]{1,0:T(8,128)(2,1)}, bf16[512,384]{1,0:T(8,128)(2,1)}, bf16[512,384]{1,0:T(8,128)(2,1)}) custom-call(s32[5]{0:T(128)S(1)} %stack.25.idx, bf16[512,2048]{1,0:T(8,128)(2,1)S(1)} %copy-done.15, f32[1,2048]{1,0:T(1,128)S(1)} %bitcast.40, f32[1,2048]{1,0:T(1,128)S(1)} %bitcast.45, ...), custom_call_target="tpu_custom_call" | custom-call | flops 3221225472 | bytes 10485760 | tf_op jit(solution)/shard_map/project/pallas_call | solution.py:107
  24.5 4.0 collective-permute-start.1
  29.9 2.7 constant_dynamic-slice_fusion.1
  43.0 6.4 %fusion.11 = (f32[2048,64]{1,0:T(8,128)}, f32[2048,64]{1,0:T(8,128)}, f32[2048,64]{1,0:T(8,128)}) fusion(f32[64]{0:T(128)} %copy-done.53, f32[2048]{0:T(1024)S(1)} %bitcast.54), kind=kLoop, calls=%fused_computation.30 | loop fusion | flops 262144 | bytes 1581312 | tf_op jit(solution)/shard_map/neg | solution.py:74
  49.3 9.4 %convolution_convert_fusion.1.gact_ref = bf16[512,2048]{1,0:T(8,128)(2,1)} fusion(bf16[2048,2048]{1,0:T(8,128)(2,1)} %param.21, bf16[256,2048]{1,0:T(8,128)(2,1)S(1)} %copy-done.16, bf16[256,2048]{1,0:T(8,128)(2,1)S(1)} %get-tuple-element.142.base_ref.refs_0_), kind=kOutput, calls=%fused_computation.1 | convolution fusion | flops 4300210176 | bytes 12582912 | tf_op jit(solution)/shard_map/dot_general | solution.py:39
  61.1 4.1 pad_maximum_fusion
  70.4 9.9 %convolution_convert_fusion.gact_ref = bf16[512,2048]{1,0:T(8,128)(2,1)} fusion(bf16[2048,2048]{1,0:T(8,128)(2,1)} %param.21, bf16[256,2048]{1,0:T(8,128)(2,1)} %collective-permute-done.5.refs_3_, bf16[256,2048]{1,0:T(8,128)(2,1)} %collective-permute-done.4.refs_2_), kind=kOutput, calls=%fused_computation | convolution fusion | flops 4300210176 | bytes 12582912 | tf_op jit(solution)/shard_map/dot_general | solution.py:39
  82.0 10.8 %collective-permute-done.3.refs_4_ = bf16[1024,256]{1,0:T(8,128)(2,1)S(1)} collective-permute-done((bf16[1024,256]{1,0:T(8,128)(2,1)S(1)}, bf16[1024,256]{1,0:T(8,128)(2,1)S(1)}, u32[]{:S(2)}, u32[]{:S(2)}) %collective-permute-start.3) | collective-permute-done | bytes 524320 | tf_op jit(solution)/shard_map/ppermute | solution.py:27
  92.9 14.5 %attend.1 = (bf16[512,128]{1,0:T(8,128)(2,1)S(1)}, bf16[512,128]{1,0:T(8,128)(2,1)S(1)}, bf16[512,128]{1,0:T(8,128)(2,1)S(1)}, bf16[512,128]{1,0:T(8,128)(2,1)S(1)}, f32[8,1,256]{2,1,0:T(1,128)S(1)}) custom-call(s32[8]{0:T(128)S(1)} %reshape.194.at_ref, s32[8]{0:T(128)S(1)} %and_select_fusion.6.low_ref, s32[16]{0:T(128)S(1)} %fusion.13.row_ref, ...), custom_call_target="tpu_custom_call" | custom-call | flops 1342177280 | bytes 4194304 | tf_op jit(solution)/shard_map/attend/pallas_call | solution.py:253
  114.1 8.0 %collective-permute-done.8.refs_2_ = bf16[512,128]{1,0:T(8,128)(2,1)S(1)} collective-permute-done((bf16[512,128]{1,0:T(8,128)(2,1)S(1)}, bf16[512,128]{1,0:T(8,128)(2,1)S(1)}, u32[]{:S(2)}, u32[]{:S(2)}) %collective-permute-start.8) | collective-permute-done | bytes 131104 | tf_op jit(solution)/shard_map/ppermute | solution.py:31
  128.9 23.6 %collective-permute-done.11.far_ref = bf16[256,2048]{1,0:T(8,128)(2,1)S(1)} collective-permute-done((bf16[256,2048]{1,0:T(8,128)(2,1)S(1)}, bf16[256,2048]{1,0:T(8,128)(2,1)S(1)}, u32[]{:S(2)}, u32[]{:S(2)}) %collective-permute-start.11) | collective-permute-done | bytes 1048608 | tf_op jit(solution)/shard_map/ppermute | solution.py:27
  155.1 2.7 collective-permute-done.12.other_ref.refs_1_
  157.8 14.1 %feed_own.1 = (bf16[512,2048]{1,0:T(8,128)(2,1)}, bf16[512,2048]{1,0:T(8,128)(2,1)}, bf16[256,2048]{1,0:T(8,128)(2,1)S(1)}, bf16[256,2048]{1,0:T(8,128)(2,1)S(1)}) custom-call(bf16[256,2048]{1,0:T(8,128)(2,1)} %get-tuple-element.74.mine_ref.refs_0_, bf16[256,2048]{1,0:T(8,128)(2,1)} %collective-permute-done.12.other_ref.refs_1_, bf16[2048,2048]{1,0:T(8,128)(2,1)} %w_ref.11, ...), custom_call_target="tpu_custom_call" | custom-call | flops 8589934592 | bytes 16777216 | tf_op jit(solution)/shard_map/feed_own/pallas_call | solution.py:484
  176.5 23.7 %collective-permute-done.17.far_ref = bf16[256,2048]{1,0:T(8,128)(2,1)S(1)} collective-permute-done((bf16[256,2048]{1,0:T(8,128)(2,1)S(1)}, bf16[256,2048]{1,0:T(8,128)(2,1)S(1)}, u32[]{:S(2)}, u32[]{:S(2)}) %collective-permute-start.17) | collective-permute-done | bytes 1048608 | tf_op jit(solution)/shard_map/ppermute | solution.py:27
  200.3 2.9 norm_back.2
  204.5 4.1 collective-permute-start.41
  208.6 22.9 %collective-permute-done.41.refs_2_ = bf16[256,2048]{1,0:T(8,128)(2,1)} collective-permute-done((bf16[256,2048]{1,0:T(8,128)(2,1)}, bf16[256,2048]{1,0:T(8,128)(2,1)}, u32[]{:S(2)}, u32[]{:S(2)}) %collective-permute-start.41) | collective-permute-done | bytes 1048608 | tf_op jit(solution)/shard_map/ppermute | solution.py:27
  233.4 12.8 %collective-permute-done.43.refs_5_ = bf16[512,512]{1,0:T(8,128)(2,1)} collective-permute-done((bf16[512,512]{1,0:T(8,128)(2,1)}, bf16[512,512]{1,0:T(8,128)(2,1)}, u32[]{:S(2)}, u32[]{:S(2)}) %collective-permute-start.43) | collective-permute-done | bytes 524320 | tf_op jit(solution)/shard_map/ppermute | solution.py:27
  246.2 4.8 product.3
  254.4 23.4 %collective-permute-done.44.mine_ref.refs_2_ = bf16[256,2048]{1,0:T(8,128)(2,1)} collective-permute-done((bf16[256,2048]{1,0:T(8,128)(2,1)}, bf16[256,2048]{1,0:T(8,128)(2,1)}, u32[]{:S(2)}, u32[]{:S(2)}) %collective-permute-start.44) | collective-permute-done | bytes 1048608 | tf_op jit(solution)/shard_map/ppermute | solution.py:27
  281.6 9.5 %feed_far.1 = (bf16[512,2048]{1,0:T(8,128)(2,1)S(1)}, bf16[512,2048]{1,0:T(8,128)(2,1)}) custom-call(bf16[256,2048]{1,0:T(8,128)(2,1)} %collective-permute-done.44.mine_ref.refs_2_, bf16[256,2048]{1,0:T(8,128)(2,1)} %collective-permute-done.45.other_ref.refs_3_, bf16[2048,2048]{1,0:T(8,128)(2,1)} %w_ref.11, ...), custom_call_target="tpu_custom_call" | custom-call | flops 4294967296 | bytes 16777216 | tf_op jit(solution)/shard_map/feed_far/pallas_call | solution.py:484
  291.2 7.0 %product.5 = bf16[1024,2048]{1,0:T(8,128)(2,1)S(1)} custom-call(s32[5]{0:T(128)S(1)} %stack.25.idx, bf16[256,2048]{1,0:T(8,128)(2,1)S(1)} %copy-done.5, bf16[256,2048]{1,0:T(8,128)(2,1)S(1)} %copy-done.17, bf16[256,2048]{1,0:T(8,128)(2,1)} %collective-permute-done.4.refs_2_, bf16[256,2048]{1,0:T(8,128)(2,1)} %collective-permute-done.5.refs_3_, ...), custom_call_target="tpu_custom_call" | custom-call | flops 4294967296 | bytes 12582912 | tf_op jit(solution)/shard_map/product/pallas_call | solution.py:526
  303.8 7.2 %product.4 = bf16[1024,2048]{1,0:T(8,128)(2,1)S(1)} custom-call(s32[5]{0:T(128)S(1)} %stack.25.idx, bf16[256,2048]{1,0:T(8,128)(2,1)} %get-tuple-element.74.mine_ref.refs_0_, bf16[256,2048]{1,0:T(8,128)(2,1)} %collective-permute-done.12.other_ref.refs_1_, bf16[256,2048]{1,0:T(8,128)(2,1)} %collective-permute-done.44.mine_ref.refs_2_, ...), custom_call_target="tpu_custom_call" | custom-call | flops 4294967296 | bytes 12582912 | tf_op jit(solution)/shard_map/product/pallas_call | solution.py:526
  314.7 3.9 out_back.1
  323.7 9.6 %collective-permute-done.19.refs_11_ = bf16[512,128]{1,0:T(8,128)(2,1)S(1)} collective-permute-done((bf16[512,128]{1,0:T(8,128)(2,1)S(1)}, bf16[512,128]{1,0:T(8,128)(2,1)S(1)}, u32[]{:S(2)}, u32[]{:S(2)}) %collective-permute-start.19) | collective-permute-done | bytes 131104 | tf_op jit(solution)/shard_map/ppermute | solution.py:31
  333.4 7.8 %collective-permute-done.20.refs_12_ = bf16[512,128]{1,0:T(8,128)(2,1)S(1)} collective-permute-done((bf16[512,128]{1,0:T(8,128)(2,1)S(1)}, bf16[512,128]{1,0:T(8,128)(2,1)S(1)}, u32[]{:S(2)}, u32[]{:S(2)}) %collective-permute-start.20) | collective-permute-done | bytes 131104 | tf_op jit(solution)/shard_map/ppermute | solution.py:31
  342.4 19.0 %attend_back.1 = (bf16[512,128]{1,0:T(8,128)(2,1)}, bf16[512,128]{1,0:T(8,128)(2,1)}, bf16[512,128]{1,0:T(8,128)(2,1)}, bf16[512,128]{1,0:T(8,128)(2,1)}, bf16[2...) custom-call(s32[8]{0:T(128)} %copy-done.26, s32[8]{0:T(128)} %copy-done.41, s32[16]{0:T(128)} %copy-done.27, ...), custom_call_target="tpu_custom_call" | custom-call | flops 3355443200 | bytes 8388608 | tf_op jit(solution)/shard_map/attend_back/pallas_call | solution.py:272
  361.5 5.4 collective-permute-start.25
  366.9 5.8 convolution_convert_fusion.2
  372.8 10.7 %collective-permute-start.22 = (bf16[512,128]{1,0:T(8,128)(2,1)S(1)}, bf16[512,128]{1,0:T(8,128)(2,1)S(1)}, u32[]{:S(2)}, u32[]{:S(2)}) collective-permute-start(bf16[512,128]{1,0:T(8,128)(2,1)S(1)} %copy-done.34), channel_id=1, source_target_pairs={{0,8},{8,0},{16,24},{24,16},{1,9},{9,1},{17,25},{25,17},{2,10},{10... | collective-permute-start | bytes 393224 | tf_op jit(solution)/shard_map/ppermute | solution.py:31
  385.8 3.7 collective-permute-done.25.got_ref
  391.1 9.2 %collective-permute-start.26 = (bf16[512,256]{1,0:T(8,128)(2,1)S(1)}, bf16[512,256]{1,0:T(8,128)(2,1)S(1)}, u32[]{:S(2)}, u32[]{:S(2)}) collective-permute-start(bf16[512,256]{1,0:T(8,128)(2,1)S(1)} %get-tuple-element.146), channel_id=1, source_target_pairs={{0,8},{8,0},{16,24},{24,16},{1,9},{9,1},{17,25},{25,17},{2,10},{10... | collective-permute-start | bytes 786440 | tf_op jit(solution)/shard_map/ppermute | solution.py:31
  400.3 3.7 collective-permute-start.27
  407.9 31.6 %collective-permute-done.24.refs_3_ = bf16[512,128]{1,0:T(8,128)(2,1)S(1)} collective-permute-done((bf16[512,128]{1,0:T(8,128)(2,1)S(1)}, bf16[512,128]{1,0:T(8,128)(2,1)S(1)}, u32[]{:S(2)}, u32[]{:S(2)}) %collective-permute-start.24) | collective-permute-done | bytes 131104 | tf_op jit(solution)/shard_map/ppermute | solution.py:31
  439.5 5.2 project_back.1
  444.8 5.7 fusion.2
  453.1 23.5 %collective-permute-done.14 = bf16[256,2048]{1,0:T(8,128)(2,1)S(1)} collective-permute-done((bf16[256,2048]{1,0:T(8,128)(2,1)S(1)}, bf16[256,2048]{1,0:T(8,128)(2,1)S(1)}, u32[]{:S(2)}, u32[]{:S(2)}) %collective-permute-start.14) | collective-permute-done | bytes 1048608 | tf_op jit(solution)/shard_map/ppermute | solution.py:27
  477.3 21.3 %collective-permute-done.30.far_ref = bf16[256,2048]{1,0:T(8,128)(2,1)S(1)} collective-permute-done((bf16[256,2048]{1,0:T(8,128)(2,1)S(1)}, bf16[256,2048]{1,0:T(8,128)(2,1)S(1)}, u32[]{:S(2)}, u32[]{:S(2)}) %collective-permute-start.30) | collective-permute-done | bytes 1048608 | tf_op jit(solution)/shard_map/ppermute | solution.py:27
  498.7 3.1 norm_back.3
  507.9 10.7 %collective-permute-start.34 = (f32[8196]{0:T(1024)S(1)}, f32[8196]{0:T(1024)S(1)}, u32[]{:S(2)}, u32[]{:S(2)}) collective-permute-start(f32[8196]{0:T(1024)S(1)} %add.175), channel_id=1, source_target_pairs={{0,8},{8,0},{16,24},{24,16},{1,9},{9,1},{17,25},{25,17},{2,10},{10... | collective-permute-start | bytes 98360 | tf_op jit(solution)/shard_map/ppermute | solution.py:31
  521.0 3.4 copy-done
  524.4 6.6 %norm_all.1.h_ref = bf16[2048,2048]{1,0:T(8,128)(2,1)S(1)} custom-call(bf16[2048,2048]{1,0:T(8,128)(2,1)S(1)} %copy-done, f32[1,2048]{1,0:T(1,128)S(1)} %bitcast.42, f32[1,2048]{1,0:T(1,128)S(1)} %bitcast.46), custom_call_target="tpu_custom_call" | custom-call | flops 67108864 | bytes 16777216 | tf_op jit(solution)/shard_map/norm_all/pallas_call | solution.py:395
  531.1 7.2 %head_product.1 = (bf16[4,384,256]{2,1,0:T(8,128)(2,1)S(1)}, bf16[4,384,256]{2,1,0:T(8,128)(2,1)S(1)}) custom-call(s32[5]{0:T(128)S(1)} %stack.25.idx, bf16[2048,2048]{1,0:T(8,128)(2,1)S(1)} %norm_all.1.h_ref, bf16[2048,256]{1,0:T(8,128)(2,1)S(1)} %copy-done.8, bf16[512,128]{1,0:T(8,128)(2,1)S(1)} %copy-done.48, bf16[512,128]{1,0:T(8,128)(2,1)S(1)} %copy-done.35, ...), custom_call_target="tpu_custom_call" | custom-call | flops 3221225472 | bytes 12582912 | tf_op jit(solution)/shard_map/head_product/pallas_call | solution.py:577
  541.0 2.8 join.3
  543.8 13.5 %collective-permute-done.37 = bf16[4,384,256]{2,1,0:T(8,128)(2,1)S(1)} collective-permute-done((bf16[4,384,256]{2,1,0:T(8,128)(2,1)S(1)}, bf16[4,384,256]{2,1,0:T(8,128)(2,1)S(1)}, u32[]{:S(2)}, u32[]{:S(2)}) %collective-permute-start.37) | collective-permute-done | bytes 786464 | tf_op jit(solution)/shard_map/ppermute | solution.py:27
  565.3 2.8 convert_element_type.124
  568.1 6.4 %collective-permute-done.39.refs_2_ = bf16[384,256]{1,0:T(8,128)(2,1)S(1)} collective-permute-done((bf16[384,256]{1,0:T(8,128)(2,1)S(1)}, bf16[384,256]{1,0:T(8,128)(2,1)S(1)}, u32[]{:S(2)}, u32[]{:S(2)}) %collective-permute-start.39) | collective-permute-done | bytes 196640 | tf_op jit(solution)/shard_map/ppermute | solution.py:31
  (273 shorter events, 103.7 us)
Async XLA Ops:
  8.0 497.4 %reduce-scatter.4.cloned.1.call-start = ((), (), s32[]{:S(2)}) async-start(), calls=%async_computation.4 | async-start | bytes 1310720 | tf_op jit(solution)/shard_map/reduce_scatter | solution.py:740
  24.5 40.7 %collective-permute-start.1 = (bf16[512,384]{1,0:T(8,128)(2,1)}, bf16[512,384]{1,0:T(8,128)(2,1)}, u32[]{:S(2)}, u32[]{:S(2)}) collective-permute-start(bf16[512,384]{1,0:T(8,128)(2,1)} %get-tuple-element.63), channel_id=1, source_target_pairs={{0,16},{8,24},{16,0},{24,8},{1,17},{9,25},{17,1},{25,9},{2,18},{10... | collective-permute-start | bytes 1179656 | tf_op jit(solution)/shard_map/ppermute | solution.py:31
  28.6 37.6 %collective-permute-start.2 = (bf16[512,384]{1,0:T(8,128)(2,1)}, bf16[512,384]{1,0:T(8,128)(2,1)}, u32[]{:S(2)}, u32[]{:S(2)}) collective-permute-start(bf16[512,384]{1,0:T(8,128)(2,1)} %get-tuple-element.64), channel_id=1, source_target_pairs={{0,24},{8,16},{16,8},{24,0},{1,25},{9,17},{17,9},{25,1},{2,26},{10... | collective-permute-start | bytes 1179656 | tf_op jit(solution)/shard_map/ppermute | solution.py:31
  32.7 26.1 %collective-permute-start.4 = (bf16[256,2048]{1,0:T(8,128)(2,1)S(1)}, bf16[256,2048]{1,0:T(8,128)(2,1)}, u32[]{:S(2)}, u32[]{:S(2)}) collective-permute-start(bf16[256,2048]{1,0:T(8,128)(2,1)S(1)} %get-tuple-element.142.base_ref.refs_0_), channel_id=1, source_target_pairs={{0,4},{4,0},{1,5},{5,1},{2,6},{6,2},{3,7},{7,3},{8,12},{12,8},{9,1... | collective-permute-start | bytes 3145736 | tf_op jit(solution)/shard_map/ppermute | solution.py:27
  34.2 33.6 %collective-permute-start = (bf16[512,384]{1,0:T(8,128)(2,1)}, bf16[512,384]{1,0:T(8,128)(2,1)}, u32[]{:S(2)}, u32[]{:S(2)}) collective-permute-start(bf16[512,384]{1,0:T(8,128)(2,1)} %get-tuple-element.62), channel_id=1, source_target_pairs={{0,8},{8,0},{16,24},{24,16},{1,9},{9,1},{17,25},{25,17},{2,10},{10... | collective-permute-start | bytes 1179656 | tf_op jit(solution)/shard_map/ppermute | solution.py:31
  58.8 11.7 %collective-permute-start.5 = (bf16[256,2048]{1,0:T(8,128)(2,1)}, bf16[256,2048]{1,0:T(8,128)(2,1)}, u32[]{:S(2)}, u32[]{:S(2)}) collective-permute-start(bf16[256,2048]{1,0:T(8,128)(2,1)} %collective-permute-done.4.refs_2_), channel_id=1, source_target_pairs={{0,1},{1,0},{2,3},{3,2},{4,5},{5,4},{6,7},{7,6},{8,9},{9,8},{10,11... | collective-permute-start | bytes 3145736 | tf_op jit(solution)/shard_map/ppermute | solution.py:27
  67.2 14.8 %collective-permute-start.6 = (bf16[1024,256]{1,0:T(8,128)(2,1)S(1)}, bf16[1024,256]{1,0:T(8,128)(2,1)S(1)}, u32[]{:S(2)}, u32[]{:S(2)}) collective-permute-start(bf16[1024,256]{1,0:T(8,128)(2,1)S(1)} %pad_maximum_fusion.3), channel_id=1, source_target_pairs={{0,4},{4,0},{1,5},{5,1},{2,6},{6,2},{3,7},{7,3},{8,12},{12,8},{9,1... | collective-permute-start | bytes 1572872 | tf_op jit(solution)/shard_map/ppermute | solution.py:27
  68.8 24.0 %collective-permute-start.3 = (bf16[1024,256]{1,0:T(8,128)(2,1)S(1)}, bf16[1024,256]{1,0:T(8,128)(2,1)S(1)}, u32[]{:S(2)}, u32[]{:S(2)}) collective-permute-start(bf16[1024,256]{1,0:T(8,128)(2,1)S(1)} %pad_maximum_fusion.2), channel_id=1, source_target_pairs={{0,4},{4,0},{1,5},{5,1},{2,6},{6,2},{3,7},{7,3},{8,12},{12,8},{9,1... | collective-permute-start | bytes 1572872 | tf_op jit(solution)/shard_map/ppermute | solution.py:27
  107.4 6.7 %collective-permute-start.7 = (bf16[512,128]{1,0:T(8,128)(2,1)S(1)}, bf16[512,128]{1,0:T(8,128)(2,1)S(1)}, u32[]{:S(2)}, u32[]{:S(2)}) collective-permute-start(bf16[512,128]{1,0:T(8,128)(2,1)S(1)} %get-tuple-element.68.refs_7_), channel_id=1, source_target_pairs={{0,8},{8,0},{16,24},{24,16},{1,9},{9,1},{17,25},{25,17},{2,10},{10... | collective-permute-start | bytes 393224 | tf_op jit(solution)/shard_map/ppermute | solution.py:31
  109.3 12.8 %collective-permute-start.8 = (bf16[512,128]{1,0:T(8,128)(2,1)S(1)}, bf16[512,128]{1,0:T(8,128)(2,1)S(1)}, u32[]{:S(2)}, u32[]{:S(2)}) collective-permute-start(bf16[512,128]{1,0:T(8,128)(2,1)S(1)} %get-tuple-element.69.refs_8_), channel_id=1, source_target_pairs={{0,16},{8,24},{16,0},{24,8},{1,17},{9,25},{17,1},{25,9},{2,18},{10... | collective-permute-start | bytes 393224 | tf_op jit(solution)/shard_map/ppermute | solution.py:31
  111.0 11.1 %collective-permute-start.9 = (bf16[512,128]{1,0:T(8,128)(2,1)S(1)}, bf16[512,128]{1,0:T(8,128)(2,1)S(1)}, u32[]{:S(2)}, u32[]{:S(2)}) collective-permute-start(bf16[512,128]{1,0:T(8,128)(2,1)S(1)} %get-tuple-element.70.refs_9_), channel_id=1, source_target_pairs={{0,24},{8,16},{16,8},{24,0},{1,25},{9,17},{17,9},{25,1},{2,26},{10... | collective-permute-start | bytes 393224 | tf_op jit(solution)/shard_map/ppermute | solution.py:31
  127.2 25.3 %collective-permute-start.11 = (bf16[256,2048]{1,0:T(8,128)(2,1)S(1)}, bf16[256,2048]{1,0:T(8,128)(2,1)S(1)}, u32[]{:S(2)}, u32[]{:S(2)}) collective-permute-start(bf16[256,2048]{1,0:T(8,128)(2,1)S(1)} %add_convert_fusion.3.chip_ref), channel_id=1, source_target_pairs={{0,2},{2,0},{1,3},{3,1},{4,6},{6,4},{5,7},{7,5},{8,10},{10,8},{9,1... | collective-permute-start | bytes 3145736 | tf_op jit(solution)/shard_map/ppermute | solution.py:27
  154.8 3.0 collective-permute-start.12
  175.0 25.3 %collective-permute-start.17 = (bf16[256,2048]{1,0:T(8,128)(2,1)S(1)}, bf16[256,2048]{1,0:T(8,128)(2,1)S(1)}, u32[]{:S(2)}, u32[]{:S(2)}) collective-permute-start(bf16[256,2048]{1,0:T(8,128)(2,1)S(1)} %add_convert_fusion.1.chip_ref), channel_id=1, source_target_pairs={{0,2},{2,0},{1,3},{3,1},{4,6},{6,4},{5,7},{7,5},{8,10},{10,8},{9,1... | collective-permute-start | bytes 3145736 | tf_op jit(solution)/shard_map/ppermute | solution.py:27
  204.5 27.0 %collective-permute-start.41 = (bf16[256,2048]{1,0:T(8,128)(2,1)}, bf16[256,2048]{1,0:T(8,128)(2,1)}, u32[]{:S(2)}, u32[]{:S(2)}) collective-permute-start(bf16[256,2048]{1,0:T(8,128)(2,1)} %get-tuple-element.82.mine_ref.refs_0_), channel_id=1, source_target_pairs={{0,4},{4,0},{1,5},{5,1},{2,6},{6,2},{3,7},{7,3},{8,12},{12,8},{9,1... | collective-permute-start | bytes 3145736 | tf_op jit(solution)/shard_map/ppermute | solution.py:27
  208.6 37.6 %collective-permute-start.18 = (bf16[256,2048]{1,0:T(8,128)(2,1)}, bf16[256,2048]{1,0:T(8,128)(2,1)}, u32[]{:S(2)}, u32[]{:S(2)}) collective-permute-start(bf16[256,2048]{1,0:T(8,128)(2,1)} %get-tuple-element.82.mine_ref.refs_0_), channel_id=1, source_target_pairs={{0,1},{1,0},{2,3},{3,2},{4,5},{5,4},{6,7},{7,6},{8,9},{9,8},{10,11... | collective-permute-start | bytes 3145736 | tf_op jit(solution)/shard_map/ppermute | solution.py:27
  231.5 14.7 %collective-permute-start.42 = (bf16[256,2048]{1,0:T(8,128)(2,1)}, bf16[256,2048]{1,0:T(8,128)(2,1)}, u32[]{:S(2)}, u32[]{:S(2)}) collective-permute-start(bf16[256,2048]{1,0:T(8,128)(2,1)} %collective-permute-done.41.refs_2_), channel_id=1, source_target_pairs={{0,1},{1,0},{2,3},{3,2},{4,5},{5,4},{6,7},{7,6},{8,9},{9,8},{10,11... | collective-permute-start | bytes 3145736 | tf_op jit(solution)/shard_map/ppermute | solution.py:27
  231.6 14.7 %collective-permute-start.43 = (bf16[512,512]{1,0:T(8,128)(2,1)}, bf16[512,512]{1,0:T(8,128)(2,1)}, u32[]{:S(2)}, u32[]{:S(2)}) collective-permute-start(bf16[512,512]{1,0:T(8,128)(2,1)} %get-tuple-element.104.refs_4_), channel_id=1, source_target_pairs={{0,4},{4,0},{1,5},{5,1},{2,6},{6,2},{3,7},{7,3},{8,12},{12,8},{9,1... | collective-permute-start | bytes 1572872 | tf_op jit(solution)/shard_map/ppermute | solution.py:27
  252.0 269.0 %all-gather.2.cloned.1.call-start = ((), (), s32[]{:S(2)}) async-start(), calls=%async_computation.3 | async-start | bytes 8912896 | tf_op jit(solution)/shard_map/all_gather | solution.py:798
  252.5 309.5 %reduce-scatter.8.cloned.1.call-start = ((), (), s32[]{:S(2)}) async-start(), calls=%async_computation.6 | async-start | bytes 5242880 | tf_op jit(solution)/shard_map/reduce_scatter | solution.py:740
  252.6 25.2 %collective-permute-start.44 = (bf16[256,2048]{1,0:T(8,128)(2,1)}, bf16[256,2048]{1,0:T(8,128)(2,1)}, u32[]{:S(2)}, u32[]{:S(2)}) collective-permute-start(bf16[256,2048]{1,0:T(8,128)(2,1)} %get-tuple-element.74.mine_ref.refs_0_), channel_id=1, source_target_pairs={{0,4},{4,0},{1,5},{5,1},{2,6},{6,2},{3,7},{7,3},{8,12},{12,8},{9,1... | collective-permute-start | bytes 3145736 | tf_op jit(solution)/shard_map/ppermute | solution.py:27
  277.8 3.9 collective-permute-start.45
  277.8 3.6 collective-permute-start.46
  300.2 265.1 %reduce-scatter.6.cloned.1.call-start = ((), (), s32[]{:S(2)}) async-start(), calls=%async_computation.5 | async-start | bytes 5242880 | tf_op jit(solution)/shard_map/reduce_scatter | solution.py:740
  319.3 14.1 %collective-permute-start.19 = (bf16[512,128]{1,0:T(8,128)(2,1)S(1)}, bf16[512,128]{1,0:T(8,128)(2,1)S(1)}, u32[]{:S(2)}, u32[]{:S(2)}) collective-permute-start(bf16[512,128]{1,0:T(8,128)(2,1)S(1)} %get-tuple-element.84), channel_id=1, source_target_pairs={{0,8},{8,0},{16,24},{24,16},{1,9},{9,1},{17,25},{25,17},{2,10},{10... | collective-permute-start | bytes 393224 | tf_op jit(solution)/shard_map/ppermute | solution.py:31
  321.3 19.9 %collective-permute-start.20 = (bf16[512,128]{1,0:T(8,128)(2,1)S(1)}, bf16[512,128]{1,0:T(8,128)(2,1)S(1)}, u32[]{:S(2)}, u32[]{:S(2)}) collective-permute-start(bf16[512,128]{1,0:T(8,128)(2,1)S(1)} %get-tuple-element.85), channel_id=1, source_target_pairs={{0,16},{8,24},{16,0},{24,8},{1,17},{9,25},{17,1},{25,9},{2,18},{10... | collective-permute-start | bytes 393224 | tf_op jit(solution)/shard_map/ppermute | solution.py:31
  322.3 19.5 %collective-permute-start.21 = (bf16[512,128]{1,0:T(8,128)(2,1)S(1)}, bf16[512,128]{1,0:T(8,128)(2,1)S(1)}, u32[]{:S(2)}, u32[]{:S(2)}) collective-permute-start(bf16[512,128]{1,0:T(8,128)(2,1)S(1)} %get-tuple-element.86), channel_id=1, source_target_pairs={{0,24},{8,16},{16,8},{24,0},{1,25},{9,17},{17,9},{25,1},{2,26},{10... | collective-permute-start | bytes 393224 | tf_op jit(solution)/shard_map/ppermute | solution.py:31
  361.5 28.0 %collective-permute-start.25 = (bf16[2048,256]{1,0:T(8,128)(2,1)}, bf16[2048,256]{1,0:T(8,128)(2,1)S(1)}, u32[]{:S(2)}, u32[]{:S(2)}) collective-permute-start(bf16[2048,256]{1,0:T(8,128)(2,1)} %get-tuple-element.92), channel_id=1, source_target_pairs={{0,4},{4,0},{1,5},{5,1},{2,6},{6,2},{3,7},{7,3},{8,12},{12,8},{9,1... | collective-permute-start | bytes 3145736 | tf_op jit(solution)/shard_map/ppermute | solution.py:27
  372.7 72.2 %collective-permute-start.13 = (bf16[256,2048]{1,0:T(8,128)(2,1)S(1)}, bf16[256,2048]{1,0:T(8,128)(2,1)S(1)}, u32[]{:S(2)}, u32[]{:S(2)}) collective-permute-start(bf16[256,2048]{1,0:T(8,128)(2,1)S(1)} %convolution_convert_fusion.2), channel_id=1, source_target_pairs={{0,1},{1,0},{2,3},{3,2},{4,5},{5,4},{6,7},{7,6},{8,9},{9,8},{10,11... | collective-permute-start | bytes 3145736 | tf_op jit(solution)/shard_map/ppermute | solution.py:27
  372.8 31.3 %collective-permute-start.22 = (bf16[512,128]{1,0:T(8,128)(2,1)S(1)}, bf16[512,128]{1,0:T(8,128)(2,1)S(1)}, u32[]{:S(2)}, u32[]{:S(2)}) collective-permute-start(bf16[512,128]{1,0:T(8,128)(2,1)S(1)} %copy-done.34), channel_id=1, source_target_pairs={{0,8},{8,0},{16,24},{24,16},{1,9},{9,1},{17,25},{25,17},{2,10},{10... | collective-permute-start | bytes 393224 | tf_op jit(solution)/shard_map/ppermute | solution.py:31
  383.5 22.0 %collective-permute-start.23 = (bf16[512,128]{1,0:T(8,128)(2,1)S(1)}, bf16[512,128]{1,0:T(8,128)(2,1)S(1)}, u32[]{:S(2)}, u32[]{:S(2)}) collective-permute-start(bf16[512,128]{1,0:T(8,128)(2,1)S(1)} %copy-done.36), channel_id=1, source_target_pairs={{0,16},{8,24},{16,0},{24,8},{1,17},{9,25},{17,1},{25,9},{2,18},{10... | collective-permute-start | bytes 393224 | tf_op jit(solution)/shard_map/ppermute | solution.py:31
  391.1 48.3 %collective-permute-start.26 = (bf16[512,256]{1,0:T(8,128)(2,1)S(1)}, bf16[512,256]{1,0:T(8,128)(2,1)S(1)}, u32[]{:S(2)}, u32[]{:S(2)}) collective-permute-start(bf16[512,256]{1,0:T(8,128)(2,1)S(1)} %get-tuple-element.146), channel_id=1, source_target_pairs={{0,8},{8,0},{16,24},{24,16},{1,9},{9,1},{17,25},{25,17},{2,10},{10... | collective-permute-start | bytes 786440 | tf_op jit(solution)/shard_map/ppermute | solution.py:31
  400.3 39.2 %collective-permute-start.27 = (bf16[512,256]{1,0:T(8,128)(2,1)S(1)}, bf16[512,256]{1,0:T(8,128)(2,1)S(1)}, u32[]{:S(2)}, u32[]{:S(2)}) collective-permute-start(bf16[512,256]{1,0:T(8,128)(2,1)S(1)} %get-tuple-element.145), channel_id=1, source_target_pairs={{0,16},{8,24},{16,0},{24,8},{1,17},{9,25},{17,1},{25,9},{2,18},{10... | collective-permute-start | bytes 786440 | tf_op jit(solution)/shard_map/ppermute | solution.py:31
  404.0 35.5 %collective-permute-start.28 = (bf16[512,256]{1,0:T(8,128)(2,1)S(1)}, bf16[512,256]{1,0:T(8,128)(2,1)S(1)}, u32[]{:S(2)}, u32[]{:S(2)}) collective-permute-start(bf16[512,256]{1,0:T(8,128)(2,1)S(1)} %get-tuple-element.144), channel_id=1, source_target_pairs={{0,24},{8,16},{16,8},{24,0},{1,25},{9,17},{17,9},{25,1},{2,26},{10... | collective-permute-start | bytes 786440 | tf_op jit(solution)/shard_map/ppermute | solution.py:31
  405.5 34.0 %collective-permute-start.24 = (bf16[512,128]{1,0:T(8,128)(2,1)S(1)}, bf16[512,128]{1,0:T(8,128)(2,1)S(1)}, u32[]{:S(2)}, u32[]{:S(2)}) collective-permute-start(bf16[512,128]{1,0:T(8,128)(2,1)S(1)} %copy-done.38), channel_id=1, source_target_pairs={{0,24},{8,16},{16,8},{24,0},{1,25},{9,17},{17,9},{25,1},{2,26},{10... | collective-permute-start | bytes 393224 | tf_op jit(solution)/shard_map/ppermute | solution.py:31
  444.8 7.4 %collective-permute-start.29 = (bf16[256,2048]{1,0:T(8,128)(2,1)S(1)}, bf16[256,2048]{1,0:T(8,128)(2,1)S(1)}, u32[]{:S(2)}, u32[]{:S(2)}) collective-permute-start(bf16[256,2048]{1,0:T(8,128)(2,1)S(1)} %get-tuple-element.94), channel_id=1, source_target_pairs={{0,1},{1,0},{2,3},{3,2},{4,5},{5,4},{6,7},{7,6},{8,9},{9,8},{10,11... | collective-permute-start | bytes 3145736 | tf_op jit(solution)/shard_map/ppermute | solution.py:27
  450.6 26.0 %collective-permute-start.14 = (bf16[256,2048]{1,0:T(8,128)(2,1)S(1)}, bf16[256,2048]{1,0:T(8,128)(2,1)S(1)}, u32[]{:S(2)}, u32[]{:S(2)}) collective-permute-start(bf16[256,2048]{1,0:T(8,128)(2,1)S(1)} %fusion.2), channel_id=1, source_target_pairs={{0,2},{2,0},{1,3},{3,1},{4,6},{6,4},{5,7},{7,5},{8,10},{10,8},{9,1... | collective-permute-start | bytes 3145736 | tf_op jit(solution)/shard_map/ppermute | solution.py:27
  452.5 46.1 %collective-permute-start.30 = (bf16[256,2048]{1,0:T(8,128)(2,1)S(1)}, bf16[256,2048]{1,0:T(8,128)(2,1)S(1)}, u32[]{:S(2)}, u32[]{:S(2)}) collective-permute-start(bf16[256,2048]{1,0:T(8,128)(2,1)S(1)} %add_convert_fusion.chip_ref), channel_id=1, source_target_pairs={{0,2},{2,0},{1,3},{3,1},{4,6},{6,4},{5,7},{7,5},{8,10},{10,8},{9,1... | collective-permute-start | bytes 3145736 | tf_op jit(solution)/shard_map/ppermute | solution.py:27
  477.1 24.8 %collective-permute-start.15 = (bf16[256,2048]{1,0:T(8,128)(2,1)S(1)}, bf16[256,2048]{1,0:T(8,128)(2,1)S(1)}, u32[]{:S(2)}, u32[]{:S(2)}) collective-permute-start(bf16[256,2048]{1,0:T(8,128)(2,1)S(1)} %add_convert_fusion.2.mine_ref), channel_id=1, source_target_pairs={{0,1},{1,0},{2,3},{3,2},{4,5},{5,4},{6,7},{7,6},{8,9},{9,8},{10,11... | collective-permute-start | bytes 3145736 | tf_op jit(solution)/shard_map/ppermute | solution.py:27
  503.9 4.0 collective-permute-start.33
  507.4 33.5 %collective-permute-start.31 = (bf16[256,2048]{1,0:T(8,128)(2,1)S(1)}, bf16[256,2048]{1,0:T(8,128)(2,1)S(1)}, u32[]{:S(2)}, u32[]{:S(2)}) collective-permute-start(bf16[256,2048]{1,0:T(8,128)(2,1)S(1)} %get-tuple-element.96.mine_ref), channel_id=1, source_target_pairs={{0,1},{1,0},{2,3},{3,2},{4,5},{5,4},{6,7},{7,6},{8,9},{9,8},{10,11... | collective-permute-start | bytes 3145736 | tf_op jit(solution)/shard_map/ppermute | solution.py:27
  507.9 31.9 %collective-permute-start.34 = (f32[8196]{0:T(1024)S(1)}, f32[8196]{0:T(1024)S(1)}, u32[]{:S(2)}, u32[]{:S(2)}) collective-permute-start(f32[8196]{0:T(1024)S(1)} %add.175), channel_id=1, source_target_pairs={{0,8},{8,0},{16,24},{24,16},{1,9},{9,1},{17,25},{25,17},{2,10},{10... | collective-permute-start | bytes 98360 | tf_op jit(solution)/shard_map/ppermute | solution.py:31
  518.6 21.2 %collective-permute-start.35 = (f32[8196]{0:T(1024)S(1)}, f32[8196]{0:T(1024)S(1)}, u32[]{:S(2)}, u32[]{:S(2)}) collective-permute-start(f32[8196]{0:T(1024)S(1)} %add.175), channel_id=1, source_target_pairs={{0,16},{8,24},{16,0},{24,8},{1,17},{9,25},{17,1},{25,9},{2,18},{10... | collective-permute-start | bytes 98360 | tf_op jit(solution)/shard_map/ppermute | solution.py:31
  519.1 20.7 %collective-permute-start.36 = (f32[8196]{0:T(1024)S(1)}, f32[8196]{0:T(1024)S(1)}, u32[]{:S(2)}, u32[]{:S(2)}) collective-permute-start(f32[8196]{0:T(1024)S(1)} %add.175), channel_id=1, source_target_pairs={{0,24},{8,16},{16,8},{24,0},{1,25},{9,17},{17,9},{25,1},{2,26},{10... | collective-permute-start | bytes 98360 | tf_op jit(solution)/shard_map/ppermute | solution.py:31
  538.2 19.1 %collective-permute-start.37 = (bf16[4,384,256]{2,1,0:T(8,128)(2,1)S(1)}, bf16[4,384,256]{2,1,0:T(8,128)(2,1)S(1)}, u32[]{:S(2)}, u32[]{:S(2)}) collective-permute-start(bf16[4,384,256]{2,1,0:T(8,128)(2,1)S(1)} %get-tuple-element.103), channel_id=1, source_target_pairs={{0,4},{4,0},{1,5},{5,1},{2,6},{6,2},{3,7},{7,3},{8,12},{12,8},{9,1... | collective-permute-start | bytes 2359304 | tf_op jit(solution)/shard_map/ppermute | solution.py:27
  557.6 10.5 %collective-permute-start.38 = (bf16[384,256]{1,0:T(8,128)(2,1)S(1)}, bf16[384,256]{1,0:T(8,128)(2,1)S(1)}, u32[]{:S(2)}, u32[]{:S(2)}) collective-permute-start(bf16[384,256]{1,0:T(8,128)(2,1)S(1)} %get-tuple-element.150), channel_id=1, source_target_pairs={{0,8},{8,0},{16,24},{24,16},{1,9},{9,1},{17,25},{25,17},{2,10},{10... | collective-permute-start | bytes 589832 | tf_op jit(solution)/shard_map/ppermute | solution.py:31
  558.4 16.1 %collective-permute-start.39 = (bf16[384,256]{1,0:T(8,128)(2,1)S(1)}, bf16[384,256]{1,0:T(8,128)(2,1)S(1)}, u32[]{:S(2)}, u32[]{:S(2)}) collective-permute-start(bf16[384,256]{1,0:T(8,128)(2,1)S(1)} %get-tuple-element.149), channel_id=1, source_target_pairs={{0,16},{8,24},{16,0},{24,8},{1,17},{9,25},{17,1},{25,9},{2,18},{10... | collective-permute-start | bytes 589832 | tf_op jit(solution)/shard_map/ppermute | solution.py:31
  560.1 14.4 %collective-permute-start.40 = (bf16[384,256]{1,0:T(8,128)(2,1)S(1)}, bf16[384,256]{1,0:T(8,128)(2,1)S(1)}, u32[]{:S(2)}, u32[]{:S(2)}) collective-permute-start(bf16[384,256]{1,0:T(8,128)(2,1)S(1)} %get-tuple-element.148), channel_id=1, source_target_pairs={{0,24},{8,16},{16,8},{24,0},{1,25},{9,17},{17,9},{25,1},{2,26},{10... | collective-permute-start | bytes 589832 | tf_op jit(solution)/shard_map/ppermute | solution.py:31
  (62 other events, 1118.9 us)
Sparse Core Ops, SparseCore 0:
  252.1 39.2 reduce-scatter.3
  300.3 134.5 reduce-scatter.7
  437.2 88.0 reduce-scatter.5
Sparse Core Ops, SparseCore 1:
  254.6 149.3 all-gather.1

commit v3 on v2

--- a/solution.py
+++ b/solution.py
@@ -80,7 +80,7 @@
 
 
 def project_kernel(idx, x_ref, gain_ref, bias_ref, cos_ref, sin_ref, w_ref, *refs):
-    outs, h_ref = refs[:HEADS], refs[HEADS]
+    q_outs, kv_outs, h_ref = refs[:HEADS], refs[HEADS : 2 * HEADS], refs[2 * HEADS]
     step = pl.program_id(0)
 
     @pl.when(step == 0)
@@ -93,13 +93,13 @@
     queries = rotate(both[:, :HD], cosine, sine).astype(BF16)
     keys = rotate(both[:, HD:], cosine, sine).astype(BF16)
     values = nn(h_ref[...], w_ref[2]).astype(BF16)
-    for k, out in enumerate(outs):
+    for k in range(HEADS):
 
         @pl.when(step == k)
-        def _(out=out):
-            out[:, :HD] = queries
-            out[:, HD : 2 * HD] = keys
-            out[:, 2 * HD :] = values
+        def _(k=k):
+            q_outs[k][...] = queries
+            kv_outs[k][:, :HD] = keys
+            kv_outs[k][:, HD:] = values
 
 
 def project(idx, x, gain, bias, cosine, sine, w_qkv):
@@ -117,10 +117,11 @@
                 whole((tok, HD)),
                 pl.BlockSpec((3, dim, HD), lambda k, idx: (0, 0, idx[0] ^ k)),
             ],
-            out_specs=[whole((tok, 3 * HD))] * HEADS,
+            out_specs=[whole((tok, HD))] * HEADS + [whole((tok, 2 * HD))] * HEADS,
             scratch_shapes=[pltpu.VMEM((tok, dim), BF16)],
         ),
-        out_shape=[jax.ShapeDtypeStruct((tok, 3 * HD), BF16)] * HEADS,
+        out_shape=[jax.ShapeDtypeStruct((tok, HD), BF16)] * HEADS
+        + [jax.ShapeDtypeStruct((tok, 2 * HD), BF16)] * HEADS,
         compiler_params=params(40),
         cost_estimate=cost(2 * tok * dim * 12 * HD, 10 * 2**20),
         name="project",
@@ -132,25 +133,18 @@
     return (key_places <= query_places) & (key_places >= query_firsts)
 
 
-def gather_refs(q_refs, kv_refs, lane0s, q_all, kv_all):
+def gather_refs(refs, whole_ref):
     at = 0
-    for ref in q_refs:
-        q_all[at : at + ref.shape[0], :] = ref[:, :HD]
+    for ref in refs:
+        whole_ref[at : at + ref.shape[0], :] = ref[...]
         at += ref.shape[0]
-    at = 0
-    for ref, lane0 in zip(kv_refs, lane0s, strict=True):
-        kv_all[at : at + ref.shape[0], :] = ref[:, lane0 : lane0 + 2 * HD]
-        at += ref.shape[0]
-
-
-def attend_kernel(tile, scale, lane0s, near_is_q, at_ref, low_ref, row_ref, first_ref, *refs):
-    n_kv = len(lane0s)
-    q_refs = refs[:HEADS]
-    kv_refs = refs[:n_kv] if near_is_q else refs[HEADS : HEADS + n_kv]
-    n_in = n_kv if near_is_q else HEADS + n_kv
-    outs = refs[n_in : n_in + HEADS]
-    lse_ref, q_all, kv_all = refs[n_in + HEADS :]
-    gather_refs(q_refs, kv_refs, lane0s, q_all, kv_all)
+
+
+def attend_kernel(tile, scale, n_kv, at_ref, low_ref, row_ref, first_ref, *refs):
+    q_refs, kv_refs, refs = refs[:HEADS], refs[HEADS : HEADS + n_kv], refs[HEADS + n_kv :]
+    outs, (lse_ref, q_all, kv_all) = refs[:HEADS], refs[HEADS:]
+    gather_refs(q_refs, q_all)
+    gather_refs(kv_refs, kv_all)
     lanes = lax.broadcasted_iota(jnp.int32, (1, tile), 1)
     per_out = outs[0].shape[0] // tile
 
@@ -193,15 +187,13 @@
 
 
 def attend_back_kernel(
-    tile, scale, lane0s, near_is_q, at_ref, low_ref, row_ref, first_ref, lse_ref, cos_ref, sin_ref, *refs
+    tile, scale, n_kv, at_ref, low_ref, row_ref, first_ref, lse_ref, cos_ref, sin_ref, *refs
 ):
-    n_kv = len(lane0s)
-    q_refs = refs[:HEADS]
-    kv_refs = refs[:n_kv] if near_is_q else refs[HEADS : HEADS + n_kv]
-    refs = refs[n_kv if near_is_q else HEADS + n_kv :]
+    q_refs, kv_refs, refs = refs[:HEADS], refs[HEADS : HEADS + n_kv], refs[HEADS + n_kv :]
     o_refs, do_refs, dq_refs = refs[:HEADS], refs[HEADS : 2 * HEADS], refs[2 * HEADS : 3 * HEADS]
     near_ref, far_ref, q_all, kv_all, acc_ref = refs[3 * HEADS :]
-    gather_refs(q_refs, kv_refs, lane0s, q_all, kv_all)
+    gather_refs(q_refs, q_all)
+    gather_refs(kv_refs, kv_all)
     acc_ref[...] = jnp.zeros_like(acc_ref)
     lanes = lax.broadcasted_iota(jnp.int32, (1, tile), 1)
     per_out = dq_refs[0].shape[0] // tile
@@ -246,12 +238,12 @@
     far_ref[:, HD:] = acc_ref[near:, HD:].astype(BF16)
 
 
-def attend(tile, scale, tables, pieces, keys_values, lane0s, near_is_q):
+def attend(tile, scale, tables, pieces, keys_values):
     rows = HEADS * pieces[0].shape[0]
     kv_rows = sum(a.shape[0] for a in keys_values)
-    operands = keys_values if near_is_q else pieces + keys_values
-    return pl.pallas_call(
-        functools.partial(attend_kernel, tile, scale, lane0s, near_is_q),
+    operands = pieces + keys_values
+    return pl.pallas_call(
+        functools.partial(attend_kernel, tile, scale, len(keys_values)),
         out_shape=[jax.ShapeDtypeStruct((rows // HEADS, HD), BF16)] * HEADS
         + [jax.ShapeDtypeStruct((rows // tile, 1, tile), F32)],
         in_specs=[SMEM] * 3 + [VMEM] * (1 + len(operands)),
@@ -263,14 +255,12 @@
     )(*tables, *operands)
 
 
-def attend_back(
-    tile, scale, tables, lse, cosine, sine, pieces, keys_values, lane0s, near_is_q, outs, grads
-):
+def attend_back(tile, scale, tables, lse, cosine, sine, pieces, keys_values, outs, grads):
     rows = HEADS * pieces[0].shape[0]
     kv_rows = sum(a.shape[0] for a in keys_values)
-    operands = (keys_values if near_is_q else pieces + keys_values) + outs + grads
-    return pl.pallas_call(
-        functools.partial(attend_back_kernel, tile, scale, lane0s, near_is_q),
+    operands = pieces + keys_values + outs + grads
+    return pl.pallas_call(
+        functools.partial(attend_back_kernel, tile, scale, len(keys_values)),
         out_shape=[jax.ShapeDtypeStruct((rows // HEADS, HD), BF16)] * HEADS
         + [jax.ShapeDtypeStruct((kv_rows // 2, 2 * HD), BF16)] * 2,
         in_specs=[SMEM] * 3 + [VMEM] * (4 + len(operands)),
@@ -498,6 +488,83 @@
         cost_estimate=cost((8 if with_back else 4) * half * dim * hidden, 16 * 2**20),
         name="feed_own" if with_back else "feed_far",
     )(mine, other, w_up, gact, keep)
+
+
+def back_act_kernel(mine_ref, other_ref, w_ref, out_ref):
+    half = mine_ref.shape[0]
+    out_ref[:half, :] = nt(mine_ref[...], w_ref[...]).astype(BF16)
+    out_ref[half:, :] = nt(other_ref[...], w_ref[...]).astype(BF16)
+
+
+def back_act(mine, other, w_down):
+    half, dim = mine.shape
+    hidden = w_down.shape[0]
+    tile = min(hidden, 512)
+    return pl.pallas_call(
+        back_act_kernel,
+        grid=(hidden // tile,),
+        out_shape=jax.ShapeDtypeStruct((2 * half, hidden), BF16),
+        in_specs=[
+            whole((half, dim)),
+            whole((half, dim)),
+            pl.BlockSpec((tile, dim), lambda i: (i, 0)),
+        ],
+        out_specs=pl.BlockSpec((2 * half, tile), lambda i: (0, i)),
+        compiler_params=params(40),
+        cost_estimate=cost(4 * half * dim * hidden, 12 * 2**20),
+        name="back_act",
+    )(mine, other, w_down)
+
+
+def quad_product_kernel(idx, *refs):
+    cols, rows, (give_ref, keep_ref, turn_ref) = refs[:16], refs[16:20], refs[20:]
+    block = give_ref.shape[0]
+    half = cols[0].shape[0]
+
+    @pl.when(pl.program_id(0) == 0)
+    def _():
+        for j in range(2):
+            for k in range(8):
+                turn_ref[j * block : (j + 1) * block, k * half : (k + 1) * half] = (
+                    cols[8 * j + k][...].astype(F32).T.astype(BF16)
+                )
+
+    tok = 2 * half
+    for j, out in ((0, give_ref), (1, keep_ref)):
+        total = None
+        for k, ref in enumerate(rows):
+            term = nn(turn_ref[j * block : (j + 1) * block, k * tok : (k + 1) * tok], ref[...])
+            total = term if total is None else total + term
+        out[...] = total.astype(out.dtype)
+
+
+def quad_product(idx, cols, rows):
+    half, dim = cols[0].shape
+    tok, width = rows[0].shape
+    block = dim // (2 * HEADS)
+    tile = min(width, 512)
+    give = pl.BlockSpec((half, block), lambda i, idx: (0, 2 * (idx[0] ^ 2) + idx[1]))
+    keep = pl.BlockSpec((half, block), lambda i, idx: (0, 2 * idx[0] + idx[1]))
+    out = pl.BlockSpec((block, tile), lambda i, idx: (0, i))
+    return pl.pallas_call(
+        quad_product_kernel,
+        grid_spec=pltpu.PrefetchScalarGridSpec(
+            num_scalar_prefetch=1,
+            grid=(width // tile,),
+            in_specs=[give] * 8
+            + [keep] * 8
+            + [pl.BlockSpec((tok, tile), lambda i, idx: (0, i))] * 4,
+            out_specs=[out, out],
+            scratch_shapes=[pltpu.VMEM((2 * block, 8 * half), BF16)],
+        ),
+        out_shape=[
+            jax.ShapeDtypeStruct((block, width), BF16),
+            jax.ShapeDtypeStruct((block, width), F32),
+        ],
+        compiler_params=params(40),
+        cost_estimate=cost(16 * half * block * width * 2, 16 * 2**20),
+        name="quad_product",
+    )(idx, *cols, *cols, *rows)
 
 
 def product_kernel(idx, *refs):
@@ -750,11 +817,21 @@
     ).reshape(tok)
     cosine, sine = rotary_tables(own_places - firsts_of(own_places))
 
+    group_buckets = lax.all_gather(buckets, ("h", "y"), axis=0, tiled=True)
+    group_buckets = group_buckets.reshape(HEADS, 2, 2, half)
+
+    def row_mask(plane, parity):
+        chosen = lax.dynamic_slice(group_buckets, (plane, parity, 0, 0), (1, 1, 2, half))
+        kept = (chosen.reshape(2, half) >= tp).astype(F32)
+        return jnp.where(c == 0, kept, kept[::-1]).reshape(tok, 1)
+
     grad_mine, grad_other = half_of(grad_out, c), half_of(grad_out, 1 - c)
-    far_grad_mine = swap(grad_mine, "y")
-
-    packed = list(project(idx, layer_input, gains[0], gains[1], cosine, sine, w_qkv))
-    packed = [packed[0]] + [plane_swap(packed[k], k) for k in range(1, HEADS)]
+    y_grad = swap(grad_mine, "y")
+
+    projected = project(idx, layer_input, gains[0], gains[1], cosine, sine, w_qkv)
+    queries, near_kv = list(projected[:HEADS]), list(projected[HEADS:])
+    near_kv = [near_kv[0]] + [plane_swap(near_kv[k], k) for k in range(1, HEADS)]
+    queries = [queries[0]] + [plane_swap(queries[k], k) for k in range(1, HEADS)]
 
     relative = h ^ jnp.arange(HEADS, dtype=jnp.int32)
     group_order = lax.dynamic_index_in_dim(
@@ -781,34 +858,29 @@
     group_cos, group_sin = rotary_tables((query_places - query_firsts).reshape(2 * HEADS * half))
     tables = (query_at, query_low, key_row, query_firsts.reshape(2 * HEADS, 1, half))
 
+    quarter = lax.dynamic_slice_in_dim(layer_input, tp * (tok // 4), tok // 4, 0)
+    quarter, near_kv[3] = ordered(quarter, near_kv[3])
+    x_all = lax.all_gather(quarter, ("h",) + TP, axis=0, tiled=True)
+
     if depth == 1:
-        far_a = swap(jnp.concatenate([packed[0][:, HD:], packed[1][:, HD:]]), "y")
-        far_b = swap(jnp.concatenate([packed[2][:, HD:], packed[3][:, HD:]]), "y")
-        keys_values, lane0s, near_is_q = packed + [far_a, far_b], [HD] * HEADS + [0, 0], True
+        keys_values = near_kv + [swap(v, "y") for v in near_kv]
     else:
-        near_kv = lax.all_gather(
-            jnp.concatenate([p[:, HD:] for p in packed]), "r", axis=0, tiled=True
-        )
-        keys_values, lane0s, near_is_q = [near_kv, swap(near_kv, "y")], [0, 0], False
-
-    quarter = lax.dynamic_slice_in_dim(layer_input, tp * (tok // 4), tok // 4, 0)
-    quarter, packed[3] = ordered(quarter, packed[3])
-    if depth == 1:
-        keys_values[3] = packed[3]
-    x_all = lax.all_gather(quarter, ("h",) + TP, axis=0, tiled=True)
-
-    far_grad_other = swap(far_grad_mine, "c")
-    grad_act = nt(jnp.concatenate([grad_mine, grad_other]), w_down).astype(BF16)
-    far_grad_act = nt(jnp.concatenate([far_grad_mine, far_grad_other]), w_down).astype(BF16)
-    keep_rows = (buckets >= tp).astype(F32)
-    far_keep = swap(keep_rows, "y")
-    keep_rows = jnp.concatenate([half_of(keep_rows, c), half_of(keep_rows, 1 - c)])[:, None]
-    far_keep = jnp.concatenate([half_of(far_keep, c), half_of(far_keep, 1 - c)])[:, None]
-    grad_act, far_grad_act, group_cos, group_sin, keys_values[-1] = ordered(
-        grad_act, far_grad_act, group_cos, group_sin, keys_values[-1]
-    )
-
-    *attended, lse = attend(half, scale, tables, packed, keys_values, lane0s, near_is_q)
+        near_all = lax.all_gather(jnp.concatenate(near_kv), "r", axis=0, tiled=True)
+        keys_values = [near_all, swap(near_all, "y")]
+    for_plane, queries[3] = ordered(grad_mine, queries[3])
+    z_grad = plane_swap(for_plane, 1)
+
+    y_grad_other = swap(y_grad, "c")
+    grad_act = back_act(grad_mine, grad_other, w_down)
+    y_grad_act = back_act(y_grad, y_grad_other, w_down)
+    masks = [row_mask(h ^ kz, y ^ ky) for kz in range(2) for ky in range(2)]
+    grad_act, y_grad_act, group_cos, group_sin, keys_values[-1], *masks = ordered(
+        grad_act, y_grad_act, group_cos, group_sin, keys_values[-1], *masks
+    )
+
+    *attended, lse = attend(half, scale, tables, queries, keys_values)
+    z_grad, attended[1] = ordered(z_grad, attended[1])
+    zy_grad = swap(z_grad, "y")
     pieces = [attended[0]] + [plane_swap(attended[k], k) for k in range(1, HEADS)]
     flat, keep, give = out_project(idx, w_out, pieces)
 
@@ -816,27 +888,27 @@
         return (keep.astype(F32) + swap(give, "c").astype(F32)).astype(BF16)
 
     chip = chip_sum(keep, give)
-    x_mid, h_mine = norm(half_of(layer_input, c), chip, swap(chip, "x"), gains[2], gains[3])
+    chip_far = swap(chip, "x")
+    z_grad_other, zy_grad_other = swap(z_grad, "c"), swap(zy_grad, "c")
+    z_grad_act = back_act(z_grad, z_grad_other, w_down)
+    zy_grad_act = back_act(zy_grad, zy_grad_other, w_down)
+    h_all = regroup(norm_all(x_all, gains[0], gains[1]))
+    z_grad_act, zy_grad_act, h_all, chip_far = ordered(z_grad_act, zy_grad_act, h_all, chip_far)
+
+    x_mid, h_mine = norm(half_of(layer_input, c), chip, chip_far, gains[2], gains[3])
     h_other = swap(h_mine, "c")
-    far_h_mine = swap(h_mine, "y")
-    far_flat = swap(flat, "y")
-    act, du, keep, give = feed_forward(h_mine, h_other, w_up, grad_act, keep_rows, True)
+    y_h = swap(h_mine, "y")
+    z_h = plane_swap(h_mine, 1)
+    act, du, keep, give = feed_forward(h_mine, h_other, w_up, grad_act, masks[0], True)
     chip = chip_sum(keep, give)
     chip_far = swap(chip, "x")
 
-    far_h_other = swap(far_h_mine, "c")
-    far_act, far_du = feed_forward(far_h_mine, far_h_other, w_up, far_grad_act, far_keep, False)
-    down_part = scatter(
-        product(
-            idx,
-            [regroup(v) for v in (grad_mine, grad_other, far_grad_mine, far_grad_other)],
-            act,
-            far_act,
-        )
-    )
-    up_part = scatter(
-        product(idx, [regroup(v) for v in (h_mine, h_other, far_h_mine, far_h_other)], du, far_du)
-    )
+    y_h_other = swap(y_h, "c")
+    y_act, y_du = feed_forward(y_h, y_h_other, w_up, y_grad_act, masks[1], False)
+    zy_h = swap(z_h, "y")
+    z_h_other = swap(z_h, "c")
+    z_act, z_du = feed_forward(z_h, z_h_other, w_up, z_grad_act, masks[2], False)
+    y_act, z_act, chip_far = ordered(y_act, z_act, chip_far)
 
     grad_mid, dy_mine, gain_two_grad, bias_two_grad = norm_back(
         chip, chip_far, x_mid, grad_mine, gains[2]
@@ -844,40 +916,40 @@
     dy_other = swap(dy_mine, "c")
     grads = list(out_back(idx, w_out, dy_mine, dy_other))
     grads = [grads[0]] + [plane_swap(grads[k], k) for k in range(1, HEADS)]
-
-    far_dy_mine = swap(dy_mine, "y")
-    far_dy_other = swap(far_dy_mine, "c")
-    wout_part = scatter(
-        product(
-            idx_rows,
-            [regroup(v) for v in (dy_mine, dy_other, far_dy_mine, far_dy_other)],
-            flat,
-            far_flat,
-        )
-    )
-    feed = [jnp.dot(act[s], w_down, preferred_element_type=F32).astype(BF16) for s in (slice(half), slice(half, tok))]
-    feed_chip = chip_sum(feed[0], feed[1])
-    out_mine = (
-        x_mid + (feed_chip.astype(F32) + swap(feed_chip, "x").astype(F32))
-    ).astype(BF16)
-    layer_output = join(idx, out_mine, swap(out_mine, "c"), BF16)
+    y_dy = swap(dy_mine, "y")
+    y_flat = swap(flat, "y")
+
+    zy_h_other = swap(zy_h, "c")
+    zy_act, zy_du = feed_forward(zy_h, zy_h_other, w_up, zy_grad_act, masks[3], False)
+    quad_grads = [grad_mine, grad_other, y_grad, y_grad_other, z_grad, z_grad_other, zy_grad, zy_grad_other]
+    down_give, down_keep = quad_product(
+        idx, [regroup(v) for v in quad_grads], [act, y_act, z_act, zy_act]
+    )
+    down_give, grads[3] = ordered(down_give, grads[3])
+    down_got = plane_swap(down_give, 2)
 
     *dq, near, far = attend_back(
-        half,
-        scale,
-        tables,
-        lse,
-        group_cos,
-        group_sin,
-        packed,
-        keys_values,
-        lane0s,
-        near_is_q,
-        attended,
-        grads,
+        half, scale, tables, lse, group_cos, group_sin, queries, keys_values, attended, grads
     )
     got = swap(far, "y")
     dq_pieces = [dq[0]] + [plane_swap(dq[k], k) for k in range(1, HEADS)]
+
+    quad_rows = [h_mine, h_other, y_h, y_h_other, z_h, z_h_other, zy_h, zy_h_other]
+    first_row, near = ordered(quad_rows[0], near)
+    quad_rows[0] = first_row
+    up_give, up_keep = quad_product(
+        idx, [regroup(v) for v in quad_rows], [du, y_du, z_du, zy_du]
+    )
+    feed_act, near = ordered(act, near)
+    feed = [
+        jnp.dot(feed_act[s], w_down, preferred_element_type=F32).astype(BF16)
+        for s in (slice(half), slice(half, tok))
+    ]
+    up_give, feed[0], feed[1], got = ordered(up_give, feed[0], feed[1], got)
+    up_got = plane_swap(up_give, 2)
+    feed_chip = chip_sum(feed[0], feed[1])
+    feed_far = swap(feed_chip, "x")
+
     if depth > 1:
         near = lax.psum_scatter(near, "r", scatter_dimension=0, tiled=True)
         got = lax.psum_scatter(got, "r", scatter_dimension=0, tiled=True)
@@ -885,22 +957,39 @@
     dkv_pieces = [dkv[:tok]] + [
         plane_swap(dkv[k * tok : (k + 1) * tok], k) for k in range(1, HEADS)
     ]
+
+    head_give, head_keep = head_product(idx, h_all, dkv, dq)
+    y_dy_other = swap(y_dy, "c")
+    wout_cols = [regroup(v) for v in (dy_mine, dy_other, y_dy, y_dy_other)]
+    wout_cols[0], dkv_pieces[0] = ordered(wout_cols[0], dkv_pieces[0])
+    wout_sum = product(idx_rows, wout_cols, flat, y_flat)
+    head_give, wout_sum, dkv_pieces[3] = ordered(head_give, wout_sum, dkv_pieces[3])
+    wout_part = scatter(wout_sum)
     keep, give = project_back(idx, w_qkv, dq_pieces, dkv_pieces)
+    head_got = swap(head_give, "y")
     chip = chip_sum(keep, give)
     chip_far = swap(chip, "x")
 
-    h_all = regroup(norm_all(x_all, gains[0], gains[1]))
-    head_give, head_keep = head_product(idx, h_all, dkv, dq)
-    head_sum = (head_keep.astype(F32) + swap(head_give, "y").astype(F32)).astype(BF16)
+    head_sum = (head_keep.astype(F32) + head_got.astype(F32)).astype(BF16)
     if depth > 1:
         head_sum = lax.psum_scatter(head_sum, "r", scatter_dimension=2, tiled=True)
     head_pieces = [head_sum[0]] + [plane_swap(head_sum[k], k) for k in range(1, HEADS)]
-    qkv_part = head_place(idx, head_pieces)
+    down_part = down_keep + down_got.astype(F32)
+    up_part = up_keep + up_got.astype(F32)
+    if depth > 1:
+        down_part, up_part = (
+            lax.psum_scatter(v, "r", scatter_dimension=0, tiled=True) for v in (down_part, up_part)
+        )
+    out_mine = (x_mid + (feed_chip.astype(F32) + feed_far.astype(F32))).astype(BF16)
+    out_other = swap(out_mine, "c")
+    layer_output = join(idx, out_mine, out_other, BF16)
+    layer_output, chip_far = ordered(layer_output, chip_far)
 
     _, grad_low, gain_one_grad, bias_one_grad = norm_back(
         chip, chip_far, half_of(layer_input, c), grad_mid, gains[0]
     )
     grad_input = join(idx, grad_low, swap(grad_low, "c"), F32)
+    qkv_part = head_place(idx, head_pieces)
 
     counts = jnp.sum(
         (half_of(buckets, c)[:, None] == jnp.arange(NB, dtype=jnp.int32)[None, :]).astype(F32),
@@ -925,8 +1014,8 @@
         wout_part.astype(F32).T,
         sums[2 * dim : 3 * dim],
         sums[3 * dim : 4 * dim],
-        up_part.astype(F32),
-        down_part.astype(F32).T,
+        up_part,
+        down_part.T,
         sums[4 * dim :].astype(jnp.int32),
     )
 

time: 594 us -> 618 us (1.040)
  waiting for transfers between devices: 258 us -> 183 us
  Pallas kernels: 127 us -> 177 us
  blocking collectives: 0 us -> 44 us
  local copies, waits for them, and re-layouts: 35.9 us -> 62.4 us
  matrix products: 30.8 us -> 13.5 us
    ppermute x26 -> x33, waiting for transfers between devices: 191 us -> 43.8 us  [swap(): return lax.ppermute(value, axis, [(0, 1), (1, 0)])]
    ppermute x21 -> x28, waiting for transfers between devices: 66.3 us -> 139 us  [plane_swap(): return lax.ppermute(value, 'h', [(i, i ^ k) for i in range(HEADS)])]
    all_gather x0 -> x1, blocking collectives: none -> 44 us  [body(): group_buckets = lax.all_gather(buckets, ('h', 'y'), axis=0, tiled=True)]
    pallas_call x2 -> x8, Pallas kernels: 33.5 us -> 70.9 us  [the longest x4 21.2 us: back_act(): pl.pallas_call(back_act_kernel, grid=(hidden // tile,), out_shape=jax.Sha...]
    unnamed x126 -> x202, local copies, waits for them, and re-layouts: 22.9 us -> 55.8 us
    pallas_call x2 -> x4, Pallas kernels: 23.6 us -> 42.6 us  [feed_forward(): pl.pallas_call(feed_kernel, grid=(hidden // tile,), out_shape=[tall, tall...]
    dot_general x4 -> x2, matrix products: 30.8 us -> 13.5 us  [body(): jnp.dot(feed_act[s], w_down, preferred_element_type=F32).astype(BF16)]
    pallas_call x3 -> x1, Pallas kernels: 19 us -> 4.32 us  [product(): pl.pallas_call(product_kernel, grid_spec=pltpu.PrefetchScalarGridSpec(num...]
  transfers between devices with their start and end apart: 51 -> 63, of which waited for: 23 -> 14; matrix products, arithmetic and copies ran while one was open for 12% -> 8% of each run, Pallas kernels for 13% -> 26%
where the time goes in v3:
time: 618 us; the launch traced here: 613 us
  waiting for transfers between devices  183 us (30%)
  Pallas kernels  177 us (29%)
  starting transfers between devices  90.9 us (15%)
  local copies, waits for them, and re-layouts  62.4 us (10%)
  blocking collectives  44 us (7%)
  other arithmetic  26.9 us (4%)
  between operations  15.7 us (3%)
  matrix products  13.5 us (2%)
    ppermute x28, waiting for transfers between devices, plane_swap(): return lax.ppermute(value, 'h', [(i, i ^ k) for i in range(HEADS)])  139 us
    ppermute x28, starting transfers between devices, plane_swap(): return lax.ppermute(value, 'h', [(i, i ^ k) for i in range(HEADS)])  57.3 us
    unnamed x202, local copies, waits for them, and re-layouts  55.8 us
    all_gather x1, blocking collectives, body(): group_buckets = lax.all_gather(buckets, ('h', 'y'), axis=0, tiled=True)  44 us
    ppermute x33, waiting for transfers between devices, swap(): return lax.ppermute(value, axis, [(0, 1), (1, 0)])  43.8 us
    pallas_call x4, Pallas kernels, feed_forward(): pl.pallas_call(feed_kernel, grid=(hidden // tile,), out_shape=[tall, tall...  42.6 us
    ppermute x33, starting transfers between devices, swap(): return lax.ppermute(value, axis, [(0, 1), (1, 0)])  33.5 us
    pallas_call x4, Pallas kernels, back_act(): pl.pallas_call(back_act_kernel, grid=(hidden // tile,), out_shape=jax.Sha...  21.2 us
  transfers between devices with their start and end apart: 63, of which 14 were waited for; matrix products, arithmetic and copies ran while one was open for 8% of the time, Pallas kernels for 26%

profile of v3, /device:TPU:0, one launch (start us, length us, event | category | flops | bytes accessed | tf_op | source)
XLA Modules:
  0.0 612.6 jit_solution(14966988686502018246)
XLA Ops:
  13.9 9.7 %project.1 = (bf16[512,128]{1,0:T(8,128)(2,1)S(1)}, bf16[512,128]{1,0:T(8,128)(2,1)}, bf16[512,128]{1,0:T(8,128)(2,1)S(1)}, bf16[512,128]{1,0:T(8,128)(2,1)S(1)}...) custom-call(s32[5]{0:T(128)S(1)} %stack.25.idx, ...), custom_call_target="tpu_custom_call" | custom-call | flops 3221225472 | bytes 10485760 | tf_op jit(solution)/shard_map/project/pallas_call | solution.py:107
  24.9 5.0 collective-permute-start.5
  30.8 5.8 collective-permute-done.5.refs_7_
  40.0 3.5 collective-permute-start.2
  43.5 3.3 collective-permute-start.3
  48.8 44.0 %all-gather = s32[8,1,512]{2,1,0:T(1,128)S(1)} all-gather(s32[1,1,512]{2,1,0:T(1,128)S(1)} %bitcast.84), channel_id=1, replica_groups=mesh['r'=1,'h'=4,'y'=2,'x'=2,'c'=2] {'h','y'}, dimensions={0}, use_global_device_ids=true | all-gather | bytes 18432 | tf_op jit(solution)/shard_map/all_gather | solution.py:820
  94.0 3.4 copy-done.49
  97.4 5.3 back_act.4.gact_ref
  102.7 3.7 fusion.2
  119.2 3.8 copy-done.50
  123.0 5.3 back_act.5.gact_ref
  129.6 15.1 %collective-permute-done.1.refs_2_ = bf16[512,128]{1,0:T(8,128)(2,1)S(1)} collective-permute-done((bf16[512,128]{1,0:T(8,128)(2,1)S(1)}, bf16[512,128]{1,0:T(8,128)(2,1)S(1)}, u32[]{:S(2)}, u32[]{:S(2)}) %collective-permute-start.1) | collective-permute-done | bytes 131104 | tf_op jit(solution)/shard_map/ppermute | solution.py:31
  144.9 13.7 %attend.1 = (bf16[512,128]{1,0:T(8,128)(2,1)S(1)}, bf16[512,128]{1,0:T(8,128)(2,1)S(1)}, bf16[512,128]{1,0:T(8,128)(2,1)S(1)}, bf16[512,128]{1,0:T(8,128)(2,1)S(1)}, f32[8,1,256]{2,1,0:T(1,128)S(1)}) custom-call(s32[8]{0:T(128)S(1)} %reshape.229.at_ref, s32[8]{0:T(128)S(1)} %and_select_fusion.6.low_ref, s32[16]{0:T(128)S(1)} %fusion.8.row_ref, ...), custom_call_target="tpu_custom_call" | custom-call | flops 1342177280 | bytes 4194304 | tf_op jit(solution)/shard_map/attend/pallas_call | solution.py:245
  164.0 7.8 %collective-permute-start.18 = (bf16[256,2048]{1,0:T(8,128)(2,1)S(1)}, bf16[256,2048]{1,0:T(8,128)(2,1)S(1)}, u32[]{:S(2)}, u32[]{:S(2)}) collective-permute-start(bf16[256,2048]{1,0:T(8,128)(2,1)S(1)} %collective-permute-done.12.mine_ref.refs_4_.refs_12_), channel_id=1, source_target_pairs={{0,4},{4,0},{1,5},{5,1},{2,6},{6,2},{3,7},{7,3},{8,12},{12,8},{9,1... | collective-permute-start | bytes 3145736 | tf_op jit(solution)/shard_map/ppermute | solution.py:27
  177.4 16.8 %collective-permute-done.18.mine_ref.refs_6_.refs_14_ = bf16[256,2048]{1,0:T(8,128)(2,1)S(1)} collective-permute-done((bf16[256,2048]{1,0:T(8,128)(2,1)S(1)}, bf16[256,2048]{1,0:T(8,128)(2,1)S(1)}, u32[]{:S(2)}, u32[]{:S(2)}) %collective-permute-start.18) | collective-permute-done | bytes 1048608 | tf_op jit(solution)/shard_map/ppermute | solution.py:27
  196.8 3.4 copy-done.51
  200.2 5.4 back_act.6.gact_ref
  206.9 5.3 back_act.7.gact_ref
  214.5 3.4 copy-done
  217.9 6.6 %norm_all.1.h_ref = bf16[2048,2048]{1,0:T(8,128)(2,1)S(1)} custom-call(bf16[2048,2048]{1,0:T(8,128)(2,1)S(1)} %copy-done, f32[1,2048]{1,0:T(1,128)S(1)} %bitcast.66, f32[1,2048]{1,0:T(1,128)S(1)} %bitcast.71), custom_call_target="tpu_custom_call" | custom-call | flops 67108864 | bytes 16777216 | tf_op jit(solution)/shard_map/norm_all/pallas_call | solution.py:385
  224.5 3.4 copy-done.1
  227.9 4.1 norm.1
  236.3 14.1 %feed_own.1 = (bf16[512,2048]{1,0:T(8,128)(2,1)}, bf16[512,2048]{1,0:T(8,128)(2,1)}, bf16[256,2048]{1,0:T(8,128)(2,1)S(1)}, bf16[256,2048]{1,0:T(8,128)(2,1)S(1)}) custom-call(bf16[256,2048]{1,0:T(8,128)(2,1)} %get-tuple-element.157.mine_ref.refs_0_.refs_8_, bf16[256,2048]{1,0:T(8,128)(2,1)} %collective-permute-done.21.other_ref.refs_1_.refs_9_, ...), custom_call_target="tpu_custom_call" | custom-call | flops 8589934592 | bytes 16777216 | tf_op jit(solution)/shard_map/feed_own/pallas_call | solution.py:474
  250.7 8.8 %collective-permute-done.25.mine_ref.refs_4_.refs_12_ = bf16[256,2048]{1,0:T(8,128)(2,1)} collective-permute-done((bf16[256,2048]{1,0:T(8,128)(2,1)}, bf16[256,2048]{1,0:T(8,128)(2,1)}, u32[]{:S(2)}, u32[]{:S(2)}) %collective-permute-start.25) | collective-permute-done | bytes 1048608 | tf_op jit(solution)/shard_map/ppermute | solution.py:31
  265.0 19.3 %collective-permute-done.31.mine_ref.refs_6_.refs_14_ = bf16[256,2048]{1,0:T(8,128)(2,1)} collective-permute-done((bf16[256,2048]{1,0:T(8,128)(2,1)}, bf16[256,2048]{1,0:T(8,128)(2,1)}, u32[]{:S(2)}, u32[]{:S(2)}) %collective-permute-start.31) | collective-permute-done | bytes 1048608 | tf_op jit(solution)/shard_map/ppermute | solution.py:27
  285.3 9.3 %feed_far.4 = (bf16[512,2048]{1,0:T(8,128)(2,1)S(1)}, bf16[512,2048]{1,0:T(8,128)(2,1)}) custom-call(bf16[256,2048]{1,0:T(8,128)(2,1)} %collective-permute-done.25.mine_ref.refs_4_.refs_12_, bf16[256,2048]{1,0:T(8,128)(2,1)} %collective-permute-done.26.other_ref.refs_5_.refs_13_, bf16[2048,2048]{1,0:T(8,128)(2,1)} %w_ref.22, bf16[512,2048]{1,0:T(8,128)(2,1)} %copy-done.80, ...), custom_call_target="tpu_custom_call" | custom-call | flops 4294967296 | bytes 16777216 | tf_op jit(solution)/shard_map/feed_far/pallas_call | solution.py:474
  295.9 9.5 %feed_far.3 = (bf16[512,2048]{1,0:T(8,128)(2,1)S(1)}, bf16[512,2048]{1,0:T(8,128)(2,1)}) custom-call(bf16[256,2048]{1,0:T(8,128)(2,1)} %collective-permute-done.23.mine_ref.refs_2_.refs_10_, bf16[256,2048]{1,0:T(8,128)(2,1)} %collective-permute-done.24.other_ref.refs_3_.refs_11_, bf16[2048,2048]{1,0:T(8,128)(2,1)} %w_ref.22, bf16[512,2048]{1,0:T(8,128)(2,1)} %copy-done.78, ...), custom_call_target="tpu_custom_call" | custom-call | flops 4294967296 | bytes 16777216 | tf_op jit(solution)/shard_map/feed_far/pallas_call | solution.py:474
  306.7 4.4 norm_back.2
  315.0 9.7 %feed_far.5 = (bf16[512,2048]{1,0:T(8,128)(2,1)S(1)}, bf16[512,2048]{1,0:T(8,128)(2,1)}) custom-call(bf16[256,2048]{1,0:T(8,128)(2,1)} %collective-permute-done.31.mine_ref.refs_6_.refs_14_, bf16[256,2048]{1,0:T(8,128)(2,1)} %collective-permute-done.32.other_ref.refs_7_.refs_15_, bf16[2048,2048]{1,0:T(8,128)(2,1)} %w_ref.22, bf16[512,2048]{1,0:T(8,128)(2,1)} %copy-done.79, ...), custom_call_target="tpu_custom_call" | custom-call | flops 4294967296 | bytes 16777216 | tf_op jit(solution)/shard_map/feed_far/pallas_call | solution.py:474
  324.8 4.7 out_back.1
  333.9 8.5 %quad_product.2 = (bf16[256,2048]{1,0:T(8,128)(2,1)}, f32[256,2048]{1,0:T(8,128)S(1)}) custom-call(s32[5]{0:T(128)S(1)} %stack.25.idx, bf16[256,2048]{1,0:T(8,128)(2,1)S(1)} %get-tuple-element.117.mine_ref.base_ref.refs_0_.refs_8_, bf16[256,2048]{1,0:T(8,128)(2,1)S(1)} %get-tuple-element.241.other_ref.refs_1_.refs_9_, bf16[256,2048]{1,0:T(8,128)(2,1)S(1)} %copy-done.7, ...), custom_call_target="tpu_custom_call" | custom-call | flops 4294967296 | bytes 16777216 | tf_op jit(solution)/shard_map/quad_product/pallas_call | solution.py:549
  344.5 18.3 %attend_back.1 = (bf16[512,128]{1,0:T(8,128)(2,1)}, bf16[512,128]{1,0:T(8,128)(2,1)}, bf16[512,128]{1,0:T(8,128)(2,1)}, bf16[512,128]{1,0:T(8,128)(2,1)}, bf16[2...) custom-call(s32[8]{0:T(128)} %copy-done.47, s32[8]{0:T(128)} %copy-done.77, s32[16]{0:T(128)} %copy-done.48, ...), custom_call_target="tpu_custom_call" | custom-call | flops 3355443200 | bytes 8388608 | tf_op jit(solution)/shard_map/attend_back/pallas_call | solution.py:262
  362.8 6.8 %convolution_convert_fusion = bf16[256,2048]{1,0:T(8,128)(2,1)} fusion(bf16[2048,2048]{1,0:T(8,128)(2,1)} %w_ref.17, bf16[512,2048]{1,0:T(8,128)(2,1)S(1)} %copy-done.29), kind=kOutput, calls=%fused_computation | convolution fusion | flops 2148007936 | bytes 10485760 | tf_op jit(solution)/shard_map/dot_general | solution.py:945
  369.5 5.7 collective-permute-start.34
  375.3 6.7 %convolution_convert_fusion.1 = bf16[256,2048]{1,0:T(8,128)(2,1)} fusion(bf16[2048,2048]{1,0:T(8,128)(2,1)} %w_ref.17, bf16[512,2048]{1,0:T(8,128)(2,1)S(1)} %copy-done.29), kind=kOutput, calls=%fused_computation.1 | convolution fusion | flops 2148007936 | bytes 10485760 | tf_op jit(solution)/shard_map/dot_general | solution.py:945
  382.0 9.3 %quad_product.3 = (bf16[256,2048]{1,0:T(8,128)(2,1)S(1)}, f32[256,2048]{1,0:T(8,128)S(1)}) custom-call(s32[5]{0:T(128)S(1)} %stack.25.idx, bf16[256,2048]{1,0:T(8,128)(2,1)} %get-tuple-element.157.mine_ref.refs_0_.refs_8_, bf16[256,2048]{1,0:T(8,128)(2,1)} %collective-permute-done.21.other_ref.refs_1_.refs_9_, ...), custom_call_target="tpu_custom_call" | custom-call | flops 4294967296 | bytes 16777216 | tf_op jit(solution)/shard_map/quad_product/pallas_call | solution.py:549
  393.6 3.9 collective-permute-done.34.got_ref
  414.6 2.9 collective-permute-start.42
  418.4 3.4 copy-done.2
  421.8 8.8 %head_product.1 = (bf16[4,384,256]{2,1,0:T(8,128)(2,1)}, bf16[4,384,256]{2,1,0:T(8,128)(2,1)S(1)}) custom-call(s32[5]{0:T(128)S(1)} %stack.25.idx, bf16[2048,2048]{1,0:T(8,128)(2,1)S(1)} %copy-done.2, bf16[2048,256]{1,0:T(8,128)(2,1)S(1)} %settle.1.dkv_ref, bf16[512,128]{1,0:T(8,128)(2,1)S(1)} %copy-done.83, bf16[512,128]{1,0:T(8,128)(2,1)} %get-tuple-element.169.refs_1_, ...), custom_call_target="tpu_custom_call" | custom-call | flops 3221225472 | bytes 12582912 | tf_op jit(solution)/shard_map/head_product/pallas_call | solution.py:644
  431.5 4.3 product.1
  442.6 5.9 project_back.1
  448.6 9.4 %collective-permute-start.60 = (bf16[256,2048]{1,0:T(8,128)(2,1)}, bf16[256,2048]{1,0:T(8,128)(2,1)}, u32[]{:S(2)}, u32[]{:S(2)}) collective-permute-start(bf16[256,2048]{1,0:T(8,128)(2,1)} %get-tuple-element.196), channel_id=1, source_target_pairs={{0,16},{8,24},{16,0},{24,8},{1,17},{9,25},{17,1},{25,9},{2,18},{10... | collective-permute-start | bytes 3145736 | tf_op jit(solution)/shard_map/ppermute | solution.py:31
  461.7 59.7 %collective-permute-done.60 = bf16[256,2048]{1,0:T(8,128)(2,1)} collective-permute-done((bf16[256,2048]{1,0:T(8,128)(2,1)}, bf16[256,2048]{1,0:T(8,128)(2,1)}, u32[]{:S(2)}, u32[]{:S(2)}) %collective-permute-start.60) | collective-permute-done | bytes 1048608 | tf_op jit(solution)/shard_map/ppermute | solution.py:31
  521.3 3.5 add_bitcast_fusion
  532.2 4.6 norm_back.3
  542.0 42.0 %collective-permute-done.59 = bf16[256,2048]{1,0:T(8,128)(2,1)S(1)} collective-permute-done((bf16[256,2048]{1,0:T(8,128)(2,1)}, bf16[256,2048]{1,0:T(8,128)(2,1)S(1)}, u32[]{:S(2)}, u32[]{:S(2)}) %collective-permute-start.59) | collective-permute-done | bytes 1048608 | tf_op jit(solution)/shard_map/ppermute | solution.py:31
  590.3 4.8 collective-permute-start.52
  (376 shorter events, 131.1 us)
Async XLA Ops:
  7.2 207.3 %all-gather.3.cloned.1.call-start = ((), (), s32[]{:S(2)}) async-start(), calls=%async_computation.1 | async-start | bytes 8912896 | tf_op jit(solution)/shard_map/all_gather | solution.py:863
  36.6 560.9 %reduce-scatter.2.cloned.1.call-start = ((), (), s32[]{:S(2)}) async-start(), calls=%async_computation.2 | async-start | bytes 1310720 | tf_op jit(solution)/shard_map/reduce_scatter | solution.py:807
  38.4 68.0 %collective-permute-start.9 = (bf16[256,2048]{1,0:T(8,128)(2,1)S(1)}, bf16[256,2048]{1,0:T(8,128)(2,1)S(1)}, u32[]{:S(2)}, u32[]{:S(2)}) collective-permute-start(bf16[256,2048]{1,0:T(8,128)(2,1)S(1)} %get-tuple-element.117.mine_ref.base_ref.refs_0_.refs_8_), channel_id=1, source_target_pairs={{0,4},{4,0},{1,5},{5,1},{2,6},{6,2},{3,7},{7,3},{8,12},{12,8},{9,1... | collective-permute-start | bytes 3145736 | tf_op jit(solution)/shard_map/ppermute | solution.py:27
  40.0 67.4 %collective-permute-start.2 = (bf16[512,128]{1,0:T(8,128)(2,1)}, bf16[512,128]{1,0:T(8,128)(2,1)S(1)}, u32[]{:S(2)}, u32[]{:S(2)}) collective-permute-start(bf16[512,128]{1,0:T(8,128)(2,1)} %copy-done.70), channel_id=1, source_target_pairs={{0,24},{8,16},{16,8},{24,0},{1,25},{9,17},{17,9},{25,1},{2,26},{10... | collective-permute-start | bytes 393224 | tf_op jit(solution)/shard_map/ppermute | solution.py:31
  43.5 68.5 %collective-permute-start.3 = (bf16[512,256]{1,0:T(8,128)(2,1)}, bf16[512,256]{1,0:T(8,128)(2,1)}, u32[]{:S(2)}, u32[]{:S(2)}) collective-permute-start(bf16[512,256]{1,0:T(8,128)(2,1)} %get-tuple-element.111), channel_id=1, source_target_pairs={{0,8},{8,0},{16,24},{24,16},{1,9},{9,1},{17,25},{25,17},{2,10},{10... | collective-permute-start | bytes 786440 | tf_op jit(solution)/shard_map/ppermute | solution.py:31
  46.8 65.3 %collective-permute-start.4 = (bf16[512,256]{1,0:T(8,128)(2,1)}, bf16[512,256]{1,0:T(8,128)(2,1)}, u32[]{:S(2)}, u32[]{:S(2)}) collective-permute-start(bf16[512,256]{1,0:T(8,128)(2,1)} %get-tuple-element.112), channel_id=1, source_target_pairs={{0,16},{8,24},{16,0},{24,8},{1,17},{9,25},{17,1},{25,9},{2,18},{10... | collective-permute-start | bytes 786440 | tf_op jit(solution)/shard_map/ppermute | solution.py:31
  46.8 60.9 %collective-permute-start = (bf16[512,128]{1,0:T(8,128)(2,1)}, bf16[512,128]{1,0:T(8,128)(2,1)}, u32[]{:S(2)}, u32[]{:S(2)}) collective-permute-start(bf16[512,128]{1,0:T(8,128)(2,1)} %get-tuple-element.106), channel_id=1, source_target_pairs={{0,8},{8,0},{16,24},{24,16},{1,9},{9,1},{17,25},{25,17},{2,10},{10... | collective-permute-start | bytes 393224 | tf_op jit(solution)/shard_map/ppermute | solution.py:31
  106.4 12.7 %collective-permute-start.10 = (bf16[256,2048]{1,0:T(8,128)(2,1)S(1)}, bf16[256,2048]{1,0:T(8,128)(2,1)S(1)}, u32[]{:S(2)}, u32[]{:S(2)}) collective-permute-start(bf16[256,2048]{1,0:T(8,128)(2,1)S(1)} %collective-permute-done.9.mine_ref.refs_2_.refs_10_), channel_id=1, source_target_pairs={{0,1},{1,0},{2,3},{3,2},{4,5},{5,4},{6,7},{7,6},{8,9},{9,8},{10,11... | collective-permute-start | bytes 3145736 | tf_op jit(solution)/shard_map/ppermute | solution.py:27
  107.4 51.3 %collective-permute-start.12 = (bf16[256,2048]{1,0:T(8,128)(2,1)S(1)}, bf16[256,2048]{1,0:T(8,128)(2,1)S(1)}, u32[]{:S(2)}, u32[]{:S(2)}) collective-permute-start(bf16[256,2048]{1,0:T(8,128)(2,1)S(1)} %get-tuple-element.117.mine_ref.base_ref.refs_0_.refs_8_), channel_id=1, source_target_pairs={{0,8},{8,0},{16,24},{24,16},{1,9},{9,1},{17,25},{25,17},{2,10},{10... | collective-permute-start | bytes 3145736 | tf_op jit(solution)/shard_map/ppermute | solution.py:31
  112.0 32.7 %collective-permute-start.6 = (bf16[512,256]{1,0:T(8,128)(2,1)S(1)}, bf16[512,256]{1,0:T(8,128)(2,1)S(1)}, u32[]{:S(2)}, u32[]{:S(2)}) collective-permute-start(bf16[512,256]{1,0:T(8,128)(2,1)S(1)} %copy-done.56), channel_id=1, source_target_pairs={{0,4},{4,0},{1,5},{5,1},{2,6},{6,2},{3,7},{7,3},{8,12},{12,8},{9,1... | collective-permute-start | bytes 786440 | tf_op jit(solution)/shard_map/ppermute | solution.py:27
  112.1 32.6 %collective-permute-start.1 = (bf16[512,128]{1,0:T(8,128)(2,1)S(1)}, bf16[512,128]{1,0:T(8,128)(2,1)S(1)}, u32[]{:S(2)}, u32[]{:S(2)}) collective-permute-start(bf16[512,128]{1,0:T(8,128)(2,1)S(1)} %copy-done.69), channel_id=1, source_target_pairs={{0,16},{8,24},{16,0},{24,8},{1,17},{9,25},{17,1},{25,9},{2,18},{10... | collective-permute-start | bytes 393224 | tf_op jit(solution)/shard_map/ppermute | solution.py:31
  117.1 27.7 %collective-permute-start.7 = (bf16[512,256]{1,0:T(8,128)(2,1)}, bf16[512,256]{1,0:T(8,128)(2,1)S(1)}, u32[]{:S(2)}, u32[]{:S(2)}) collective-permute-start(bf16[512,256]{1,0:T(8,128)(2,1)} %collective-permute-done.3.refs_5_), channel_id=1, source_target_pairs={{0,4},{4,0},{1,5},{5,1},{2,6},{6,2},{3,7},{7,3},{8,12},{12,8},{9,1... | collective-permute-start | bytes 786440 | tf_op jit(solution)/shard_map/ppermute | solution.py:27
  119.1 25.7 %collective-permute-start.8 = (bf16[512,256]{1,0:T(8,128)(2,1)}, bf16[512,256]{1,0:T(8,128)(2,1)S(1)}, u32[]{:S(2)}, u32[]{:S(2)}) collective-permute-start(bf16[512,256]{1,0:T(8,128)(2,1)} %collective-permute-done.4.refs_6_), channel_id=1, source_target_pairs={{0,4},{4,0},{1,5},{5,1},{2,6},{6,2},{3,7},{7,3},{8,12},{12,8},{9,1... | collective-permute-start | bytes 786440 | tf_op jit(solution)/shard_map/ppermute | solution.py:27
  158.7 13.0 %collective-permute-start.13 = (bf16[512,128]{1,0:T(8,128)(2,1)S(1)}, bf16[512,128]{1,0:T(8,128)(2,1)S(1)}, u32[]{:S(2)}, u32[]{:S(2)}) collective-permute-start(bf16[512,128]{1,0:T(8,128)(2,1)S(1)} %get-tuple-element.119.refs_13_), channel_id=1, source_target_pairs={{0,8},{8,0},{16,24},{24,16},{1,9},{9,1},{17,25},{25,17},{2,10},{10... | collective-permute-start | bytes 393224 | tf_op jit(solution)/shard_map/ppermute | solution.py:31
  164.0 30.2 %collective-permute-start.18 = (bf16[256,2048]{1,0:T(8,128)(2,1)S(1)}, bf16[256,2048]{1,0:T(8,128)(2,1)S(1)}, u32[]{:S(2)}, u32[]{:S(2)}) collective-permute-start(bf16[256,2048]{1,0:T(8,128)(2,1)S(1)} %collective-permute-done.12.mine_ref.refs_4_.refs_12_), channel_id=1, source_target_pairs={{0,4},{4,0},{1,5},{5,1},{2,6},{6,2},{3,7},{7,3},{8,12},{12,8},{9,1... | collective-permute-start | bytes 3145736 | tf_op jit(solution)/shard_map/ppermute | solution.py:27
  176.9 17.3 %collective-permute-start.16 = (bf16[256,2048]{1,0:T(8,128)(2,1)S(1)}, bf16[256,2048]{1,0:T(8,128)(2,1)S(1)}, u32[]{:S(2)}, u32[]{:S(2)}) collective-permute-start(bf16[256,2048]{1,0:T(8,128)(2,1)S(1)} %get-tuple-element.123), channel_id=1, source_target_pairs={{0,1},{1,0},{2,3},{3,2},{4,5},{5,4},{6,7},{7,6},{8,9},{9,8},{10,11... | collective-permute-start | bytes 3145736 | tf_op jit(solution)/shard_map/ppermute | solution.py:27
  176.9 19.8 %collective-permute-start.17 = (bf16[256,2048]{1,0:T(8,128)(2,1)S(1)}, bf16[256,2048]{1,0:T(8,128)(2,1)S(1)}, u32[]{:S(2)}, u32[]{:S(2)}) collective-permute-start(bf16[256,2048]{1,0:T(8,128)(2,1)S(1)} %collective-permute-done.12.mine_ref.refs_4_.refs_12_), channel_id=1, source_target_pairs={{0,1},{1,0},{2,3},{3,2},{4,5},{5,4},{6,7},{7,6},{8,9},{9,8},{10,11... | collective-permute-start | bytes 3145736 | tf_op jit(solution)/shard_map/ppermute | solution.py:27
  194.2 12.7 %collective-permute-start.19 = (bf16[256,2048]{1,0:T(8,128)(2,1)S(1)}, bf16[256,2048]{1,0:T(8,128)(2,1)S(1)}, u32[]{:S(2)}, u32[]{:S(2)}) collective-permute-start(bf16[256,2048]{1,0:T(8,128)(2,1)S(1)} %collective-permute-done.18.mine_ref.refs_6_.refs_14_), channel_id=1, source_target_pairs={{0,1},{1,0},{2,3},{3,2},{4,5},{5,4},{6,7},{7,6},{8,9},{9,8},{10,11... | collective-permute-start | bytes 3145736 | tf_op jit(solution)/shard_map/ppermute | solution.py:27
  195.6 32.3 %collective-permute-start.20 = (bf16[256,2048]{1,0:T(8,128)(2,1)}, bf16[256,2048]{1,0:T(8,128)(2,1)}, u32[]{:S(2)}, u32[]{:S(2)}) collective-permute-start(bf16[256,2048]{1,0:T(8,128)(2,1)} %add_convert_fusion.4.chip_ref), channel_id=1, source_target_pairs={{0,2},{2,0},{1,3},{3,1},{4,6},{6,4},{5,7},{7,5},{8,10},{10,8},{9,1... | collective-permute-start | bytes 3145736 | tf_op jit(solution)/shard_map/ppermute | solution.py:27
  233.7 25.7 %collective-permute-start.25 = (bf16[256,2048]{1,0:T(8,128)(2,1)}, bf16[256,2048]{1,0:T(8,128)(2,1)}, u32[]{:S(2)}, u32[]{:S(2)}) collective-permute-start(bf16[256,2048]{1,0:T(8,128)(2,1)} %get-tuple-element.157.mine_ref.refs_0_.refs_8_), channel_id=1, source_target_pairs={{0,8},{8,0},{16,24},{24,16},{1,9},{9,1},{17,25},{25,17},{2,10},{10... | collective-permute-start | bytes 3145736 | tf_op jit(solution)/shard_map/ppermute | solution.py:31
  234.6 26.7 %collective-permute-start.23 = (bf16[256,2048]{1,0:T(8,128)(2,1)}, bf16[256,2048]{1,0:T(8,128)(2,1)}, u32[]{:S(2)}, u32[]{:S(2)}) collective-permute-start(bf16[256,2048]{1,0:T(8,128)(2,1)} %get-tuple-element.157.mine_ref.refs_0_.refs_8_), channel_id=1, source_target_pairs={{0,4},{4,0},{1,5},{5,1},{2,6},{6,2},{3,7},{7,3},{8,12},{12,8},{9,1... | collective-permute-start | bytes 3145736 | tf_op jit(solution)/shard_map/ppermute | solution.py:27
  259.4 24.9 %collective-permute-start.31 = (bf16[256,2048]{1,0:T(8,128)(2,1)}, bf16[256,2048]{1,0:T(8,128)(2,1)}, u32[]{:S(2)}, u32[]{:S(2)}) collective-permute-start(bf16[256,2048]{1,0:T(8,128)(2,1)} %collective-permute-done.25.mine_ref.refs_4_.refs_12_), channel_id=1, source_target_pairs={{0,4},{4,0},{1,5},{5,1},{2,6},{6,2},{3,7},{7,3},{8,12},{12,8},{9,1... | collective-permute-start | bytes 3145736 | tf_op jit(solution)/shard_map/ppermute | solution.py:27
  261.2 23.1 %collective-permute-start.26 = (bf16[256,2048]{1,0:T(8,128)(2,1)}, bf16[256,2048]{1,0:T(8,128)(2,1)}, u32[]{:S(2)}, u32[]{:S(2)}) collective-permute-start(bf16[256,2048]{1,0:T(8,128)(2,1)} %collective-permute-done.25.mine_ref.refs_4_.refs_12_), channel_id=1, source_target_pairs={{0,1},{1,0},{2,3},{3,2},{4,5},{5,4},{6,7},{7,6},{8,9},{9,8},{10,11... | collective-permute-start | bytes 3145736 | tf_op jit(solution)/shard_map/ppermute | solution.py:27
  261.2 34.7 %collective-permute-start.24 = (bf16[256,2048]{1,0:T(8,128)(2,1)}, bf16[256,2048]{1,0:T(8,128)(2,1)}, u32[]{:S(2)}, u32[]{:S(2)}) collective-permute-start(bf16[256,2048]{1,0:T(8,128)(2,1)} %collective-permute-done.23.mine_ref.refs_2_.refs_10_), channel_id=1, source_target_pairs={{0,1},{1,0},{2,3},{3,2},{4,5},{5,4},{6,7},{7,6},{8,9},{9,8},{10,11... | collective-permute-start | bytes 3145736 | tf_op jit(solution)/shard_map/ppermute | solution.py:27
  263.1 43.7 %collective-permute-start.27 = (bf16[256,2048]{1,0:T(8,128)(2,1)}, bf16[256,2048]{1,0:T(8,128)(2,1)}, u32[]{:S(2)}, u32[]{:S(2)}) collective-permute-start(bf16[256,2048]{1,0:T(8,128)(2,1)} %add_convert_fusion.3.chip_ref), channel_id=1, source_target_pairs={{0,2},{2,0},{1,3},{3,1},{4,6},{6,4},{5,7},{7,5},{8,10},{10,8},{9,1... | collective-permute-start | bytes 3145736 | tf_op jit(solution)/shard_map/ppermute | solution.py:27
  284.3 30.7 %collective-permute-start.32 = (bf16[256,2048]{1,0:T(8,128)(2,1)}, bf16[256,2048]{1,0:T(8,128)(2,1)}, u32[]{:S(2)}, u32[]{:S(2)}) collective-permute-start(bf16[256,2048]{1,0:T(8,128)(2,1)} %collective-permute-done.31.mine_ref.refs_6_.refs_14_), channel_id=1, source_target_pairs={{0,1},{1,0},{2,3},{3,2},{4,5},{5,4},{6,7},{7,6},{8,9},{9,8},{10,11... | collective-permute-start | bytes 3145736 | tf_op jit(solution)/shard_map/ppermute | solution.py:27
  313.2 85.3 %collective-permute-start.43 = (bf16[256,2048]{1,0:T(8,128)(2,1)}, bf16[256,2048]{1,0:T(8,128)(2,1)}, u32[]{:S(2)}, u32[]{:S(2)}) collective-permute-start(bf16[256,2048]{1,0:T(8,128)(2,1)} %get-tuple-element.177.mine_ref.refs_0_), channel_id=1, source_target_pairs={{0,4},{4,0},{1,5},{5,1},{2,6},{6,2},{3,7},{7,3},{8,12},{12,8},{9,1... | collective-permute-start | bytes 3145736 | tf_op jit(solution)/shard_map/ppermute | solution.py:27
  329.5 14.3 %collective-permute-start.33 = (bf16[512,128]{1,0:T(8,128)(2,1)S(1)}, bf16[512,128]{1,0:T(8,128)(2,1)S(1)}, u32[]{:S(2)}, u32[]{:S(2)}) collective-permute-start(bf16[512,128]{1,0:T(8,128)(2,1)S(1)} %get-tuple-element.154), channel_id=1, source_target_pairs={{0,24},{8,16},{16,8},{24,0},{1,25},{9,17},{17,9},{25,1},{2,26},{10... | collective-permute-start | bytes 393224 | tf_op jit(solution)/shard_map/ppermute | solution.py:31
  331.0 12.8 %collective-permute-start.29 = (bf16[512,128]{1,0:T(8,128)(2,1)S(1)}, bf16[512,128]{1,0:T(8,128)(2,1)S(1)}, u32[]{:S(2)}, u32[]{:S(2)}) collective-permute-start(bf16[512,128]{1,0:T(8,128)(2,1)S(1)} %get-tuple-element.145), channel_id=1, source_target_pairs={{0,8},{8,0},{16,24},{24,16},{1,9},{9,1},{17,25},{25,17},{2,10},{10... | collective-permute-start | bytes 393224 | tf_op jit(solution)/shard_map/ppermute | solution.py:31
  331.0 12.8 %collective-permute-start.30 = (bf16[512,128]{1,0:T(8,128)(2,1)S(1)}, bf16[512,128]{1,0:T(8,128)(2,1)S(1)}, u32[]{:S(2)}, u32[]{:S(2)}) collective-permute-start(bf16[512,128]{1,0:T(8,128)(2,1)S(1)} %get-tuple-element.146), channel_id=1, source_target_pairs={{0,16},{8,24},{16,0},{24,8},{1,17},{9,25},{17,1},{25,9},{2,18},{10... | collective-permute-start | bytes 393224 | tf_op jit(solution)/shard_map/ppermute | solution.py:31
  369.5 28.0 %collective-permute-start.34 = (bf16[2048,256]{1,0:T(8,128)(2,1)S(1)}, bf16[2048,256]{1,0:T(8,128)(2,1)S(1)}, u32[]{:S(2)}, u32[]{:S(2)}) collective-permute-start(bf16[2048,256]{1,0:T(8,128)(2,1)S(1)} %copy-done.91), channel_id=1, source_target_pairs={{0,4},{4,0},{1,5},{5,1},{2,6},{6,2},{3,7},{7,3},{8,12},{12,8},{9,1... | collective-permute-start | bytes 3145736 | tf_op jit(solution)/shard_map/ppermute | solution.py:27
  398.5 16.1 %collective-permute-start.44 = (bf16[256,2048]{1,0:T(8,128)(2,1)}, bf16[256,2048]{1,0:T(8,128)(2,1)}, u32[]{:S(2)}, u32[]{:S(2)}) collective-permute-start(bf16[256,2048]{1,0:T(8,128)(2,1)} %collective-permute-done.43.refs_2_), channel_id=1, source_target_pairs={{0,1},{1,0},{2,3},{3,2},{4,5},{5,4},{6,7},{7,6},{8,9},{9,8},{10,11... | collective-permute-start | bytes 3145736 | tf_op jit(solution)/shard_map/ppermute | solution.py:27
  399.1 14.0 %collective-permute-start.45 = (bf16[512,512]{1,0:T(8,128)(2,1)}, bf16[512,512]{1,0:T(8,128)(2,1)S(1)}, u32[]{:S(2)}, u32[]{:S(2)}) collective-permute-start(bf16[512,512]{1,0:T(8,128)(2,1)} %copy-done.39), channel_id=1, source_target_pairs={{0,4},{4,0},{1,5},{5,1},{2,6},{6,2},{3,7},{7,3},{8,12},{12,8},{9,1... | collective-permute-start | bytes 1572872 | tf_op jit(solution)/shard_map/ppermute | solution.py:27
  400.8 13.7 %collective-permute-start.38 = (bf16[512,128]{1,0:T(8,128)(2,1)}, bf16[512,128]{1,0:T(8,128)(2,1)S(1)}, u32[]{:S(2)}, u32[]{:S(2)}) collective-permute-start(bf16[512,128]{1,0:T(8,128)(2,1)} %get-tuple-element.169.refs_1_), channel_id=1, source_target_pairs={{0,8},{8,0},{16,24},{24,16},{1,9},{9,1},{17,25},{25,17},{2,10},{10... | collective-permute-start | bytes 393224 | tf_op jit(solution)/shard_map/ppermute | solution.py:31
  401.1 35.8 %collective-permute-start.39 = (bf16[512,128]{1,0:T(8,128)(2,1)}, bf16[512,128]{1,0:T(8,128)(2,1)}, u32[]{:S(2)}, u32[]{:S(2)}) collective-permute-start(bf16[512,128]{1,0:T(8,128)(2,1)} %get-tuple-element.170.refs_2_), channel_id=1, source_target_pairs={{0,16},{8,24},{16,0},{24,8},{1,17},{9,25},{17,1},{25,9},{2,18},{10... | collective-permute-start | bytes 393224 | tf_op jit(solution)/shard_map/ppermute | solution.py:31
  413.1 23.8 %collective-permute-start.40 = (bf16[512,128]{1,0:T(8,128)(2,1)S(1)}, bf16[512,128]{1,0:T(8,128)(2,1)S(1)}, u32[]{:S(2)}, u32[]{:S(2)}) collective-permute-start(bf16[512,128]{1,0:T(8,128)(2,1)S(1)} %copy-done.71), channel_id=1, source_target_pairs={{0,24},{8,16},{16,8},{24,0},{1,25},{9,17},{17,9},{25,1},{2,26},{10... | collective-permute-start | bytes 393224 | tf_op jit(solution)/shard_map/ppermute | solution.py:31
  414.6 23.0 %collective-permute-start.41 = (bf16[512,256]{1,0:T(8,128)(2,1)}, bf16[512,256]{1,0:T(8,128)(2,1)S(1)}, u32[]{:S(2)}, u32[]{:S(2)}) collective-permute-start(bf16[512,256]{1,0:T(8,128)(2,1)} %get-tuple-element.245), channel_id=1, source_target_pairs={{0,8},{8,0},{16,24},{24,16},{1,9},{9,1},{17,25},{25,17},{2,10},{10... | collective-permute-start | bytes 786440 | tf_op jit(solution)/shard_map/ppermute | solution.py:31
  414.6 23.4 %collective-permute-start.42 = (bf16[512,256]{1,0:T(8,128)(2,1)}, bf16[512,256]{1,0:T(8,128)(2,1)S(1)}, u32[]{:S(2)}, u32[]{:S(2)}) collective-permute-start(bf16[512,256]{1,0:T(8,128)(2,1)} %get-tuple-element.244), channel_id=1, source_target_pairs={{0,16},{8,24},{16,0},{24,8},{1,17},{9,25},{17,1},{25,9},{2,18},{10... | collective-permute-start | bytes 786440 | tf_op jit(solution)/shard_map/ppermute | solution.py:31
  417.5 40.4 %collective-permute-start.36 = (bf16[256,2048]{1,0:T(8,128)(2,1)}, bf16[256,2048]{1,0:T(8,128)(2,1)}, u32[]{:S(2)}, u32[]{:S(2)}) collective-permute-start(bf16[256,2048]{1,0:T(8,128)(2,1)} %add_convert_fusion.2), channel_id=1, source_target_pairs={{0,2},{2,0},{1,3},{3,1},{4,6},{6,4},{5,7},{7,5},{8,10},{10,8},{9,1... | collective-permute-start | bytes 3145736 | tf_op jit(solution)/shard_map/ppermute | solution.py:27
  448.6 72.8 %collective-permute-start.60 = (bf16[256,2048]{1,0:T(8,128)(2,1)}, bf16[256,2048]{1,0:T(8,128)(2,1)}, u32[]{:S(2)}, u32[]{:S(2)}) collective-permute-start(bf16[256,2048]{1,0:T(8,128)(2,1)} %get-tuple-element.196), channel_id=1, source_target_pairs={{0,16},{8,24},{16,0},{24,8},{1,17},{9,25},{17,1},{25,9},{2,18},{10... | collective-permute-start | bytes 3145736 | tf_op jit(solution)/shard_map/ppermute | solution.py:31
  457.9 69.8 %collective-permute-start.55 = (bf16[4,384,256]{2,1,0:T(8,128)(2,1)}, bf16[4,384,256]{2,1,0:T(8,128)(2,1)}, u32[]{:S(2)}, u32[]{:S(2)}) collective-permute-start(bf16[4,384,256]{2,1,0:T(8,128)(2,1)} %get-tuple-element.191), channel_id=1, source_target_pairs={{0,4},{4,0},{1,5},{5,1},{2,6},{6,2},{3,7},{7,3},{8,12},{12,8},{9,1... | collective-permute-start | bytes 2359304 | tf_op jit(solution)/shard_map/ppermute | solution.py:27
  459.9 69.4 %collective-permute-start.37 = (bf16[256,2048]{1,0:T(8,128)(2,1)S(1)}, bf16[256,2048]{1,0:T(8,128)(2,1)}, u32[]{:S(2)}, u32[]{:S(2)}) collective-permute-start(bf16[256,2048]{1,0:T(8,128)(2,1)S(1)} %add_convert_fusion.1.mine_ref), channel_id=1, source_target_pairs={{0,1},{1,0},{2,3},{3,2},{4,5},{5,4},{6,7},{7,6},{8,9},{9,8},{10,11... | collective-permute-start | bytes 3145736 | tf_op jit(solution)/shard_map/ppermute | solution.py:27
  460.6 71.6 %collective-permute-start.48 = (bf16[256,2048]{1,0:T(8,128)(2,1)S(1)}, bf16[256,2048]{1,0:T(8,128)(2,1)}, u32[]{:S(2)}, u32[]{:S(2)}) collective-permute-start(bf16[256,2048]{1,0:T(8,128)(2,1)S(1)} %add_convert_fusion.chip_ref), channel_id=1, source_target_pairs={{0,2},{2,0},{1,3},{3,1},{4,6},{6,4},{5,7},{7,5},{8,10},{10,8},{9,1... | collective-permute-start | bytes 3145736 | tf_op jit(solution)/shard_map/ppermute | solution.py:27
  527.8 56.3 %collective-permute-start.59 = (bf16[256,2048]{1,0:T(8,128)(2,1)}, bf16[256,2048]{1,0:T(8,128)(2,1)S(1)}, u32[]{:S(2)}, u32[]{:S(2)}) collective-permute-start(bf16[256,2048]{1,0:T(8,128)(2,1)} %copy-done.54), channel_id=1, source_target_pairs={{0,16},{8,24},{16,0},{24,8},{1,17},{9,25},{17,1},{25,9},{2,18},{10... | collective-permute-start | bytes 3145736 | tf_op jit(solution)/shard_map/ppermute | solution.py:31
  536.9 48.8 %collective-permute-start.56 = (bf16[384,256]{1,0:T(8,128)(2,1)S(1)}, bf16[384,256]{1,0:T(8,128)(2,1)S(1)}, u32[]{:S(2)}, u32[]{:S(2)}) collective-permute-start(bf16[384,256]{1,0:T(8,128)(2,1)S(1)} %get-tuple-element.249), channel_id=1, source_target_pairs={{0,8},{8,0},{16,24},{24,16},{1,9},{9,1},{17,25},{25,17},{2,10},{10... | collective-permute-start | bytes 589832 | tf_op jit(solution)/shard_map/ppermute | solution.py:31
  539.5 48.8 %collective-permute-start.57 = (bf16[384,256]{1,0:T(8,128)(2,1)S(1)}, bf16[384,256]{1,0:T(8,128)(2,1)S(1)}, u32[]{:S(2)}, u32[]{:S(2)}) collective-permute-start(bf16[384,256]{1,0:T(8,128)(2,1)S(1)} %get-tuple-element.248), channel_id=1, source_target_pairs={{0,16},{8,24},{16,0},{24,8},{1,17},{9,25},{17,1},{25,9},{2,18},{10... | collective-permute-start | bytes 589832 | tf_op jit(solution)/shard_map/ppermute | solution.py:31
  540.0 48.3 %collective-permute-start.58 = (bf16[384,256]{1,0:T(8,128)(2,1)S(1)}, bf16[384,256]{1,0:T(8,128)(2,1)S(1)}, u32[]{:S(2)}, u32[]{:S(2)}) collective-permute-start(bf16[384,256]{1,0:T(8,128)(2,1)S(1)} %get-tuple-element.247), channel_id=1, source_target_pairs={{0,24},{8,16},{16,8},{24,0},{1,25},{9,17},{17,9},{25,1},{2,26},{10... | collective-permute-start | bytes 589832 | tf_op jit(solution)/shard_map/ppermute | solution.py:31
  541.9 48.4 %collective-permute-start.51 = (f32[8196]{0:T(1024)S(1)}, f32[8196]{0:T(1024)S(1)}, u32[]{:S(2)}, u32[]{:S(2)}) collective-permute-start(f32[8196]{0:T(1024)S(1)} %add.189), channel_id=1, source_target_pairs={{0,4},{4,0},{1,5},{5,1},{2,6},{6,2},{3,7},{7,3},{8,12},{12,8},{9,1... | collective-permute-start | bytes 98360 | tf_op jit(solution)/shard_map/ppermute | solution.py:27
  (110 other events, 1157.0 us)
Sparse Core Ops, SparseCore 0:
  36.7 95.9 all-gather.2
  461.8 45.6 reduce-scatter.1
